TPU v7x, 32 devices: a whole 2x2x4 slice. The times are simulated.
32 devices in a mesh: seq: 8 (over y, x, core), head: 4 (over z).
Axes of the slice: x: 2, y: 2, z: 4, core: 2. Of those that a mesh axis runs over, the one named last changes fastest.
Arguments:
- histories: bfloat16 [9, 4096, 2048], P(None, ('seq', 'head'))
- norm_gains: float32 [4, 2048], replicated, may hold values from 0.1 to 1.9
- mix_in: bfloat16 [2048, 40], replicated, may hold values from -0.125 to 0.125
- mix_out: bfloat16 [40, 36], replicated, may hold values from -0.3125 to 0.3125
- mix_bias: float32 [36], replicated, may hold values from -1.3 to 1.3
- w_query: bfloat16 [2048, 2048], P(None, 'head'), may hold values from -0.125 to 0.125
- w_key: bfloat16 [2048, 2048], P(None, 'head'), may hold values from -0.125 to 0.125
- w_value: bfloat16 [2048, 2048], P(None, 'head'), may hold values from -0.125 to 0.125
- w_out: bfloat16 [2048, 2048], P('head'), may hold values from -0.5 to 0.5
- w_up: bfloat16 [2048, 8192], P(None, 'head'), may hold values from -0.125 to 0.125
- w_down: bfloat16 [8192, 2048], P('head'), may hold values from -0.0625 to 0.0625
- cotangent: bfloat16 [4096, 2048], P(('seq', 'head')), may hold values from -6 to 6
- doc_ids: int32 [4096], replicated, may hold values from 0 to 2, as said below
- positions: int32 [4096], P('seq'), may hold values from 0 to 3583, as said below
Outputs:
- layer_out: bfloat16 [4096, 2048], P(('seq', 'head'))
- grad_histories: bfloat16 [9, 4096, 2048], P(None, ('seq', 'head'))
- grad_norm_gains: float32 [4, 2048], replicated
- grad_mix_in: float32 [2048, 40], replicated
- grad_mix_out: float32 [40, 36], replicated
- grad_mix_bias: float32 [36], replicated
- grad_w_query: float32 [2048, 2048], P(None, 'head')
- grad_w_key: float32 [2048, 2048], P(None, 'head')
- grad_w_value: float32 [2048, 2048], P(None, 'head')
- grad_w_out: float32 [2048, 2048], P('head')
- grad_w_up: float32 [2048, 8192], P(None, 'head')
- grad_w_down: float32 [8192, 2048], P('head')
Inputs may be any that keep to these rules, and one draw needn't show every extreme that they name: `doc_ids`: three contiguous documents numbered 0, 1, 2 in order; document 0 has 1 to 511 tokens, document 2 has 512 minus that many, document 1 has 3584 tokens. `positions`: each token's offset from the first token of its document.
All inputs are finite; a program needn't handle non-finite values.
Results may differ from a plain program's by a relative error of at most 0.023.
Values may be sent and summed in bfloat16 or wider, within the bound.
No kernel may reach another device: no remote copies, remote signals or barrier semaphores. Data moves between devices by JAX's collectives and lax.ppermute only.
A program may use at most 256 MiB of HBM per device.

v0:
```python
import jax
import jax.numpy as jnp
from jax import lax
from jax.sharding import PartitionSpec as P

HD = 128
ROT = 32


eps_norm = 1e-05
eps_rms = 1e-06
rope_base = 10000.0
hidden_mask = -1e30
highest = lax.Precision.HIGHEST


def from_behind(block, axis, distance):
    devices = range(lax.axis_size(axis))
    route = [(i - distance, i) for i in devices if i - distance in devices]
    return lax.ppermute(block, axis, route)


def passed_along(x, axis, by):
    count = lax.axis_size(axis)
    return lax.ppermute(x, axis, [(i, (i + by) % count) for i in range(count)])


def layer_norm(values, gain_rows):
    centre = values - jnp.mean(values, axis=-1, keepdims=True)
    spread = jnp.mean(centre * centre, axis=-1, keepdims=True)
    return centre * lax.rsqrt(spread + eps_norm) * gain_rows


def rms_scale(newest):
    return newest * lax.rsqrt(jnp.mean(newest * newest, axis=-1, keepdims=True) + eps_rms)


def exact_gelu(values):
    return jax.nn.gelu(values, approximate=False)


def rope_tables(positions):
    half_rot = ROT // 2
    frequency = rope_base ** (-(jnp.arange(half_rot, dtype=jnp.float32) * 2.0 / ROT))
    angles = positions.astype(jnp.float32)[:, None] * frequency[None, :]
    return (jnp.cos(angles)[:, None, :], jnp.sin(angles)[:, None, :])


def rotate(head_rows, cos_rows, sin_rows):
    half_rot = ROT // 2
    first_half = head_rows[..., :half_rot]
    second = head_rows[..., half_rot:ROT]
    return jnp.concatenate(
        [
            first_half * cos_rows - second * sin_rows,
            second * cos_rows + first_half * sin_rows,
            head_rows[..., ROT:],
        ],
        axis=-1,
    )


def rotate_back(grad_rows, cos_rows, sin_rows):
    half_rot = ROT // 2
    first_half = grad_rows[..., :half_rot]
    second = grad_rows[..., half_rot:ROT]
    return jnp.concatenate(
        [
            first_half * cos_rows + second * sin_rows,
            second * cos_rows - first_half * sin_rows,
            grad_rows[..., ROT:],
        ],
        axis=-1,
    )


def outer_product(left_side, right_side):
    return lax.dot_general(
        left_side, right_side, (((0,), (0,)), ((), ())), preferred_element_type=jnp.float32
    )


def outer_exact(left_side, right_side):
    return lax.dot_general(left_side, right_side, (((0,), (0,)), ((), ())), precision=highest)


def times_transpose(left_side, right_side):
    return lax.dot_general(
        left_side, right_side, (((1,), (1,)), ((), ())), preferred_element_type=jnp.float32
    )


def back_project(grad_rows, weight):
    return times_transpose(grad_rows, weight)


def body(
    histories,
    norm_gains,
    mix_in,
    mix_out,
    mix_bias,
    w_query,
    w_key,
    w_value,
    w_out,
    w_up,
    w_down,
    cotangent,
    doc_ids,
    positions,
):
    seq_count = lax.axis_size("seq")
    seq_rank = lax.axis_index("seq")
    block_rows = positions.shape[0]
    hist_count, tok_rows, model_width = histories.shape
    stream_count = norm_gains.shape[0]
    local_width = w_query.shape[1]
    local_heads = local_width // HD
    cycle_steps = seq_count - 1
    score_scale = HD ** (-0.5)
    hist_wide = histories.astype(jnp.float32)
    rms_last = rms_scale(hist_wide[hist_count - 1])
    rms_low = rms_last.astype(jnp.bfloat16)
    mix_pre = jnp.dot(rms_low, mix_in, preferred_element_type=jnp.float32)
    mix_hidden = exact_gelu(mix_pre).astype(jnp.bfloat16)
    coefficient = (
        jnp.dot(mix_hidden, mix_out, preferred_element_type=jnp.float32) + mix_bias
    ).reshape(tok_rows, stream_count, hist_count)
    streams = jnp.einsum("tcj,jtd->tcd", coefficient, hist_wide, precision=highest)
    normed = layer_norm(streams, norm_gains[None, :, :]).astype(jnp.bfloat16)
    gathered = lax.all_gather(normed, "head", axis=0, tiled=True)
    query_proj = jnp.dot(gathered[:, 0], w_query, preferred_element_type=jnp.float32)
    key_proj = jnp.dot(gathered[:, 1], w_key, preferred_element_type=jnp.float32)
    value_proj = jnp.dot(gathered[:, 2], w_value, preferred_element_type=jnp.float32)
    hidden_pre = jnp.dot(gathered[:, 3], w_up, preferred_element_type=jnp.float32)
    cos_rows, sin_rows = rope_tables(positions)
    query_low = rotate(query_proj.reshape(block_rows, local_heads, HD), cos_rows, sin_rows).astype(
        jnp.bfloat16
    )
    key_low = rotate(key_proj.reshape(block_rows, local_heads, HD), cos_rows, sin_rows).astype(
        jnp.bfloat16
    )
    value_low = value_proj.reshape(block_rows, local_heads, HD).astype(jnp.bfloat16)
    activated = exact_gelu(hidden_pre).astype(jnp.bfloat16)
    row_index = jnp.arange(block_rows, dtype=jnp.int32)
    query_ids = lax.dynamic_slice_in_dim(doc_ids, seq_rank * block_rows, block_rows)
    query_place = seq_rank * block_rows + row_index

    def visible(source):
        safe_source = jnp.maximum(source, 0)
        key_ids = lax.dynamic_slice_in_dim(doc_ids, safe_source * block_rows, block_rows)
        key_place = source * block_rows + row_index
        return (
            (query_ids[:, None] == key_ids[None, :])
            & (key_place[None, :] <= query_place[:, None])
            & (source >= 0)
        )

    def attend(carried, key_block, value_block, source):
        row_peak, row_total, accumulated = carried
        seen_mask = visible(source)[None]
        scores = (
            jnp.einsum("qhd,khd->hqk", query_low, key_block, preferred_element_type=jnp.float32)
            * score_scale
        )
        scores = jnp.where(seen_mask, scores, hidden_mask)
        new_peak = jnp.maximum(row_peak, jnp.max(scores, axis=-1))
        weights = jnp.where(seen_mask, jnp.exp(scores - new_peak[..., None]), 0.0)
        factor = jnp.exp(row_peak - new_peak)
        row_total = row_total * factor + jnp.sum(weights, axis=-1)
        accumulated = accumulated * factor[..., None] + jnp.einsum(
            "hqk,khd->hqd",
            weights.astype(jnp.bfloat16),
            value_block,
            preferred_element_type=jnp.float32,
        )
        return (new_peak, row_total, accumulated)

    def attend_from(carried, key_block, value_block, source):
        return attend(carried, key_block, value_block, source)

    start_state = (
        jnp.full((local_heads, block_rows), hidden_mask, jnp.float32),
        jnp.zeros((local_heads, block_rows), jnp.float32),
        jnp.zeros((local_heads, block_rows, HD), jnp.float32),
    )
    carried = attend(start_state, key_low, value_low, seq_rank)

    def cycle_step(cycle_carry, offset):
        carried, key_block, value_block = cycle_carry
        key_block, value_block = from_behind((key_block, value_block), "seq", 1)
        carried = attend_from(carried, key_block, value_block, seq_rank - offset)
        kept_blocks = None
        return ((carried, key_block, value_block), kept_blocks)

    cycle_offsets = jnp.arange(1, cycle_steps + 1, dtype=jnp.int32)
    cycle_final, visited = lax.scan(cycle_step, (carried, key_low, value_low), cycle_offsets)
    row_peak, row_total, accumulated = cycle_final[0]
    log_total = row_peak + jnp.log(row_total)
    attended_wide = jnp.transpose(accumulated / row_total[..., None], (1, 0, 2))
    attended_low = attended_wide.reshape(block_rows, local_width).astype(jnp.bfloat16)
    branch_sum = lax.psum_scatter(
        (
            jnp.dot(attended_low, w_out, preferred_element_type=jnp.float32)
            + jnp.dot(activated, w_down, preferred_element_type=jnp.float32)
        ).astype(jnp.bfloat16),
        "head",
        scatter_dimension=0,
        tiled=True,
    ).astype(jnp.float32)
    layer_out = (streams[:, 3] + branch_sum).astype(jnp.bfloat16)
    grad_full = lax.all_gather(cotangent, "head", axis=0, tiled=True)
    grad_attended = times_transpose(grad_full, w_out)
    grad_activated = times_transpose(grad_full, w_down)
    grad_w_out = outer_product(attended_low, grad_full)
    grad_w_down = outer_product(activated, grad_full)
    gelu_pull = jax.vjp(exact_gelu, hidden_pre)[1]
    grad_hidden = gelu_pull(grad_activated)[0].astype(jnp.bfloat16)
    grad_heads = grad_attended.reshape(block_rows, local_heads, HD).astype(jnp.bfloat16)
    row_delta = jnp.transpose(jnp.sum(grad_heads.astype(jnp.float32) * attended_wide, axis=-1))
    zero_heads = jnp.zeros((block_rows, local_heads, HD), jnp.float32)

    def key_pieces(key_block, value_block, source):
        seen_mask = visible(source)[None]
        scores = (
            jnp.einsum("qhd,khd->hqk", query_low, key_block, preferred_element_type=jnp.float32)
            * score_scale
        )
        weights = jnp.where(seen_mask, jnp.exp(scores - log_total[..., None]), 0.0)
        grad_weights = jnp.einsum(
            "qhd,khd->hqk", grad_heads, value_block, preferred_element_type=jnp.float32
        )
        grad_scores = (weights * (grad_weights - row_delta[..., None])).astype(jnp.bfloat16)
        part_query = (
            jnp.einsum("hqk,khd->qhd", grad_scores, key_block, preferred_element_type=jnp.float32)
            * score_scale
        )
        part_key = (
            jnp.einsum("hqk,qhd->khd", grad_scores, query_low, preferred_element_type=jnp.float32)
            * score_scale
        )
        part_value = jnp.einsum(
            "hqk,qhd->khd",
            weights.astype(jnp.bfloat16),
            grad_heads,
            preferred_element_type=jnp.float32,
        )
        return (part_query, part_key, part_value)

    def pieces_from(key_block, value_block, source):
        return key_pieces(key_block, value_block, source)

    def back_step(back_carry, offset):
        key_block, value_block, grad_key_acc, grad_value_acc, grad_query_acc = back_carry
        part_query, part_key, part_value = pieces_from(key_block, value_block, seq_rank - offset)
        key_block, value_block = from_behind((key_block, value_block), "seq", 1)
        grad_key_acc, grad_value_acc = (
            passed_along((grad_key_acc + part_key).astype(jnp.bfloat16), "seq", 1).astype(
                jnp.float32
            ),
            passed_along((grad_value_acc + part_value).astype(jnp.bfloat16), "seq", 1).astype(
                jnp.float32
            ),
        )
        return (
            (key_block, value_block, grad_key_acc, grad_value_acc, grad_query_acc + part_query),
            None,
        )

    back_final = lax.scan(
        back_step,
        (key_low, value_low, zero_heads, zero_heads, zero_heads),
        jnp.arange(cycle_steps, dtype=jnp.int32),
    )[0]
    key_block, value_block, grad_key_acc, grad_value_acc, grad_query_acc = back_final
    part_query, part_key, part_value = pieces_from(key_block, value_block, seq_rank - cycle_steps)
    grad_query_acc = grad_query_acc + part_query
    grad_key_acc, grad_value_acc = (
        passed_along((grad_key_acc + part_key).astype(jnp.bfloat16), "seq", -cycle_steps).astype(
            jnp.float32
        ),
        passed_along(
            (grad_value_acc + part_value).astype(jnp.bfloat16), "seq", -cycle_steps
        ).astype(jnp.float32),
    )
    grad_query_low = (
        rotate_back(grad_query_acc, cos_rows, sin_rows)
        .reshape(block_rows, local_width)
        .astype(jnp.bfloat16)
    )
    grad_key_low = (
        rotate_back(grad_key_acc, cos_rows, sin_rows)
        .reshape(block_rows, local_width)
        .astype(jnp.bfloat16)
    )
    grad_value_low = grad_value_acc.reshape(block_rows, local_width).astype(jnp.bfloat16)
    grad_w_query = outer_product(gathered[:, 0], grad_query_low)
    grad_w_key = outer_product(gathered[:, 1], grad_key_low)
    grad_w_value = outer_product(gathered[:, 2], grad_value_low)
    grad_w_up = outer_product(gathered[:, 3], grad_hidden)
    projected = [
        back_project(grad_query_low, w_query),
        back_project(grad_key_low, w_key),
        back_project(grad_value_low, w_value),
        back_project(grad_hidden, w_up),
    ]
    grad_normed = lax.psum_scatter(
        jnp.stack(projected, axis=1).astype(jnp.bfloat16), "head", scatter_dimension=0, tiled=True
    ).astype(jnp.float32)
    norm_pull = jax.vjp(layer_norm, streams, norm_gains[None, :, :])[1]
    grad_streams, grad_gain_rows = norm_pull(grad_normed)
    grad_gains = jnp.sum(grad_gain_rows, axis=0)
    grad_streams = grad_streams.at[:, 3].add(cotangent.astype(jnp.float32))
    grad_coeff = jnp.einsum("tcd,jtd->tcj", grad_streams, hist_wide, precision=highest).reshape(
        tok_rows, stream_count * hist_count
    )
    grad_hist = jnp.einsum("tcj,tcd->jtd", coefficient, grad_streams, precision=highest)
    grad_bias = jnp.sum(grad_coeff, axis=0)
    grad_mix_out = outer_exact(mix_hidden.astype(jnp.float32), grad_coeff)
    grad_mix_hidden = lax.dot_general(
        grad_coeff, mix_out.astype(jnp.float32), (((1,), (1,)), ((), ())), precision=highest
    )
    grad_mix_pre = jax.vjp(exact_gelu, mix_pre)[1](grad_mix_hidden)[0]
    grad_mix_in = outer_exact(rms_low.astype(jnp.float32), grad_mix_pre)
    grad_rms = lax.dot_general(
        grad_mix_pre, mix_in.astype(jnp.float32), (((1,), (1,)), ((), ())), precision=highest
    )
    grad_newest = jax.vjp(rms_scale, hist_wide[hist_count - 1])[1](grad_rms)[0]
    grad_hist = grad_hist.at[hist_count - 1].add(grad_newest)
    weight_grads = (
        lax.psum(grad_w_query.astype(jnp.bfloat16), "seq").astype(jnp.float32),
        lax.psum(grad_w_key.astype(jnp.bfloat16), "seq").astype(jnp.float32),
        lax.psum(grad_w_value.astype(jnp.bfloat16), "seq").astype(jnp.float32),
        lax.psum(grad_w_out.astype(jnp.bfloat16), "seq").astype(jnp.float32),
        lax.psum(grad_w_up.astype(jnp.bfloat16), "seq").astype(jnp.float32),
        lax.psum(grad_w_down.astype(jnp.bfloat16), "seq").astype(jnp.float32),
    )
    small_grads = lax.psum((grad_gains, grad_mix_in, grad_mix_out, grad_bias), ("seq", "head"))
    return (
        layer_out,
        grad_hist.astype(jnp.bfloat16),
        small_grads[0],
        small_grads[1],
        small_grads[2],
        small_grads[3],
        weight_grads[0],
        weight_grads[1],
        weight_grads[2],
        weight_grads[3],
        weight_grads[4],
        weight_grads[5],
    )


def solution(mesh):
    return jax.shard_map(
        body,
        mesh=mesh,
        in_specs=(
            P(None, ("seq", "head"), None),
            P(),
            P(),
            P(),
            P(),
            P(None, "head"),
            P(None, "head"),
            P(None, "head"),
            P("head", None),
            P(None, "head"),
            P("head", None),
            P(("seq", "head"), None),
            P(),
            P("seq"),
        ),
        out_specs=(
            P(("seq", "head"), None),
            P(None, ("seq", "head"), None),
            P(),
            P(),
            P(),
            P(),
            P(None, "head"),
            P(None, "head"),
            P(None, "head"),
            P("head", None),
            P(None, "head"),
            P("head", None),
        ),
        check_vma=False,
    )
```

profile of v0, /device:TPU:0, one launch (start us, length us, event | category | flops | bytes accessed | tf_op | source)
XLA Modules:
  0.0 1543.4 jit_solution(3641561019810664736)
XLA Ops:
  12.4 8.6 fusion.144
  45.2 135.8 %all-gather.3.cloned.1.call-done = bf16[512,4,2048]{2,1,0:T(4,128)(2,1)} async-done(((bf16[128,4,2048]{2,1,0:T(4,128)(2,1)}), bf16[512,4,2048]{2,1,0:T(4,128)(2,1)}) %all-gather.3.cloned.1.call-update) | async-done | bytes 8388624 | tf_op jit(solution)/shard_map/all_gather | solution.py:132
  181.0 27.0 %fusion.142 = (bf16[512,1,2048]{2,1,0:T(2,128)(2,1)}, bf16[512,1,2048]{2,1,0:T(2,128)(2,1)}, bf16[512,1,2048]{2,1,0:T(2,128)(2,1)}, bf16[512,1,2048]{2,1,0:T(2,128)(2,1)S(1)}) fusion(bf16[512,4,2048]{2,1,0:T(4,128)(2,1)} %all-gather.3.cloned.1.call-done), kind=kLoop, calls=%fused_computation.215 | loop fusion | bytes 16777216 | tf_op jit(solution)/shard_map/slice | solution.py:135
  210.0 9.9 fusion.110
  220.0 6.8 all-gather.5.cloned.1.call-done
  226.8 18.6 %add_convert_fusion = (bf16[512,2048]{1,0:T(8,128)(2,1)}, f32[512,2048]{1,0:T(8,128)S(1)}) fusion(f32[512,2048]{1,0:T(8,128)} %fusion.110, bf16[512,2048]{1,0:T(8,128)(2,1)} %all-gather.5.cloned.1.call-done, bf16[2048,2048]{1,0:T(8,128)(2,1)} %param.32), kind=kOutput, calls=%fused_computation.59 | convolution fusion | flops 4370464768 | bytes 20971520 | tf_op jit(solution)/shard_map/dot_general | solution.py:88
  246.4 10.7 fusion.147
  275.9 151.2 %while.40 = (s32[]{:T(128)}, f32[4,512]{1,0:T(4,128)S(1)}, f32[4,512]{1,0:T(4,128)S(1)}, f32[4,512,128]{2,1,0:T(8,128)}, bf16[512,4,128]{2,0,1:T(8,128)(2,1)}, /...) while((s32[]{:T(128)}, f32[4,512]{1,0:T(4,128)S(1)}, ...), condition=%wide.region_8.9_spmd.clone, body=%wide.region_5.8_spmd.clone.sunk | while | flops 552080384 | bytes 32129424 | solution.py:198
  441.4 284.6 %while.41 = (s32[]{:T(128)}, bf16[512,4,128]{2,0,1:T(8,128)(2,1)}, bf16[512,4,128]{2,0,1:T(8,128)(2,1)}, f32[512,4,128]{2,0,1:T(8,128)}, f32[512,4,128]{2,0,1:T(...) while((s32[]{:T(128)}, bf16[512,4,128]{2,0,1:T(8,128)(2,1)}, ...), condition=%wide.region_12.13_spmd.clone, body=%wide.region_11.12_spmd.clone.sunk | while | flops 1356858368 | bytes 69583504 | solution.py:271
  464.1 6.6 collective-permute-start.2
  504.4 6.7 collective-permute-start.2
  544.9 6.8 collective-permute-start.2
  585.3 6.8 collective-permute-start.2
  625.9 6.8 collective-permute-start.2
  666.3 6.8 collective-permute-start.2
  706.9 6.8 collective-permute-start.2
  741.2 10.0 fusion.61
  769.8 20.4 %copy.211 = bf16[512,4,2048]{2,1,0:T(4,128)(2,1)} copy(bf16[512,4,2048]{2,0,1:T(8,128)(2,1)S(1)} %pad_maximum_fusion) | data formatting | bytes 16777216 | tf_op jit(solution)/shard_map/stack | solution.py:309
  795.6 8.1 convolution_convert_fusion.1
  803.7 7.1 convolution_convert_fusion
  831.1 254.8 %all-reduce.9.cloned.1.call-done = bf16[512,4,2048]{2,1,0:T(4,128)(2,1)} async-done(((bf16[512,4,2048]{2,1,0:T(4,128)(2,1)}), bf16[512,4,2048]{2,1,0:T(4,128)(2,1)}) %all-reduce.9.cloned.1.call-update) | async-done | bytes 8388624
  1090.1 5.9 fusion.50
  1105.1 19.8 %scatter-add.6 = f32[128,4,2048]{2,1,0:T(4,128)} dynamic-update-slice(f32[128,4,2048]{2,1,0:T(4,128)} %copy-done.5, f32[128,1,2048]{2,1,0:T(1,128)} %slice_add_fusion, s32[]{:T(128)} %constant.217.clone.1, s32[]{:T(128)} %constant.232.clone.1, s32[]{:T(128)} %constant.217.clone.1) | dynamic-update-slice | bytes 2097156 | tf_op jit(solution)/shard_map/scatter-add | solution.py:314
  1124.9 18.2 %fusion.148 = f32[128,2048,9]{1,2,0:T(8,128)} fusion(f32[128,4,2048]{2,1,0:T(4,128)} %scatter-add.6, f32[128,4,9]{2,1,0:T(4,128)S(1)} %copy-done.12), kind=kOutput, calls=%fused_computation.221 | convolution fusion | flops 113246208 | bytes 13649920 | tf_op jit(solution)/shard_map/tcj,tcd->jtd/dot_general | solution.py:318
  1147.7 9.2 fusion.145
  1161.9 20.7 %scatter-add.9 = f32[9,128,2048]{2,0,1:T(8,128)} dynamic-update-slice(f32[9,128,2048]{2,0,1:T(8,128)} %bitcast.29, f32[1,128,2048]{2,0,1:T(1,128)S(1)} %copy.219, s32[]{:T(128)} %constant.233.clone.1, s32[]{:T(128)} %constant.217.clone.1, s32[]{:T(128)} %constant.217.clone.1) | dynamic-update-slice | bytes 2097156 | tf_op jit(solution)/shard_map/scatter-add | solution.py:330
  1182.6 7.0 convert_element_type.194
  1197.1 40.1 %all-reduce.1 = (f32[4,2048]{1,0:T(4,128)}, f32[40,36]{1,0:T(8,128)}, f32[36]{0:T(128)}) all-reduce(f32[4,2048]{1,0:T(4,128)S(1)} %get-tuple-element.475, f32[40,36]{1,0:T(8,128)S(1)} %fusion.150, f32[36]{0:T(128)S(1)} %reduce_sum.119), channel_id=1, replica_groups=mesh['seq'=8,'head'=4] {'seq','head'}, use_global_device_ids=true, to_apply=%region_18.19 | all-reduce | flops 9668 | bytes 77344 | tf_op jit(solution)/shard_map/psum | solution.py:339
  1237.2 165.8 %all-reduce.11.cloned.1.call-done = (bf16[2048,512]{1,0:T(8,128)(2,1)}, bf16[2048,512]{1,0:T(8,128)(2,1)}, bf16[2048,512]{1,0:T(8,128)(2,1)}, bf16[512,2048]{1,0...) async-done(((bf16[2048,512]{1,0:T(8,128)(2,1)}, bf16[2048,512]{1,0:T(8,128)(2,1)}, bf16[2048,512]{1,0:T(8,128)(2,1)}, bf16[512,2048]{1,0:T(8,128)(2,1)}, ...) | async-done | bytes 25165840 | tf_op jit(solution)/shard_map/psum | solution.py:332
  1415.2 11.7 convert_element_type.204
  1426.9 11.9 convert_element_type.206
  1438.7 95.9 %all-reduce.7.cloned.1.call-done = f32[2048,40]{0,1:T(8,128)} async-done(((f32[2048,40]{0,1:T(8,128)}), f32[2048,40]{0,1:T(8,128)}) %all-reduce.7.cloned.1.call-update) | async-done | bytes 327696 | tf_op jit(solution)/shard_map/psum | solution.py:339
  (652 shorter events, 545.6 us)
Async XLA Ops:
  7.2 173.8 %all-gather.3.cloned.1.call-start = ((), (), s32[]{:S(2)}) async-start(), calls=%async_computation.1 | async-start | bytes 10485760 | tf_op jit(solution)/shard_map/all_gather | solution.py:132
  28.5 198.2 %all-gather.5.cloned.1.call-start = ((), (), s32[]{:S(2)}) async-start(), calls=%async_computation.3 | async-start | bytes 2621440 | tf_op jit(solution)/shard_map/all_gather | solution.py:213
  29.3 799.6 %reduce-scatter.2.cloned.1.call-start = ((), (), s32[]{:S(2)}) async-start(), calls=%async_computation.2 | async-start | bytes 2621440 | tf_op jit(solution)/shard_map/reduce_scatter | solution.py:203
  294.4 13.6 collective-permute-start
  338.6 13.6 collective-permute-start
  382.9 13.6 collective-permute-start
  405.0 13.6 collective-permute-start
  436.0 649.9 %all-reduce.9.cloned.1.call-start = ((), (), s32[]{:S(2)}) async-start(), calls=%async_computation.5 | async-start | bytes 16777216
  455.6 22.0 %collective-permute-start.4 = (bf16[512,4,128]{2,0,1:T(8,128)(2,1)}, bf16[512,4,128]{2,0,1:T(8,128)(2,1)}, u32[]{:S(2)}, u32[]{:S(2)}) collective-permute-start(bf16[512,4,128]{2,0,1:T(8,128)(2,1)} %fusion.250), channel_id=1, source_target_pairs={{0,4},{4,8},{8,12},{12,16},{16,20},{20,24},{24,28},{28,0},{1,5},{5... | collective-permute-start | bytes 1572872 | tf_op jit(solution)/shard_map/while/body/eval_jaxpr/ppermute | solution.py:25
  460.9 18.8 %collective-permute-start.5 = (bf16[512,4,128]{2,0,1:T(8,128)(2,1)}, bf16[512,4,128]{2,0,1:T(8,128)(2,1)}, u32[]{:S(2)}, u32[]{:S(2)}) collective-permute-start(bf16[512,4,128]{2,0,1:T(8,128)(2,1)} %fusion.251), channel_id=1, source_target_pairs={{0,4},{4,8},{8,12},{12,16},{16,20},{20,24},{24,28},{28,0},{1,5},{5... | collective-permute-start | bytes 1572872 | tf_op jit(solution)/shard_map/while/body/eval_jaxpr/ppermute | solution.py:25
  464.1 17.7 %collective-permute-start.2 = (bf16[512,4,128]{2,0,1:T(8,128)(2,1)S(1)}, bf16[512,4,128]{2,0,1:T(8,128)(2,1)}, u32[]{:S(2)}, u32[]{:S(2)}) collective-permute-start(bf16[512,4,128]{2,0,1:T(8,128)(2,1)S(1)} %copy.308), channel_id=1, source_target_pairs={{0,4},{4,8},{8,12},{12,16},{16,20},{20,24},{24,28},{1,5},{5,9},{9,... | collective-permute-start | bytes 1572872 | tf_op jit(solution)/shard_map/while/body/eval_jaxpr/ppermute | solution.py:20
  495.7 23.7 %collective-permute-start.4 = (bf16[512,4,128]{2,0,1:T(8,128)(2,1)}, bf16[512,4,128]{2,0,1:T(8,128)(2,1)}, u32[]{:S(2)}, u32[]{:S(2)}) collective-permute-start(bf16[512,4,128]{2,0,1:T(8,128)(2,1)} %fusion.250), channel_id=1, source_target_pairs={{0,4},{4,8},{8,12},{12,16},{16,20},{20,24},{24,28},{28,0},{1,5},{5... | collective-permute-start | bytes 1572872 | tf_op jit(solution)/shard_map/while/body/eval_jaxpr/ppermute | solution.py:25
  501.9 19.5 %collective-permute-start.5 = (bf16[512,4,128]{2,0,1:T(8,128)(2,1)}, bf16[512,4,128]{2,0,1:T(8,128)(2,1)}, u32[]{:S(2)}, u32[]{:S(2)}) collective-permute-start(bf16[512,4,128]{2,0,1:T(8,128)(2,1)} %fusion.251), channel_id=1, source_target_pairs={{0,4},{4,8},{8,12},{12,16},{16,20},{20,24},{24,28},{28,0},{1,5},{5... | collective-permute-start | bytes 1572872 | tf_op jit(solution)/shard_map/while/body/eval_jaxpr/ppermute | solution.py:25
  504.4 19.1 %collective-permute-start.2 = (bf16[512,4,128]{2,0,1:T(8,128)(2,1)S(1)}, bf16[512,4,128]{2,0,1:T(8,128)(2,1)}, u32[]{:S(2)}, u32[]{:S(2)}) collective-permute-start(bf16[512,4,128]{2,0,1:T(8,128)(2,1)S(1)} %copy.308), channel_id=1, source_target_pairs={{0,4},{4,8},{8,12},{12,16},{16,20},{20,24},{24,28},{1,5},{5,9},{9,... | collective-permute-start | bytes 1572872 | tf_op jit(solution)/shard_map/while/body/eval_jaxpr/ppermute | solution.py:20
  537.4 22.5 %collective-permute-start.4 = (bf16[512,4,128]{2,0,1:T(8,128)(2,1)}, bf16[512,4,128]{2,0,1:T(8,128)(2,1)}, u32[]{:S(2)}, u32[]{:S(2)}) collective-permute-start(bf16[512,4,128]{2,0,1:T(8,128)(2,1)} %fusion.250), channel_id=1, source_target_pairs={{0,4},{4,8},{8,12},{12,16},{16,20},{20,24},{24,28},{28,0},{1,5},{5... | collective-permute-start | bytes 1572872 | tf_op jit(solution)/shard_map/while/body/eval_jaxpr/ppermute | solution.py:25
  542.4 19.6 %collective-permute-start.5 = (bf16[512,4,128]{2,0,1:T(8,128)(2,1)}, bf16[512,4,128]{2,0,1:T(8,128)(2,1)}, u32[]{:S(2)}, u32[]{:S(2)}) collective-permute-start(bf16[512,4,128]{2,0,1:T(8,128)(2,1)} %fusion.251), channel_id=1, source_target_pairs={{0,4},{4,8},{8,12},{12,16},{16,20},{20,24},{24,28},{28,0},{1,5},{5... | collective-permute-start | bytes 1572872 | tf_op jit(solution)/shard_map/while/body/eval_jaxpr/ppermute | solution.py:25
  544.9 19.2 %collective-permute-start.2 = (bf16[512,4,128]{2,0,1:T(8,128)(2,1)S(1)}, bf16[512,4,128]{2,0,1:T(8,128)(2,1)}, u32[]{:S(2)}, u32[]{:S(2)}) collective-permute-start(bf16[512,4,128]{2,0,1:T(8,128)(2,1)S(1)} %copy.308), channel_id=1, source_target_pairs={{0,4},{4,8},{8,12},{12,16},{16,20},{20,24},{24,28},{1,5},{5,9},{9,... | collective-permute-start | bytes 1572872 | tf_op jit(solution)/shard_map/while/body/eval_jaxpr/ppermute | solution.py:20
  577.9 22.5 %collective-permute-start.4 = (bf16[512,4,128]{2,0,1:T(8,128)(2,1)}, bf16[512,4,128]{2,0,1:T(8,128)(2,1)}, u32[]{:S(2)}, u32[]{:S(2)}) collective-permute-start(bf16[512,4,128]{2,0,1:T(8,128)(2,1)} %fusion.250), channel_id=1, source_target_pairs={{0,4},{4,8},{8,12},{12,16},{16,20},{20,24},{24,28},{28,0},{1,5},{5... | collective-permute-start | bytes 1572872 | tf_op jit(solution)/shard_map/while/body/eval_jaxpr/ppermute | solution.py:25
  582.9 19.6 %collective-permute-start.5 = (bf16[512,4,128]{2,0,1:T(8,128)(2,1)}, bf16[512,4,128]{2,0,1:T(8,128)(2,1)}, u32[]{:S(2)}, u32[]{:S(2)}) collective-permute-start(bf16[512,4,128]{2,0,1:T(8,128)(2,1)} %fusion.251), channel_id=1, source_target_pairs={{0,4},{4,8},{8,12},{12,16},{16,20},{20,24},{24,28},{28,0},{1,5},{5... | collective-permute-start | bytes 1572872 | tf_op jit(solution)/shard_map/while/body/eval_jaxpr/ppermute | solution.py:25
  585.3 19.2 %collective-permute-start.2 = (bf16[512,4,128]{2,0,1:T(8,128)(2,1)S(1)}, bf16[512,4,128]{2,0,1:T(8,128)(2,1)}, u32[]{:S(2)}, u32[]{:S(2)}) collective-permute-start(bf16[512,4,128]{2,0,1:T(8,128)(2,1)S(1)} %copy.308), channel_id=1, source_target_pairs={{0,4},{4,8},{8,12},{12,16},{16,20},{20,24},{24,28},{1,5},{5,9},{9,... | collective-permute-start | bytes 1572872 | tf_op jit(solution)/shard_map/while/body/eval_jaxpr/ppermute | solution.py:20
  618.4 22.5 %collective-permute-start.4 = (bf16[512,4,128]{2,0,1:T(8,128)(2,1)}, bf16[512,4,128]{2,0,1:T(8,128)(2,1)}, u32[]{:S(2)}, u32[]{:S(2)}) collective-permute-start(bf16[512,4,128]{2,0,1:T(8,128)(2,1)} %fusion.250), channel_id=1, source_target_pairs={{0,4},{4,8},{8,12},{12,16},{16,20},{20,24},{24,28},{28,0},{1,5},{5... | collective-permute-start | bytes 1572872 | tf_op jit(solution)/shard_map/while/body/eval_jaxpr/ppermute | solution.py:25
  623.4 19.6 %collective-permute-start.5 = (bf16[512,4,128]{2,0,1:T(8,128)(2,1)}, bf16[512,4,128]{2,0,1:T(8,128)(2,1)}, u32[]{:S(2)}, u32[]{:S(2)}) collective-permute-start(bf16[512,4,128]{2,0,1:T(8,128)(2,1)} %fusion.251), channel_id=1, source_target_pairs={{0,4},{4,8},{8,12},{12,16},{16,20},{20,24},{24,28},{28,0},{1,5},{5... | collective-permute-start | bytes 1572872 | tf_op jit(solution)/shard_map/while/body/eval_jaxpr/ppermute | solution.py:25
  625.9 19.2 %collective-permute-start.2 = (bf16[512,4,128]{2,0,1:T(8,128)(2,1)S(1)}, bf16[512,4,128]{2,0,1:T(8,128)(2,1)}, u32[]{:S(2)}, u32[]{:S(2)}) collective-permute-start(bf16[512,4,128]{2,0,1:T(8,128)(2,1)S(1)} %copy.308), channel_id=1, source_target_pairs={{0,4},{4,8},{8,12},{12,16},{16,20},{20,24},{24,28},{1,5},{5,9},{9,... | collective-permute-start | bytes 1572872 | tf_op jit(solution)/shard_map/while/body/eval_jaxpr/ppermute | solution.py:20
  658.9 22.5 %collective-permute-start.4 = (bf16[512,4,128]{2,0,1:T(8,128)(2,1)}, bf16[512,4,128]{2,0,1:T(8,128)(2,1)}, u32[]{:S(2)}, u32[]{:S(2)}) collective-permute-start(bf16[512,4,128]{2,0,1:T(8,128)(2,1)} %fusion.250), channel_id=1, source_target_pairs={{0,4},{4,8},{8,12},{12,16},{16,20},{20,24},{24,28},{28,0},{1,5},{5... | collective-permute-start | bytes 1572872 | tf_op jit(solution)/shard_map/while/body/eval_jaxpr/ppermute | solution.py:25
  663.9 19.6 %collective-permute-start.5 = (bf16[512,4,128]{2,0,1:T(8,128)(2,1)}, bf16[512,4,128]{2,0,1:T(8,128)(2,1)}, u32[]{:S(2)}, u32[]{:S(2)}) collective-permute-start(bf16[512,4,128]{2,0,1:T(8,128)(2,1)} %fusion.251), channel_id=1, source_target_pairs={{0,4},{4,8},{8,12},{12,16},{16,20},{20,24},{24,28},{28,0},{1,5},{5... | collective-permute-start | bytes 1572872 | tf_op jit(solution)/shard_map/while/body/eval_jaxpr/ppermute | solution.py:25
  666.3 19.2 %collective-permute-start.2 = (bf16[512,4,128]{2,0,1:T(8,128)(2,1)S(1)}, bf16[512,4,128]{2,0,1:T(8,128)(2,1)}, u32[]{:S(2)}, u32[]{:S(2)}) collective-permute-start(bf16[512,4,128]{2,0,1:T(8,128)(2,1)S(1)} %copy.308), channel_id=1, source_target_pairs={{0,4},{4,8},{8,12},{12,16},{16,20},{20,24},{24,28},{1,5},{5,9},{9,... | collective-permute-start | bytes 1572872 | tf_op jit(solution)/shard_map/while/body/eval_jaxpr/ppermute | solution.py:20
  699.4 22.5 %collective-permute-start.4 = (bf16[512,4,128]{2,0,1:T(8,128)(2,1)}, bf16[512,4,128]{2,0,1:T(8,128)(2,1)}, u32[]{:S(2)}, u32[]{:S(2)}) collective-permute-start(bf16[512,4,128]{2,0,1:T(8,128)(2,1)} %fusion.250), channel_id=1, source_target_pairs={{0,4},{4,8},{8,12},{12,16},{16,20},{20,24},{24,28},{28,0},{1,5},{5... | collective-permute-start | bytes 1572872 | tf_op jit(solution)/shard_map/while/body/eval_jaxpr/ppermute | solution.py:25
  704.4 19.6 %collective-permute-start.5 = (bf16[512,4,128]{2,0,1:T(8,128)(2,1)}, bf16[512,4,128]{2,0,1:T(8,128)(2,1)}, u32[]{:S(2)}, u32[]{:S(2)}) collective-permute-start(bf16[512,4,128]{2,0,1:T(8,128)(2,1)} %fusion.251), channel_id=1, source_target_pairs={{0,4},{4,8},{8,12},{12,16},{16,20},{20,24},{24,28},{28,0},{1,5},{5... | collective-permute-start | bytes 1572872 | tf_op jit(solution)/shard_map/while/body/eval_jaxpr/ppermute | solution.py:25
  706.9 19.2 %collective-permute-start.2 = (bf16[512,4,128]{2,0,1:T(8,128)(2,1)S(1)}, bf16[512,4,128]{2,0,1:T(8,128)(2,1)}, u32[]{:S(2)}, u32[]{:S(2)}) collective-permute-start(bf16[512,4,128]{2,0,1:T(8,128)(2,1)S(1)} %copy.308), channel_id=1, source_target_pairs={{0,4},{4,8},{8,12},{12,16},{16,20},{20,24},{24,28},{1,5},{5,9},{9,... | collective-permute-start | bytes 1572872 | tf_op jit(solution)/shard_map/while/body/eval_jaxpr/ppermute | solution.py:20
  738.4 19.9 %collective-permute-start.6 = (bf16[512,4,128]{0,2,1:T(8,128)(2,1)}, bf16[512,4,128]{0,2,1:T(8,128)(2,1)S(1)}, u32[]{:S(2)}, u32[]{:S(2)}) collective-permute-start(bf16[512,4,128]{0,2,1:T(8,128)(2,1)} %fusion.99), channel_id=1, source_target_pairs={{0,4},{4,8},{8,12},{12,16},{16,20},{20,24},{24,28},{28,0},{1,5},{5... | collective-permute-start | bytes 1572872 | tf_op jit(solution)/shard_map/ppermute | solution.py:25
  790.3 612.8 %all-reduce.11.cloned.1.call-start = ((), (), s32[]{:S(2)}) async-start(), calls=%async_computation.6 | async-start | bytes 50331648 | tf_op jit(solution)/shard_map/psum | solution.py:332
  824.0 710.6 %all-reduce.7.cloned.1.call-start = ((), (), s32[]{:S(2)}) async-start(), calls=%async_computation.4 | async-start | bytes 655360 | tf_op jit(solution)/shard_map/psum | solution.py:339
  (156 other events, 3061.7 us)
Sparse Core Ops, SparseCore 0:
  28.6 152.3 all-gather.2
  182.6 44.1 all-gather.4
  436.1 51.8 reduce-scatter.1
  790.4 295.4 all-reduce.8
  1092.5 310.5 all-reduce.10
  1408.8 125.7 all-reduce.6
where the time goes:
time: 1560 us; the launch traced here: 1540 us
  waiting for transfers between devices  664 us (43%)
  matrix products  285 us (18%)
  local copies, waits for them, and re-layouts  210 us (13%)
  starting transfers between devices  194 us (12%)
  other arithmetic  123 us (8%)
  blocking collectives  40.1 us (3%)
  between operations  16.1 us (1%)
    unnamed x7, waiting for transfers between devices  256 us
    psum x1, waiting for transfers between devices, body(): lax.psum(grad_w_query.astype(jnp.bfloat16), 'seq').astype(jnp.float32)  166 us
    ppermute x28, starting transfers between devices, from_behind(): return lax.ppermute(block, axis, route)  151 us
    all_gather x1, waiting for transfers between devices, body(): gathered = lax.all_gather(normed, 'head', axis=0, tiled=True)  136 us
    psum x1, waiting for transfers between devices, body(): lax.psum((grad_gains, grad_mix_in, grad_mix_out, grad_bias), ('seq', 'hea...  95.9 us
    while x161, local copies, waits for them, and re-layouts  46.1 us
    ppermute x16, starting transfers between devices, passed_along(): return lax.ppermute(x, axis, [(i, (i + by) % count) for i in range(count)])  42.6 us
    psum x1, blocking collectives, body(): lax.psum((grad_gains, grad_mix_in, grad_mix_out, grad_bias), ('seq', 'hea...  40.1 us
  transfers between devices with their start and end apart: 50, of which 6 were waited for; matrix products, arithmetic and copies ran while one was open for 32% of the time, Pallas kernels for 0%

commit v1 on v0

v1 whole, which is shorter than its diff:
```python
import functools

import jax
import jax.numpy as jnp
from jax import lax
from jax.experimental import pallas as pl
from jax.experimental.pallas import tpu as pltpu
from jax.sharding import PartitionSpec as P

HD = 128
ROT = 32
HALF = ROT // 2
MIB = 1024 * 1024

eps_norm = 1e-05
eps_rms = 1e-06
rope_base = 10000.0
hidden_mask = -1e30
highest = lax.Precision.HIGHEST
f32 = jnp.float32
bf16 = jnp.bfloat16
sqrt_half = 0.7071067811865476
inv_sqrt_2pi = 0.3989422804014327
log2e = 1.4426950408889634


def vmem():
    return pl.BlockSpec(memory_space=pltpu.VMEM)


def params(mib, **more):
    return pltpu.CompilerParams(vmem_limit_bytes=mib * MIB, **more)


def cdf(x):
    return 0.5 * (1.0 + lax.erf(x * sqrt_half))


def pdf(x):
    return jnp.exp(x * x * -0.5) * inv_sqrt_2pi


def dot(a, b):
    return jnp.dot(a, b, preferred_element_type=f32)


def dot_nt(a, b):
    return lax.dot_general(a, b, (((1,), (1,)), ((), ())), preferred_element_type=f32)


def dot_tn(a, b):
    return lax.dot_general(a, b, (((0,), (0,)), ((), ())), preferred_element_type=f32)


def mix_kernel(tile, hist, gains, mix_in, mix_out, mix_bias, n3, nkv, nq, streams, coef, mix_pre):
    hist_count, rows, width = hist.shape
    count = gains.shape[0]
    newest = hist[hist_count - 1].astype(f32)
    scale = lax.rsqrt(jnp.mean(newest * newest, axis=-1, keepdims=True) + eps_rms)
    rms_low = (newest * scale).astype(bf16)
    pre = dot(rms_low, mix_in[...])
    mix_pre[...] = pre
    hidden = (pre * cdf(pre)).astype(bf16)
    coef[...] = dot(hidden, mix_out[...]) + mix_bias[...]
    chunk = 512

    def step(i, carry):
        at = pl.ds(pl.multiple_of(i * tile, tile), tile)
        rows_coef = coef[at, :]
        columns = [
            [rows_coef[:, c * hist_count + j : c * hist_count + j + 1] for j in range(hist_count)]
            for c in range(count)
        ]
        totals = [jnp.zeros((tile, 1), f32) for _ in range(count)]
        for lane in range(0, width, chunk):
            sums = [jnp.zeros((tile, chunk), f32) for _ in range(count)]
            for j in range(hist_count):
                h = hist[j, at, lane : lane + chunk].astype(f32)
                for c in range(count):
                    sums[c] = sums[c] + columns[c][j] * h
            for c in range(count):
                streams[c, at, lane : lane + chunk] = sums[c]
                totals[c] = totals[c] + jnp.sum(sums[c], axis=-1, keepdims=True)
        for c in range(count):
            x = streams[c, at, :]
            centre = x - totals[c] * (1.0 / width)
            spread = jnp.mean(centre * centre, axis=-1, keepdims=True)
            out = (centre * lax.rsqrt(spread + eps_norm) * gains[c : c + 1, :]).astype(bf16)
            if c == 0:
                nq[at, :] = out
            elif c == 3:
                n3[at, :] = out
            else:
                nkv[at, (c - 1) * width : c * width] = out
        return carry

    lax.fori_loop(0, rows // tile, step, 0)


def mix_forward(histories, norm_gains, mix_in, mix_out, mix_bias):
    hist_count, rows, width = histories.shape
    count = norm_gains.shape[0]
    return pl.pallas_call(
        functools.partial(mix_kernel, 16),
        out_shape=(
            jax.ShapeDtypeStruct((rows, width), bf16),
            jax.ShapeDtypeStruct((rows, 2 * width), bf16),
            jax.ShapeDtypeStruct((rows, width), bf16),
            jax.ShapeDtypeStruct((count, rows, width), f32),
            jax.ShapeDtypeStruct((rows, count * hist_count), f32),
            jax.ShapeDtypeStruct((rows, mix_in.shape[1]), f32),
        ),
        in_specs=[vmem()] * 5,
        out_specs=[vmem()] * 6,
        compiler_params=params(48),
        name="mix_forward",
    )(histories, norm_gains, mix_in, mix_out, mix_bias)


def unmix_kernel(
    hist, streams, gn3, gnkv, gnq, cot, coef, mix_pre, gains, mix_in, mix_out, ghist, pack, gs, rms_keep, hid_keep, gc_keep, gmp_keep
):
    hist_count, tile, width = hist.shape
    count = gains.shape[0]
    hidden_units = mix_in.shape[1]
    step = pl.program_id(0)

    @pl.when(step == 0)
    def _():
        pack[...] = jnp.zeros_like(pack)

    for c in range(count):
        x = streams[c]
        centre = x - jnp.mean(x, axis=-1, keepdims=True)
        inv = lax.rsqrt(jnp.mean(centre * centre, axis=-1, keepdims=True) + eps_norm)
        unit = centre * inv
        if c == 0:
            g = gnq[...].astype(f32)
        elif c == 3:
            g = gn3[...].astype(f32)
        else:
            g = gnkv[:, (c - 1) * width : c * width].astype(f32)
        pack[hidden_units + c : hidden_units + c + 1, 0:width] += jnp.sum(g * unit, axis=0, keepdims=True)
        d = g * gains[c : c + 1, :]
        out = inv * (
            d
            - jnp.mean(d, axis=-1, keepdims=True)
            - unit * jnp.mean(d * unit, axis=-1, keepdims=True)
        )
        if c == 3:
            out = out + cot[...].astype(f32)
        gs[c] = out
    lanes = lax.broadcasted_iota(jnp.int32, (tile, count * hist_count), 1)
    gc = jnp.zeros((tile, count * hist_count), f32)
    rows_coef = coef[...]
    for j in range(hist_count):
        h = hist[j].astype(f32)
        for c in range(count):
            k = c * hist_count + j
            gc = jnp.where(lanes == k, jnp.sum(gs[c] * h, axis=-1, keepdims=True), gc)
    for j in range(hist_count):
        total = rows_coef[:, j : j + 1] * gs[0]
        for c in range(1, count):
            k = c * hist_count + j
            total = total + rows_coef[:, k : k + 1] * gs[c]
        if j < hist_count - 1:
            ghist[j] = total.astype(bf16)
    pre = mix_pre[...]
    phi = cdf(pre)
    gmh = lax.dot_general(
        gc, mix_out[...].astype(f32), (((1,), (1,)), ((), ())), precision=highest
    )
    gmp = (phi + pre * pdf(pre)) * gmh
    gmp_low = gmp.astype(bf16)
    grad_rms = dot_nt(gmp_low, mix_in[...])
    newest = hist[hist_count - 1].astype(f32)
    scale = lax.rsqrt(jnp.mean(newest * newest, axis=-1, keepdims=True) + eps_rms)
    inner = jnp.mean(grad_rms * newest, axis=-1, keepdims=True)
    total = total + scale * grad_rms - newest * (scale * scale * scale * inner)
    ghist[hist_count - 1] = total.astype(bf16)
    at = pl.ds(pl.multiple_of(step * tile, tile), tile)
    rms_keep[at, :] = (newest * scale).astype(bf16)
    hid_keep[at, :] = (pre * phi).astype(bf16).astype(f32)
    gc_keep[at, :] = gc
    gmp_keep[at, :] = gmp_low

    @pl.when(step == pl.num_programs(0) - 1)
    def _():
        pack[0:hidden_units, 0:width] = dot_tn(gmp_keep[...], rms_keep[...])
        pack[0:hidden_units, width : width + count * hist_count] = lax.dot_general(
            hid_keep[...], gc_keep[...], (((0,), (0,)), ((), ())), precision=highest
        )
        pack[hidden_units : hidden_units + 1, width : width + count * hist_count] = jnp.sum(
            gc_keep[...], axis=0, keepdims=True
        )


def unmix(histories, streams, gn3, gnkv, gnq, cotangent, coef, mix_pre, norm_gains, mix_in, mix_out):
    hist_count, rows, width = histories.shape
    count = norm_gains.shape[0]
    units = mix_in.shape[1]
    mixes = count * hist_count
    tile = 16
    whole = lambda shape: pl.BlockSpec(shape, lambda i: (0, 0))
    return pl.pallas_call(
        unmix_kernel,
        grid=(rows // tile,),
        out_shape=(
            jax.ShapeDtypeStruct((hist_count, rows, width), bf16),
            jax.ShapeDtypeStruct((units + 8, width + 128), f32),
        ),
        in_specs=[
            pl.BlockSpec((hist_count, tile, width), lambda i: (0, i, 0)),
            pl.BlockSpec((count, tile, width), lambda i: (0, i, 0)),
            pl.BlockSpec((tile, width), lambda i: (i, 0)),
            pl.BlockSpec((tile, 2 * width), lambda i: (i, 0)),
            pl.BlockSpec((tile, width), lambda i: (i, 0)),
            pl.BlockSpec((tile, width), lambda i: (i, 0)),
            pl.BlockSpec((tile, mixes), lambda i: (i, 0)),
            pl.BlockSpec((tile, units), lambda i: (i, 0)),
            whole((count, width)),
            whole((width, units)),
            whole((units, mixes)),
        ],
        out_specs=[
            pl.BlockSpec((hist_count, tile, width), lambda i: (0, i, 0)),
            whole((units + 8, width + 128)),
        ],
        scratch_shapes=[
            pltpu.VMEM((count, tile, width), f32),
            pltpu.VMEM((rows, width), bf16),
            pltpu.VMEM((rows, units), f32),
            pltpu.VMEM((rows, mixes), f32),
            pltpu.VMEM((rows, units), bf16),
        ],
        compiler_params=params(48),
        name="unmix",
    )(histories, streams, gn3, gnkv, gnq, cotangent, coef, mix_pre, norm_gains, mix_in, mix_out)


def ff_kernel(n3, cot, w_up, w_down, ff_out, gn3, gw_up, gw_down, out_acc, gn_acc):
    step = pl.program_id(0)
    last = pl.num_programs(0) - 1
    pre = dot(n3[...], w_up[...])
    phi = cdf(pre)
    act = (pre * phi).astype(bf16)
    slope = phi + pre * pdf(pre)
    grad = (dot_nt(cot[...], w_down[...]) * slope).astype(bf16)
    gw_down[...] = dot_tn(act, cot[...]).astype(bf16)
    gw_up[...] = dot_tn(n3[...], grad).astype(bf16)
    part_out = dot(act, w_down[...])
    part_gn = dot_nt(grad, w_up[...])

    @pl.when(step == 0)
    def _():
        out_acc[...] = part_out
        gn_acc[...] = part_gn

    @pl.when(step > 0)
    def _():
        out_acc[...] += part_out
        gn_acc[...] += part_gn

    @pl.when(step == last)
    def _():
        ff_out[...] = out_acc[...]
        gn3[...] = gn_acc[...].astype(bf16)


def feed_forward(n3, cot, w_up, w_down):
    rows, width = n3.shape
    hidden = w_up.shape[1]
    block = min(512, hidden)
    fixed = pl.BlockSpec((rows, width), lambda i: (0, 0))
    return pl.pallas_call(
        ff_kernel,
        grid=(hidden // block,),
        out_shape=(
            jax.ShapeDtypeStruct((rows, width), f32),
            jax.ShapeDtypeStruct((rows, width), bf16),
            jax.ShapeDtypeStruct((width, hidden), bf16),
            jax.ShapeDtypeStruct((hidden, width), bf16),
        ),
        in_specs=[
            fixed,
            fixed,
            pl.BlockSpec((width, block), lambda i: (0, i)),
            pl.BlockSpec((block, width), lambda i: (i, 0)),
        ],
        out_specs=[
            fixed,
            fixed,
            pl.BlockSpec((width, block), lambda i: (0, i)),
            pl.BlockSpec((block, width), lambda i: (i, 0)),
        ],
        scratch_shapes=[pltpu.VMEM((rows, width), f32), pltpu.VMEM((rows, width), f32)],
        compiler_params=params(60),
        cost_estimate=pl.CostEstimate(
            flops=12 * rows * width * hidden, bytes_accessed=8 * width * hidden, transcendentals=0
        ),
        name="feed_forward",
    )(n3, cot, w_up, w_down)


def turn(x, same, down, up):
    return x * same + pltpu.roll(x, HD - HALF, 1) * down + pltpu.roll(x, HALF, 1) * up


def rotated(x, same, down, up):
    heads = [
        turn(x[:, h : h + HD], same, down, up).astype(bf16) for h in range(0, x.shape[1], HD)
    ]
    return jnp.concatenate(heads, axis=1)


def query_kernel(n, w, same, down, up, out):
    out[...] = rotated(dot(n[...], w[...]), same[...], down[...], up[...])


def key_value_kernel(n, wk, wv, same, down, up, key, value):
    width = wk.shape[0]
    key[...] = rotated(dot(n[:, 0:width], wk[...]), same[...], down[...], up[...])
    value[...] = dot(n[:, width : 2 * width], wv[...]).astype(bf16)


def project(kernel, n, weights, tables, outs, name):
    rows = n.shape[0]
    width, local = weights[0].shape
    block = min(256, rows)
    spec = lambda cols: pl.BlockSpec((block, cols), lambda i: (i, 0))
    return pl.pallas_call(
        kernel,
        grid=(rows // block,),
        out_shape=tuple(jax.ShapeDtypeStruct((rows, local), bf16) for _ in range(outs)),
        in_specs=[spec(n.shape[1])]
        + [pl.BlockSpec((width, local), lambda i: (0, 0))] * len(weights)
        + [spec(HD)] * 3,
        out_specs=tuple(spec(local) for _ in range(outs)),
        compiler_params=params(48),
        cost_estimate=pl.CostEstimate(
            flops=2 * rows * width * local * outs, bytes_accessed=8 * MIB, transcendentals=0
        ),
        name=name,
    )(n, *weights, *tables)


def rope_lanes(positions):
    frequency = rope_base ** (-(jnp.arange(HALF, dtype=f32) * 2.0 / ROT))
    angles = positions.astype(f32)[:, None] * frequency[None, :]
    cos, sin = jnp.cos(angles), jnp.sin(angles)
    rows = positions.shape[0]
    ones = jnp.ones((rows, HD - ROT), f32)
    zeros = jnp.zeros((rows, HD - HALF), f32)
    same = jnp.concatenate([cos, cos, ones], axis=1)
    down = jnp.concatenate([-sin, zeros], axis=1)
    up = jnp.concatenate([zeros[:, :HALF], sin, zeros[:, : HD - ROT]], axis=1)
    return (same, down, up)


def masked(scores, kb, block, first, last_seen):
    place = lax.broadcasted_iota(jnp.int32, scores.shape, 0) + kb * block
    seen = (place >= first) & (place <= last_seen)
    return jnp.where(seen, scores, hidden_mask)


def attend_kernel(scale2, info, kslot, vslot, q, k, v, span, out, lse, peak, total, acc):
    kb = pl.program_id(1)
    rank, reach = info[0], info[1]
    block = k.shape[0]

    @pl.when(kb == 0)
    def _():
        peak[...] = jnp.full_like(peak, hidden_mask)
        total[...] = jnp.zeros_like(total)
        acc[...] = jnp.zeros_like(acc)

    def update(scores):
        old = peak[...]
        new = jnp.maximum(old, jnp.max(scores, axis=0, keepdims=True))
        weights = jnp.exp2(scores - new)
        factor = jnp.exp2(old - new)
        peak[...] = new
        total[...] = total[...] * factor + jnp.sum(weights, axis=0, keepdims=True)
        acc[...] = acc[...] * factor + dot_tn(v[...], weights.astype(bf16))

    needs = (kb == rank) | (reach > kb * block)

    @pl.when((kb <= rank) & jnp.logical_not(needs))
    def _():
        update(dot_nt(k[...], q[...]) * scale2)

    @pl.when((kb <= rank) & needs)
    def _():
        scores = dot_nt(k[...], q[...]) * scale2
        update(masked(scores, kb, block, span[0:1, :], span[1:2, :]))

    @pl.when(kb == pl.num_programs(1) - 1)
    def _():
        out[...] = jnp.transpose(acc[...] / total[...]).astype(bf16)
        lse[...] = (peak[...] + jnp.log2(total[...]))[None]


def attend(q, k_all, v_all, info, kslot, vslot, span, blocks):
    rows, local = q.shape
    heads = local // HD
    block = k_all.shape[0] // blocks
    scale2 = HD ** (-0.5) * log2e
    grid_spec = pltpu.PrefetchScalarGridSpec(
        num_scalar_prefetch=3,
        grid=(heads, blocks),
        in_specs=[
            pl.BlockSpec((rows, HD), lambda h, b, info, ks, vs: (0, h)),
            pl.BlockSpec((block, HD), lambda h, b, info, ks, vs: (ks[jnp.minimum(b, info[0])], h)),
            pl.BlockSpec((block, HD), lambda h, b, info, ks, vs: (vs[jnp.minimum(b, info[0])], h)),
            pl.BlockSpec((8, rows), lambda h, b, info, ks, vs: (0, 0)),
        ],
        out_specs=[
            pl.BlockSpec((rows, HD), lambda h, b, info, ks, vs: (0, h)),
            pl.BlockSpec((1, 1, rows), lambda h, b, info, ks, vs: (h, 0, 0)),
        ],
        scratch_shapes=[
            pltpu.VMEM((1, rows), f32),
            pltpu.VMEM((1, rows), f32),
            pltpu.VMEM((HD, rows), f32),
        ],
    )
    return pl.pallas_call(
        functools.partial(attend_kernel, scale2),
        grid_spec=grid_spec,
        out_shape=(
            jax.ShapeDtypeStruct((rows, local), bf16),
            jax.ShapeDtypeStruct((heads, 1, rows), f32),
        ),
        compiler_params=params(32),
        cost_estimate=pl.CostEstimate(
            flops=8 * rows * block * blocks * local, bytes_accessed=8 * MIB, transcendentals=0
        ),
        name="attend",
    )(info, kslot, vslot, q, k_all, v_all, span)


def attend_back_kernel(
    scale, scale2, info, kslot, vslot, q, k, v, do, o, lse, span, same, down, up, gq, gk, gv, delta, acc
):
    kb = pl.program_id(1)
    rank, reach = info[0], info[1]
    block = k.shape[0]

    @pl.when(kb == 0)
    def _():
        both = do[...].astype(f32) * o[...].astype(f32)
        delta[...] = jnp.sum(jnp.transpose(both), axis=0, keepdims=True)
        acc[...] = jnp.zeros_like(acc)

    def update(scores):
        weights = jnp.exp2(scores - lse[0])
        gv[...] = dot(weights.astype(bf16), do[...]).astype(bf16)
        grad_weights = dot_nt(v[...], do[...])
        grad_scores = (weights * (grad_weights - delta[...])).astype(bf16)
        gk[...] = (dot(grad_scores, q[...]) * scale).astype(bf16)
        acc[...] += dot_tn(k[...], grad_scores)

    needs = (kb == rank) | (reach > kb * block)

    @pl.when((kb <= rank) & jnp.logical_not(needs))
    def _():
        update(dot_nt(k[...], q[...]) * scale2)

    @pl.when((kb <= rank) & needs)
    def _():
        scores = dot_nt(k[...], q[...]) * scale2
        update(masked(scores, kb, block, span[0:1, :], span[1:2, :]))

    @pl.when(kb > rank)
    def _():
        gk[...] = jnp.zeros_like(gk)
        gv[...] = jnp.zeros_like(gv)

    @pl.when(kb == pl.num_programs(1) - 1)
    def _():
        x = jnp.transpose(acc[...]) * scale
        gq[...] = turn(x, same[...], -down[...], -up[...]).astype(bf16)


def attend_back(q, k_all, v_all, do, o, lse, info, kslot, vslot, span, tables, blocks):
    rows, local = q.shape
    heads = local // HD
    block = k_all.shape[0] // blocks
    scale = HD ** (-0.5)
    at_query = pl.BlockSpec((rows, HD), lambda h, b, info, ks, vs: (0, h))
    table = pl.BlockSpec((rows, HD), lambda h, b, info, ks, vs: (0, 0))
    grid_spec = pltpu.PrefetchScalarGridSpec(
        num_scalar_prefetch=3,
        grid=(heads, blocks),
        in_specs=[
            at_query,
            pl.BlockSpec((block, HD), lambda h, b, info, ks, vs: (ks[jnp.minimum(b, info[0])], h)),
            pl.BlockSpec((block, HD), lambda h, b, info, ks, vs: (vs[jnp.minimum(b, info[0])], h)),
            at_query,
            at_query,
            pl.BlockSpec((1, 1, rows), lambda h, b, info, ks, vs: (h, 0, 0)),
            pl.BlockSpec((8, rows), lambda h, b, info, ks, vs: (0, 0)),
            table,
            table,
            table,
        ],
        out_specs=[
            at_query,
            pl.BlockSpec((block, HD), lambda h, b, info, ks, vs: (ks[b], h)),
            pl.BlockSpec((block, HD), lambda h, b, info, ks, vs: (vs[b], h)),
        ],
        scratch_shapes=[pltpu.VMEM((1, rows), f32), pltpu.VMEM((HD, rows), f32)],
    )
    return pl.pallas_call(
        functools.partial(attend_back_kernel, scale, scale * log2e),
        grid_spec=grid_spec,
        out_shape=(
            jax.ShapeDtypeStruct((rows, local), bf16),
            jax.ShapeDtypeStruct(k_all.shape, bf16),
            jax.ShapeDtypeStruct(v_all.shape, bf16),
        ),
        compiler_params=params(32),
        cost_estimate=pl.CostEstimate(
            flops=20 * rows * block * blocks * local, bytes_accessed=20 * MIB, transcendentals=0
        ),
        name="attend_back",
    )(info, kslot, vslot, q, k_all, v_all, do, o, lse, span, *tables)


def flipped(x, axis, bit):
    count = lax.axis_size(axis)
    return lax.ppermute(x, axis, [(i, i ^ bit) for i in range(count)])


def bits_of(count):
    bits = []
    while (1 << len(bits)) < count:
        bits.append(1 << len(bits))
    return bits


def slot_order(bits):
    order = [0]
    for bit in bits:
        order = order + [m | bit for m in order]
    return order


def slots_for(bits, rank, count):
    order = slot_order(bits)
    table = [0] * count
    for slot, m in enumerate(order):
        table[m] = slot
    return jnp.take(jnp.array(table, jnp.int32), jnp.arange(count, dtype=jnp.int32) ^ rank)


def collect(block, bits):
    pieces = [block]
    held = block
    for bit in bits:
        got = flipped(held, "seq", bit)
        pieces.append(got)
        held = jnp.concatenate([held, got], axis=0)
    return held


def summed(a, b):
    return (a.astype(f32) + b.astype(f32)).astype(bf16)


def disperse(parts, bits):
    held = parts
    for at, bit in enumerate(reversed(bits)):
        half = held.shape[0] // 2
        got = flipped(held[half:], "seq", bit)
        if at == len(bits) - 1:
            return held[:half].astype(f32) + got.astype(f32)
        held = summed(held[:half], got)
    return held.astype(f32)


def small_sum(x):
    x = x.astype(bf16)
    for axis in ("seq", "head"):
        for bit in bits_of(lax.axis_size(axis)):
            x = summed(x, flipped(x, axis, bit))
    return x.astype(f32)


def body(
    histories,
    norm_gains,
    mix_in,
    mix_out,
    mix_bias,
    w_query,
    w_key,
    w_value,
    w_out,
    w_up,
    w_down,
    cotangent,
    doc_ids,
    positions,
):
    seq_count = lax.axis_size("seq")
    rank = lax.axis_index("seq")
    block_rows = positions.shape[0]
    hist_count, tok_rows, width = histories.shape
    count = norm_gains.shape[0]
    units = mix_in.shape[1]
    mixes = mix_out.shape[1]

    def gather(x):
        return lax.all_gather(x, "head", axis=0, tiled=True)

    def scatter(x):
        return lax.psum_scatter(x, "head", scatter_dimension=0, tiled=True)

    tables = rope_lanes(positions)
    place = rank * block_rows + jnp.arange(block_rows, dtype=jnp.int32)
    first = place - positions
    span = jnp.concatenate([first[None], place[None], jnp.zeros((6, block_rows), jnp.int32)], axis=0)
    info = jnp.stack([rank.astype(jnp.int32), jnp.max(first)])
    bits = bits_of(seq_count)
    key_bits = bits[1:] + bits[:1]
    value_bits = bits[1:][::-1] + bits[:1]
    key_slots = slots_for(key_bits, rank, seq_count)
    value_slots = slots_for(value_bits, rank, seq_count)

    cot_full = gather(cotangent)
    n3, nkv, nq, streams, coef, mix_pre = mix_forward(
        histories, norm_gains, mix_in, mix_out, mix_bias[None, :]
    )
    n3_full = gather(n3)
    nkv_full = gather(nkv)
    nq_full = gather(nq)
    ff_out, gn3_part, gw_up, gw_down = feed_forward(n3_full, cot_full, w_up, w_down)
    gn3 = scatter(gn3_part)
    key, value = project(key_value_kernel, nkv_full, (w_key, w_value), tables, 2, "project_kv")
    (query,) = project(query_kernel, nq_full, (w_query,), tables, 1, "project_q")
    k_all = collect(key, key_bits)
    v_all = collect(value, value_bits)
    attended, lse = attend(query, k_all, v_all, info, key_slots, value_slots, span, seq_count)
    branch = scatter((ff_out + dot(attended, w_out)).astype(bf16))
    layer_out = (streams[3] + branch.astype(f32)).astype(bf16)
    do = dot_nt(cot_full, w_out).astype(bf16)
    gw_out = dot_tn(attended, cot_full).astype(bf16)
    gq, gk_parts, gv_parts = attend_back(
        query, k_all, v_all, do, attended, lse, info, key_slots, value_slots, span, tables, seq_count
    )
    gnq = scatter(dot_nt(gq, w_query).astype(bf16))
    gk_wide = disperse(gk_parts, key_bits)
    gv = disperse(gv_parts, value_bits).astype(bf16)
    same, down, up = tables
    heads = gk_wide.shape[1] // HD
    gk3 = gk_wide.reshape(block_rows, heads, HD)
    cos, sin = same[:, None, :HALF], -down[:, None, :HALF]
    a, b = gk3[..., :HALF], gk3[..., HALF:ROT]
    gk = (
        jnp.concatenate([a * cos + b * sin, b * cos - a * sin, gk3[..., ROT:]], axis=-1)
        .reshape(gk_wide.shape)
        .astype(bf16)
    )
    gnkv = scatter(jnp.concatenate([dot_nt(gk, w_key), dot_nt(gv, w_value)], axis=1).astype(bf16))
    gw_query = dot_tn(nq_full, gq).astype(bf16)
    gw_key = dot_tn(nkv_full[:, :width], gk).astype(bf16)
    gw_value = dot_tn(nkv_full[:, width:], gv).astype(bf16)
    ghist, pack = unmix(
        histories, streams, gn3, gnkv, gnq, cotangent, coef, mix_pre, norm_gains, mix_in, mix_out
    )
    big = lax.psum((gw_up, gw_down), "seq")
    tied = lax.optimization_barrier((gw_query, gw_key, gw_value, gw_out) + big)
    rest = lax.psum(tied[:4], "seq")
    big = tied[4:]
    pack = small_sum(pack)
    return (
        layer_out,
        ghist,
        pack[units : units + count, :width],
        jnp.transpose(pack[:units, :width]),
        pack[:units, width : width + mixes],
        pack[units, width : width + mixes],
        rest[0].astype(f32),
        rest[1].astype(f32),
        rest[2].astype(f32),
        rest[3].astype(f32),
        big[0].astype(f32),
        big[1].astype(f32),
    )


def solution(mesh):
    return jax.shard_map(
        body,
        mesh=mesh,
        in_specs=(
            P(None, ("seq", "head"), None),
            P(),
            P(),
            P(),
            P(),
            P(None, "head"),
            P(None, "head"),
            P(None, "head"),
            P("head", None),
            P(None, "head"),
            P("head", None),
            P(("seq", "head"), None),
            P(),
            P("seq"),
        ),
        out_specs=(
            P(("seq", "head"), None),
            P(None, ("seq", "head"), None),
            P(),
            P(),
            P(),
            P(),
            P(None, "head"),
            P(None, "head"),
            P(None, "head"),
            P("head", None),
            P(None, "head"),
            P("head", None),
        ),
        check_vma=False,
    )
```

time: 1560 us -> 867 us (0.56)
  matrix products: 285 us -> 25.7 us
  local copies, waits for them, and re-layouts: 210 us -> 41.6 us
  starting transfers between devices: 194 us -> 68.2 us
  waiting for transfers between devices: 664 us -> 555 us
  Pallas kernels: 0 us -> 88.7 us
  other arithmetic: 123 us -> 64.8 us
  blocking collectives: 40.1 us -> 0 us
    dot_general x83 -> x9, matrix products: 285 us -> 25.7 us  [the longest x4 13.5 us: dot_tn(): lax.dot_general(a, b, (((0,), (0,)), ((), ())), preferred_element_type=f32)]
    unnamed x7 -> x10, waiting for transfers between devices: 256 us -> 2 us
    reduce_scatter x1 -> x4, waiting for transfers between devices: 0.02 us -> 171 us  [scatter(): return lax.psum_scatter(x, 'head', scatter_dimension=0, tiled=True)]
    ppermute x44 -> x17, starting transfers between devices: 193 us -> 67.2 us  [flipped(): return lax.ppermute(x, axis, [(i, i ^ bit) for i in range(count)])]
    pallas_call x0 -> x7, Pallas kernels: none -> 88.7 us  [the longest x1 38.4 us: feed_forward(): pl.pallas_call(ff_kernel, grid=(hidden // block,), out_shape=(jax.ShapeDt...]
    psum x2, waiting for transfers between devices: 262 us -> 180 us  [the longest x1 120 us: body(): rest = lax.psum(tied[:4], 'seq')]
    ppermute x44 -> x17, waiting for transfers between devices: 4.38 us -> 82.1 us  [flipped(): return lax.ppermute(x, axis, [(i, i ^ bit) for i in range(count)])]
    while x165 -> x0, local copies, waits for them, and re-layouts: 51.8 us -> none
  transfers between devices with their start and end apart: 50 -> 27, of which waited for: 6 -> 15; matrix products, arithmetic and copies ran while one was open for 32% -> 12% of each run, Pallas kernels for 0% -> 10%
where the time goes in v1:
time: 867 us; the launch traced here: 859 us
  waiting for transfers between devices  555 us (64%)
  Pallas kernels  88.7 us (10%)
  starting transfers between devices  68.2 us (8%)
  other arithmetic  64.8 us (7%)
  local copies, waits for them, and re-layouts  41.6 us (5%)
  matrix products  25.7 us (3%)
  between operations  15.2 us (2%)
    reduce_scatter x4, waiting for transfers between devices, scatter(): return lax.psum_scatter(x, 'head', scatter_dimension=0, tiled=True)  171 us
    psum x1, waiting for transfers between devices, body(): rest = lax.psum(tied[:4], 'seq')  120 us
    all_gather x4, waiting for transfers between devices, gather(): return lax.all_gather(x, 'head', axis=0, tiled=True)  120 us
    ppermute x17, waiting for transfers between devices, flipped(): return lax.ppermute(x, axis, [(i, i ^ bit) for i in range(count)])  82.1 us
    ppermute x17, starting transfers between devices, flipped(): return lax.ppermute(x, axis, [(i, i ^ bit) for i in range(count)])  67.2 us
    psum x1, waiting for transfers between devices, body(): big = lax.psum((gw_up, gw_down), 'seq')  59.9 us
    pallas_call x1, Pallas kernels, feed_forward(): pl.pallas_call(ff_kernel, grid=(hidden // block,), out_shape=(jax.ShapeDt...  38.4 us
    unnamed x123, local copies, waits for them, and re-layouts  26.3 us
  transfers between devices with their start and end apart: 27, of which 15 were waited for; matrix products, arithmetic and copies ran while one was open for 12% of the time, Pallas kernels for 10%

profile of v1, /device:TPU:0, one launch (start us, length us, event | category | flops | bytes accessed | tf_op | source)
XLA Modules:
  0.0 859.4 jit_solution(10120440520470972281)
XLA Ops:
  11.3 10.1 %mix_forward.1 = (bf16[128,2048]{1,0:T(8,128)(2,1)}, bf16[128,4096]{1,0:T(8,128)(2,1)S(1)}, bf16[128,2048]{1,0:T(8,128)(2,1)}, f32[4,128,2048]{2,1,0:T(8,128)}, ...) custom-call(bf16[9,128,2048]{2,1,0:T(8,128)(2,1)} %hist.3, f32[4,2048]{1,0:T(4,128)S(1)} %copy-done.24, ...), custom_call_target="tpu_custom_call" | custom-call | tf_op jit(solution)/shard_map/mix_forward/pallas_call | solution.py:103
  23.8 34.5 %all-gather.7.cloned.1.call-done.cot = bf16[512,2048]{1,0:T(8,128)(2,1)} async-done(((bf16[128,2048]{1,0:T(8,128)(2,1)}), bf16[512,2048]{1,0:T(8,128)(2,1)}) %all-gather.7.cloned.1.call-update) | async-done | bytes 2097168 | tf_op jit(solution)/shard_map/all_gather | solution.py:615
  58.3 46.8 %all-gather.5.cloned.1.call-done.n3 = bf16[512,2048]{1,0:T(8,128)(2,1)} async-done(((bf16[128,2048]{1,0:T(8,128)(2,1)}), bf16[512,2048]{1,0:T(8,128)(2,1)}) %all-gather.5.cloned.1.call-update) | async-done | bytes 2097168 | tf_op jit(solution)/shard_map/all_gather | solution.py:615
  105.1 38.4 %feed_forward.1 = (f32[512,2048]{1,0:T(8,128)}, bf16[512,2048]{1,0:T(8,128)(2,1)}, bf16[2048,2048]{1,0:T(8,128)(2,1)}, bf16[2048,2048]{1,0:T(8,128)(2,1)}) custom-call(bf16[512,2048]{1,0:T(8,128)(2,1)} %all-gather.5.cloned.1.call-done.n3, bf16[512,2048]{1,0:T(8,128)(2,1)} %all-gather.7.cloned.1.call-done.cot, bf16[2048,2048]{1,0:T(8,128)(2,1)} %w_up.1, ...), custom_call_target="tpu_custom_call" | custom-call | flops 25769803776 | bytes 33554432 | tf_op jit(solution)/shard_map/feed_forward/pallas_call | solution.py:275
  148.2 38.6 %all-gather.11.cloned.1.call-done.n = bf16[512,4096]{1,0:T(8,128)(2,1)} async-done(((bf16[128,4096]{1,0:T(8,128)(2,1)}), bf16[512,4096]{1,0:T(8,128)(2,1)}) %all-gather.11.cloned.1.call-update) | async-done | bytes 4194320 | tf_op jit(solution)/shard_map/all_gather | solution.py:615
  191.8 4.2 project_kv.1
  199.0 10.7 %collective-permute-done = bf16[512,512]{1,0:T(8,128)(2,1)S(1)} collective-permute-done((bf16[512,512]{1,0:T(8,128)(2,1)S(1)}, bf16[512,512]{1,0:T(8,128)(2,1)S(1)}, u32[]{:S(2)}, u32[]{:S(2)}) %collective-permute-start) | collective-permute-done | bytes 524320 | tf_op jit(solution)/shard_map/ppermute | solution.py:532
  216.9 18.3 %collective-permute-done.1 = bf16[1024,512]{1,0:T(8,128)(2,1)} collective-permute-done((bf16[1024,512]{1,0:T(8,128)(2,1)}, bf16[1024,512]{1,0:T(8,128)(2,1)}, u32[]{:S(2)}, u32[]{:S(2)}) %collective-permute-start.1) | collective-permute-done | bytes 1048608 | tf_op jit(solution)/shard_map/ppermute | solution.py:532
  235.2 3.0 pad_maximum_fusion.1
  259.5 6.8 attend.1
  267.4 12.0 %attend_back.1 = (bf16[512,512]{1,0:T(8,128)(2,1)S(1)}, bf16[4096,512]{1,0:T(8,128)(2,1)S(1)}, bf16[4096,512]{1,0:T(8,128)(2,1)S(1)}) custom-call(s32[2]{0:T(128)S(1)} %copy-done.31, s32[8]{0:T(128)S(1)} %copy-done.30, s32[8]{0:T(128)S(1)} %copy-done.29, bf16[512,512]{1,0:T(8,128)(2,1)S(1)} %copy-done.23, ...), custom_call_target="tpu_custom_call" | custom-call | flops 21474836480 | bytes 20971520 | tf_op jit(solution)/shard_map/attend_back/pallas_call | solution.py:514
  281.0 6.8 collective-permute-start.6
  294.3 3.0 add_convert_fusion.1
  297.4 26.5 %collective-permute-start.7 = (bf16[1024,512]{1,0:T(8,128)(2,1)S(1)}, bf16[1024,512]{1,0:T(8,128)(2,1)S(1)}, u32[]{:S(2)}, u32[]{:S(2)}) collective-permute-start(bf16[1024,512]{1,0:T(8,128)(2,1)S(1)} %slice.102), channel_id=1, source_target_pairs={{0,16},{4,20},{8,24},{12,28},{16,0},{20,4},{24,8},{28,12},{1,17},{... | collective-permute-start | bytes 3145736 | tf_op jit(solution)/shard_map/ppermute | solution.py:532
  326.4 17.0 %collective-permute-start.10 = (bf16[1024,512]{1,0:T(8,128)(2,1)S(1)}, bf16[1024,512]{1,0:T(8,128)(2,1)S(1)}, u32[]{:S(2)}, u32[]{:S(2)}) collective-permute-start(bf16[1024,512]{1,0:T(8,128)(2,1)S(1)} %slice.109), channel_id=1, source_target_pairs={{0,8},{4,12},{8,0},{12,4},{16,24},{20,28},{24,16},{28,20},{1,9},{5... | collective-permute-start | bytes 3145736 | tf_op jit(solution)/shard_map/ppermute | solution.py:532
  343.5 22.0 %collective-permute-done.7 = bf16[1024,512]{1,0:T(8,128)(2,1)S(1)} collective-permute-done((bf16[1024,512]{1,0:T(8,128)(2,1)S(1)}, bf16[1024,512]{1,0:T(8,128)(2,1)S(1)}, u32[]{:S(2)}, u32[]{:S(2)}) %collective-permute-start.7) | collective-permute-done | bytes 1048608 | tf_op jit(solution)/shard_map/ppermute | solution.py:532
  369.9 18.9 %collective-permute-done.8 = bf16[512,512]{1,0:T(8,128)(2,1)S(1)} collective-permute-done((bf16[512,512]{1,0:T(8,128)(2,1)S(1)}, bf16[512,512]{1,0:T(8,128)(2,1)S(1)}, u32[]{:S(2)}, u32[]{:S(2)}) %collective-permute-start.8) | collective-permute-done | bytes 524320 | tf_op jit(solution)/shard_map/ppermute | solution.py:532
  403.5 4.8 add_convert_fusion.2
  408.6 4.5 convolution_convert_fusion.3
  416.5 2.7 convolution_convert_fusion.2
  419.2 3.7 convolution_convert_fusion.1
  422.9 59.9 %all-reduce.8.cloned.1.call-done = (bf16[2048,2048]{1,0:T(8,128)(2,1)}, bf16[2048,2048]{1,0:T(8,128)(2,1)}) async-done(((bf16[2048,2048]{1,0:T(8,128)(2,1)}, bf16[2048,2048]{1,0:T(8,128)(2,1)}), (bf16[2048,2048]{1,0:T(8,128)(2,1)}, bf16[2048,2048]{1,0:T(8,128)(2,1)})) %all-reduce.8.cloned.1.call-update) | async-done | bytes 16777232 | tf_op jit(solution)/shard_map/psum | solution.py:672
  482.8 46.7 %reduce-scatter.7.cloned.1.call-done.gn3 = bf16[128,2048]{1,0:T(8,128)(2,1)} async-done(((bf16[512,2048]{1,0:T(8,128)(2,1)}), bf16[128,2048]{1,0:T(8,128)(2,1)}) %reduce-scatter.7.cloned.1.call-update) | async-done | bytes 524304 | tf_op jit(solution)/shard_map/reduce_scatter | solution.py:618
  529.5 45.5 %reduce-scatter.11.cloned.1.call-done.gnq = bf16[128,2048]{1,0:T(8,128)(2,1)} async-done(((bf16[512,2048]{1,0:T(8,128)(2,1)}), bf16[128,2048]{1,0:T(8,128)(2,1)}) %reduce-scatter.11.cloned.1.call-update) | async-done | bytes 524304 | tf_op jit(solution)/shard_map/reduce_scatter | solution.py:618
  575.0 79.1 %reduce-scatter.9.cloned.1.call-done.gnkv = bf16[128,4096]{1,0:T(8,128)(2,1)} async-done(((bf16[512,4096]{1,0:T(8,128)(2,1)}), bf16[128,4096]{1,0:T(8,128)(2,1)}) %reduce-scatter.9.cloned.1.call-update) | async-done | bytes 1048592 | tf_op jit(solution)/shard_map/reduce_scatter | solution.py:618
  657.4 15.3 %unmix.1 = (bf16[9,128,2048]{2,1,0:T(8,128)(2,1)}, f32[48,2176]{1,0:T(8,128)S(1)}) custom-call(bf16[9,128,2048]{2,1,0:T(8,128)(2,1)} %hist.3, f32[4,128,2048]{2,1,0:T(8,128)} %get-tuple-element.38.streams, bf16[128,2048]{1,0:T(8,128)(2,1)S(1)} %copy-done.20, bf16[128,4096]{1,0:T(8,128)(2,1)S(1)} %copy-done.18, bf16[128,2048]{1,0:T(8,128)(2,1)S(1)} %copy-done.21, ...), custom_call_target="tpu_custom_call" | custom-call | tf_op jit(solution)/shard_map/unmix/pallas_call | solution.py:205
  675.9 5.7 collective-permute-done.13
  683.2 5.0 collective-permute-done.14
  689.8 11.7 %convert_element_type.204 = f32[2048,2048]{1,0:T(8,128)} convert(bf16[2048,2048]{1,0:T(8,128)(2,1)} %get-tuple-element.61) | non-fusion elementwise | flops 4194304 | bytes 25165824 | tf_op jit(solution)/shard_map/convert_element_type | solution.py:688
  701.5 11.7 %convert_element_type.205 = f32[2048,2048]{1,0:T(8,128)} convert(bf16[2048,2048]{1,0:T(8,128)(2,1)} %get-tuple-element.62) | non-fusion elementwise | flops 4194304 | bytes 25165824 | tf_op jit(solution)/shard_map/convert_element_type | solution.py:689
  717.6 119.9 %all-reduce.6.cloned.1.call-done = (bf16[2048,512]{1,0:T(8,128)(2,1)}, bf16[2048,512]{1,0:T(8,128)(2,1)}, bf16[2048,512]{1,0:T(8,128)(2,1)}, bf16[512,2048]{1,0:T(8,128)(2,1)}) async-done(((bf16[2048,512]{1,0:T(8,128)(2,1)}, bf16[2048,512]{1,0:T(8,128)(2,1)}, bf16[2048,512]{1,0:T(8,128)(2,1)}, bf16[512,2048]{1,0:T(8,128)(2,1)}), (bf16[2048,512]{1,0:T(8,128)(2,1)}, bf16[2048,512]{1,0:T(8,128)(2,1)}, ...) | async-done | bytes 8388624 | tf_op jit(solution)/shard_map/psum | solution.py:674
  837.5 4.3 convert_element_type.200
  (231 shorter events, 106.1 us)
Async XLA Ops:
  7.2 243.4 %copy-start = (bf16[512,2048]{1,0:T(8,128)(2,1)S(1)}, bf16[512,2048]{1,0:T(8,128)(2,1)}, u32[]{:S(2)}) copy-start(bf16[512,2048]{1,0:T(8,128)(2,1)} %param.26) | copy-start | bytes 6291460
  7.2 51.1 %all-gather.7.cloned.1.call-start = ((), (), s32[]{:S(2)}) async-start(), calls=%async_computation.5 | async-start | bytes 2621440 | tf_op jit(solution)/shard_map/all_gather | solution.py:615
  7.9 97.2 %all-gather.5.cloned.1.call-start = ((), (), s32[]{:S(2)}) async-start(), calls=%async_computation.4 | async-start | bytes 2621440 | tf_op jit(solution)/shard_map/all_gather | solution.py:615
  22.4 164.4 %all-gather.11.cloned.1.call-start = ((), (), s32[]{:S(2)}) async-start(), calls=%async_computation.7 | async-start | bytes 5242880 | tf_op jit(solution)/shard_map/all_gather | solution.py:615
  23.1 220.3 %all-gather.9.cloned.1.call-start = ((), (), s32[]{:S(2)}) async-start(), calls=%async_computation.6 | async-start | bytes 2621440 | tf_op jit(solution)/shard_map/all_gather | solution.py:615
  23.7 459.1 %all-reduce.8.cloned.1.call-start = ((), (), s32[]{:S(2)}) async-start(), calls=%async_computation.13 | async-start | bytes 33554432 | tf_op jit(solution)/shard_map/psum | solution.py:672
  143.5 386.0 %reduce-scatter.7.cloned.1.call-start = ((), (), s32[]{:S(2)}) async-start(), calls=%async_computation.9 | async-start | bytes 2621440 | tf_op jit(solution)/shard_map/reduce_scatter | solution.py:618
  196.0 13.7 %collective-permute-start = (bf16[512,512]{1,0:T(8,128)(2,1)S(1)}, bf16[512,512]{1,0:T(8,128)(2,1)S(1)}, u32[]{:S(2)}, u32[]{:S(2)}) collective-permute-start(bf16[512,512]{1,0:T(8,128)(2,1)S(1)} %get-tuple-element.43), channel_id=1, source_target_pairs={{0,8},{4,12},{8,0},{12,4},{16,24},{20,28},{24,16},{28,20},{1,9},{5... | collective-permute-start | bytes 1572872 | tf_op jit(solution)/shard_map/ppermute | solution.py:532
  197.6 14.8 %collective-permute-start.3 = (bf16[512,512]{1,0:T(8,128)(2,1)S(1)}, bf16[512,512]{1,0:T(8,128)(2,1)S(1)}, u32[]{:S(2)}, u32[]{:S(2)}) collective-permute-start(bf16[512,512]{1,0:T(8,128)(2,1)S(1)} %get-tuple-element.44), channel_id=1, source_target_pairs={{0,16},{4,20},{8,24},{12,28},{16,0},{20,4},{24,8},{28,12},{1,17},{... | collective-permute-start | bytes 1572872 | tf_op jit(solution)/shard_map/ppermute | solution.py:532
  210.8 24.4 %collective-permute-start.1 = (bf16[1024,512]{1,0:T(8,128)(2,1)}, bf16[1024,512]{1,0:T(8,128)(2,1)}, u32[]{:S(2)}, u32[]{:S(2)}) collective-permute-start(bf16[1024,512]{1,0:T(8,128)(2,1)} %pad_maximum_fusion.3), channel_id=1, source_target_pairs={{0,16},{4,20},{8,24},{12,28},{16,0},{20,4},{24,8},{28,12},{1,17},{... | collective-permute-start | bytes 3145736 | tf_op jit(solution)/shard_map/ppermute | solution.py:532
  213.5 24.7 %collective-permute-start.4 = (bf16[1024,512]{1,0:T(8,128)(2,1)}, bf16[1024,512]{1,0:T(8,128)(2,1)}, u32[]{:S(2)}, u32[]{:S(2)}) collective-permute-start(bf16[1024,512]{1,0:T(8,128)(2,1)} %pad_maximum_fusion.4), channel_id=1, source_target_pairs={{0,8},{4,12},{8,0},{12,4},{16,24},{20,28},{24,16},{28,20},{1,9},{5... | collective-permute-start | bytes 3145736 | tf_op jit(solution)/shard_map/ppermute | solution.py:532
  238.2 17.6 %collective-permute-start.2 = (bf16[2048,512]{1,0:T(8,128)(2,1)}, bf16[2048,512]{1,0:T(8,128)(2,1)}, u32[]{:S(2)}, u32[]{:S(2)}) collective-permute-start(bf16[2048,512]{1,0:T(8,128)(2,1)} %pad_maximum_fusion.1), channel_id=1, source_target_pairs={{0,4},{4,0},{8,12},{12,8},{16,20},{20,16},{24,28},{28,24},{1,5},{5... | collective-permute-start | bytes 6291464 | tf_op jit(solution)/shard_map/ppermute | solution.py:532
  240.9 16.8 %collective-permute-start.5 = (bf16[2048,512]{1,0:T(8,128)(2,1)}, bf16[2048,512]{1,0:T(8,128)(2,1)}, u32[]{:S(2)}, u32[]{:S(2)}) collective-permute-start(bf16[2048,512]{1,0:T(8,128)(2,1)} %pad_maximum_fusion.2), channel_id=1, source_target_pairs={{0,4},{4,0},{8,12},{12,8},{16,20},{20,16},{24,28},{28,24},{1,5},{5... | collective-permute-start | bytes 6291464 | tf_op jit(solution)/shard_map/ppermute | solution.py:532
  243.4 331.7 %reduce-scatter.11.cloned.1.call-start = ((), (), s32[]{:S(2)}) async-start(), calls=%async_computation.11 | async-start | bytes 2621440 | tf_op jit(solution)/shard_map/reduce_scatter | solution.py:618
  281.0 13.3 %collective-permute-start.6 = (bf16[2048,512]{1,0:T(8,128)(2,1)}, bf16[2048,512]{1,0:T(8,128)(2,1)}, u32[]{:S(2)}, u32[]{:S(2)}) collective-permute-start(bf16[2048,512]{1,0:T(8,128)(2,1)} %slice.77), channel_id=1, source_target_pairs={{0,4},{4,0},{8,12},{12,8},{16,20},{20,16},{24,28},{28,24},{1,5},{5... | collective-permute-start | bytes 6291464 | tf_op jit(solution)/shard_map/ppermute | solution.py:532
  289.3 34.6 %collective-permute-start.9 = (bf16[2048,512]{1,0:T(8,128)(2,1)}, bf16[2048,512]{1,0:T(8,128)(2,1)}, u32[]{:S(2)}, u32[]{:S(2)}) collective-permute-start(bf16[2048,512]{1,0:T(8,128)(2,1)} %slice.86), channel_id=1, source_target_pairs={{0,4},{4,0},{8,12},{12,8},{16,20},{20,16},{24,28},{28,24},{1,5},{5... | collective-permute-start | bytes 6291464 | tf_op jit(solution)/shard_map/ppermute | solution.py:532
  294.0 360.1 %reduce-scatter.9.cloned.1.call-start = ((), (), s32[]{:S(2)}) async-start(), calls=%async_computation.10 | async-start | bytes 5242880 | tf_op jit(solution)/shard_map/reduce_scatter | solution.py:618
  294.3 29.6 %copy-start.4 = (bf16[4096,512]{1,0:T(8,128)(2,1)S(1)}, bf16[4096,512]{1,0:T(8,128)(2,1)}, u32[]{:S(2)}) copy-start(bf16[4096,512]{1,0:T(8,128)(2,1)} %copy-done.3) | copy-start | bytes 12582916
  297.4 68.1 %collective-permute-start.7 = (bf16[1024,512]{1,0:T(8,128)(2,1)S(1)}, bf16[1024,512]{1,0:T(8,128)(2,1)S(1)}, u32[]{:S(2)}, u32[]{:S(2)}) collective-permute-start(bf16[1024,512]{1,0:T(8,128)(2,1)S(1)} %slice.102), channel_id=1, source_target_pairs={{0,16},{4,20},{8,24},{12,28},{16,0},{20,4},{24,8},{28,12},{1,17},{... | collective-permute-start | bytes 3145736 | tf_op jit(solution)/shard_map/ppermute | solution.py:532
  326.4 40.9 %collective-permute-start.10 = (bf16[1024,512]{1,0:T(8,128)(2,1)S(1)}, bf16[1024,512]{1,0:T(8,128)(2,1)S(1)}, u32[]{:S(2)}, u32[]{:S(2)}) collective-permute-start(bf16[1024,512]{1,0:T(8,128)(2,1)S(1)} %slice.109), channel_id=1, source_target_pairs={{0,8},{4,12},{8,0},{12,4},{16,24},{20,28},{24,16},{28,20},{1,9},{5... | collective-permute-start | bytes 3145736 | tf_op jit(solution)/shard_map/ppermute | solution.py:532
  365.8 23.0 %collective-permute-start.8 = (bf16[512,512]{1,0:T(8,128)(2,1)S(1)}, bf16[512,512]{1,0:T(8,128)(2,1)S(1)}, u32[]{:S(2)}, u32[]{:S(2)}) collective-permute-start(bf16[512,512]{1,0:T(8,128)(2,1)S(1)} %slice.104), channel_id=1, source_target_pairs={{0,8},{4,12},{8,0},{12,4},{16,24},{20,28},{24,16},{28,20},{1,9},{5... | collective-permute-start | bytes 1572872 | tf_op jit(solution)/shard_map/ppermute | solution.py:532
  369.5 28.5 %collective-permute-start.11 = (bf16[512,512]{1,0:T(8,128)(2,1)}, bf16[512,512]{1,0:T(8,128)(2,1)}, u32[]{:S(2)}, u32[]{:S(2)}) collective-permute-start(bf16[512,512]{1,0:T(8,128)(2,1)} %slice.111), channel_id=1, source_target_pairs={{0,16},{4,20},{8,24},{12,28},{16,0},{20,4},{24,8},{28,12},{1,17},{... | collective-permute-start | bytes 1572872 | tf_op jit(solution)/shard_map/ppermute | solution.py:532
  403.5 311.5 %reduce-scatter.5.cloned.1.call-start = ((), (), s32[]{:S(2)}) async-start(), calls=%async_computation.8 | async-start | bytes 2621440 | tf_op jit(solution)/shard_map/reduce_scatter | solution.py:618
  408.3 429.2 %all-reduce.6.cloned.1.call-start = ((), (), s32[]{:S(2)}) async-start(), calls=%async_computation.12 | async-start | bytes 16777216 | tf_op jit(solution)/shard_map/psum | solution.py:674
  482.8 171.3 %copy-start.10 = (bf16[128,2048]{1,0:T(8,128)(2,1)S(1)}, bf16[128,2048]{1,0:T(8,128)(2,1)}, u32[]{:S(2)}) copy-start(bf16[128,2048]{1,0:T(8,128)(2,1)} %cot.1) | copy-start | bytes 1572868
  482.8 171.3 %copy-start.25 = (f32[4,2048]{1,0:T(4,128)S(1)}, f32[4,2048]{1,0:T(4,128)}, u32[]{:S(2)}) copy-start(f32[4,2048]{1,0:T(4,128)} %gains.3) | copy-start | bytes 98308
  482.8 171.3 %copy-start.27 = (bf16[40,36]{1,0:T(8,128)(2,1)S(1)}, bf16[40,36]{1,0:T(8,128)(2,1)}, u32[]{:S(2)}) copy-start(bf16[40,36]{1,0:T(8,128)(2,1)} %mix_out.3) | copy-start | bytes 8644
  672.8 1.5 collective-permute-start.12
  674.3 7.3 collective-permute-start.13
  681.7 6.5 collective-permute-start.14
  688.3 24.9 %collective-permute-start.15 = (bf16[48,2176]{1,0:T(8,128)(2,1)S(1)}, bf16[48,2176]{1,0:T(8,128)(2,1)S(1)}, u32[]{:S(2)}, u32[]{:S(2)}) collective-permute-start(bf16[48,2176]{1,0:T(8,128)(2,1)S(1)} %add_convert_fusion.9), channel_id=1, source_target_pairs={{0,1},{1,0},{2,3},{3,2},{4,5},{5,4},{6,7},{7,6},{8,9},{9,8},{10,11... | collective-permute-start | bytes 626696 | tf_op jit(solution)/shard_map/ppermute | solution.py:532
  713.3 136.4 %collective-permute-start.16 = (bf16[48,2176]{1,0:T(8,128)(2,1)S(1)}, bf16[48,2176]{1,0:T(8,128)(2,1)S(1)}, u32[]{:S(2)}, u32[]{:S(2)}) collective-permute-start(bf16[48,2176]{1,0:T(8,128)(2,1)S(1)} %add_convert_fusion.8), channel_id=1, source_target_pairs={{0,2},{1,3},{2,0},{3,1},{4,6},{5,7},{6,4},{7,5},{8,10},{9,11},{10,... | collective-permute-start | bytes 626696 | tf_op jit(solution)/shard_map/ppermute | solution.py:532
  (53 other events, 222.4 us)
Sparse Core Ops, SparseCore 0:
  9.6 48.6 all-gather.6
  60.4 44.6 all-gather.4
  107.2 79.4 all-gather.10
  188.2 44.4 all-gather.8
  237.1 245.6 all-reduce.7
  485.6 43.8 reduce-scatter.6
  531.8 43.1 reduce-scatter.10
  578.0 76.0 reduce-scatter.8
  657.0 48.7 reduce-scatter.4
  710.6 126.8 all-reduce.5

commit v2 on v1

--- a/solution.py
+++ b/solution.py
@@ -22,6 +22,7 @@
 sqrt_half = 0.7071067811865476
 inv_sqrt_2pi = 0.3989422804014327
 log2e = 1.4426950408889634
+small_cost = pl.CostEstimate(flops=MIB, bytes_accessed=MIB, transcendentals=0)
 
 
 def vmem():
@@ -238,9 +239,41 @@
     )(histories, streams, gn3, gnkv, gnq, cotangent, coef, mix_pre, norm_gains, mix_in, mix_out)
 
 
-def ff_kernel(n3, cot, w_up, w_down, ff_out, gn3, gw_up, gw_down, out_acc, gn_acc):
+def ff_kernel(count, rank_ref, *refs):
+    pieces = 2 * count - 1
+    sources = (refs[:pieces], refs[pieces : 2 * pieces])
+    w_up, w_down, ff_out, gn3, gw_up, gw_down, cot, n3, gn_acc, sems = refs[2 * pieces :]
     step = pl.program_id(0)
     last = pl.num_programs(0) - 1
+
+    @pl.when(step == 0)
+    def _():
+        rank = rank_ref[0]
+
+        def each(act):
+            for which, target in ((0, n3), (1, cot)):
+                rows = target.shape[0] // count
+                for at in range(pieces):
+                    if at == 0:
+                        block, there = rank, None
+                    elif at < count:
+                        block, there = rank - at, rank >= at
+                    else:
+                        k = at - count + 1
+                        block, there = rank + k, rank + k < count
+
+                    def one(block=block, at=at):
+                        to = target.at[pl.ds(pl.multiple_of(block * rows, rows), rows), :]
+                        act(pltpu.make_async_copy(sources[which][at], to, sems.at[which, at]))
+
+                    if there is None:
+                        one()
+                    else:
+                        pl.when(there)(one)
+
+        each(lambda copy: copy.start())
+        each(lambda copy: copy.wait())
+
     pre = dot(n3[...], w_up[...])
     phi = cdf(pre)
     act = (pre * phi).astype(bf16)
@@ -253,53 +286,62 @@
 
     @pl.when(step == 0)
     def _():
-        out_acc[...] = part_out
+        ff_out[...] = part_out
         gn_acc[...] = part_gn
 
     @pl.when(step > 0)
     def _():
-        out_acc[...] += part_out
+        ff_out[...] += part_out
         gn_acc[...] += part_gn
 
     @pl.when(step == last)
     def _():
-        ff_out[...] = out_acc[...]
         gn3[...] = gn_acc[...].astype(bf16)
 
 
-def feed_forward(n3, cot, w_up, w_down):
-    rows, width = n3.shape
+def feed_forward(rank, n3_pieces, cot_pieces, w_up, w_down):
+    count = (len(n3_pieces) + 1) // 2
+    rows, width = n3_pieces[0].shape
+    rows = rows * count
     hidden = w_up.shape[1]
     block = min(512, hidden)
-    fixed = pl.BlockSpec((rows, width), lambda i: (0, 0))
+    fixed = pl.BlockSpec((rows, width), lambda i, r: (0, 0))
+    anywhere = pl.BlockSpec(memory_space=pl.ANY)
+    grid_spec = pltpu.PrefetchScalarGridSpec(
+        num_scalar_prefetch=1,
+        grid=(hidden // block,),
+        in_specs=[anywhere] * (2 * len(n3_pieces))
+        + [
+            pl.BlockSpec((width, block), lambda i, r: (0, i)),
+            pl.BlockSpec((block, width), lambda i, r: (i, 0)),
+        ],
+        out_specs=[
+            fixed,
+            fixed,
+            pl.BlockSpec((width, block), lambda i, r: (0, i)),
+            pl.BlockSpec((block, width), lambda i, r: (i, 0)),
+            fixed,
+        ],
+        scratch_shapes=[
+            pltpu.VMEM((rows, width), bf16),
+            pltpu.VMEM((rows, width), f32),
+            pltpu.SemaphoreType.DMA((2, len(n3_pieces))),
+        ],
+    )
     return pl.pallas_call(
-        ff_kernel,
-        grid=(hidden // block,),
+        functools.partial(ff_kernel, count),
+        grid_spec=grid_spec,
         out_shape=(
             jax.ShapeDtypeStruct((rows, width), f32),
             jax.ShapeDtypeStruct((rows, width), bf16),
             jax.ShapeDtypeStruct((width, hidden), bf16),
             jax.ShapeDtypeStruct((hidden, width), bf16),
+            jax.ShapeDtypeStruct((rows, width), bf16),
         ),
-        in_specs=[
-            fixed,
-            fixed,
-            pl.BlockSpec((width, block), lambda i: (0, i)),
-            pl.BlockSpec((block, width), lambda i: (i, 0)),
-        ],
-        out_specs=[
-            fixed,
-            fixed,
-            pl.BlockSpec((width, block), lambda i: (0, i)),
-            pl.BlockSpec((block, width), lambda i: (i, 0)),
-        ],
-        scratch_shapes=[pltpu.VMEM((rows, width), f32), pltpu.VMEM((rows, width), f32)],
         compiler_params=params(60),
-        cost_estimate=pl.CostEstimate(
-            flops=12 * rows * width * hidden, bytes_accessed=8 * width * hidden, transcendentals=0
-        ),
+        cost_estimate=small_cost,
         name="feed_forward",
-    )(n3, cot, w_up, w_down)
+    )(rank, *n3_pieces, *cot_pieces, w_up, w_down)
 
 
 def turn(x, same, down, up):
@@ -337,9 +379,7 @@
         + [spec(HD)] * 3,
         out_specs=tuple(spec(local) for _ in range(outs)),
         compiler_params=params(48),
-        cost_estimate=pl.CostEstimate(
-            flops=2 * rows * width * local * outs, bytes_accessed=8 * MIB, transcendentals=0
-        ),
+        cost_estimate=small_cost,
         name=name,
     )(n, *weights, *tables)
 
@@ -357,179 +397,354 @@
     return (same, down, up)
 
 
-def masked(scores, kb, block, first, last_seen):
-    place = lax.broadcasted_iota(jnp.int32, scores.shape, 0) + kb * block
-    seen = (place >= first) & (place <= last_seen)
-    return jnp.where(seen, scores, hidden_mask)
-
-
-def attend_kernel(scale2, info, kslot, vslot, q, k, v, span, out, lse, peak, total, acc):
-    kb = pl.program_id(1)
+def hide(kb, block, span, bias):
+    place = lax.broadcasted_iota(jnp.int32, bias.shape, 0) + kb * block
+    seen = (place >= span[0:1, :]) & (place <= span[1:2, :])
+    bias[...] = jnp.where(seen, 0.0, hidden_mask)
+
+
+def take(step, sources, target):
+    for i, source in enumerate(sources):
+
+        @pl.when(step == i)
+        def _(source=source):
+            target[...] = source[...]
+
+
+def attend_kernel(scale2, heads, blocks, info, offsets, q, span, *refs):
+    keys, values = refs[:blocks], refs[blocks : 2 * blocks]
+    out, lse, peak, total, acc, bias, k, v = refs[2 * blocks :]
+    step = pl.program_id(0)
     rank, reach = info[0], info[1]
+    kb = offsets[step]
     block = k.shape[0]
 
-    @pl.when(kb == 0)
+    @pl.when(step == 0)
     def _():
         peak[...] = jnp.full_like(peak, hidden_mask)
         total[...] = jnp.zeros_like(total)
         acc[...] = jnp.zeros_like(acc)
 
-    def update(scores):
-        old = peak[...]
-        new = jnp.maximum(old, jnp.max(scores, axis=0, keepdims=True))
-        weights = jnp.exp2(scores - new)
-        factor = jnp.exp2(old - new)
-        peak[...] = new
-        total[...] = total[...] * factor + jnp.sum(weights, axis=0, keepdims=True)
-        acc[...] = acc[...] * factor + dot_tn(v[...], weights.astype(bf16))
+    def update(extra):
+        for h in range(heads):
+            lanes = slice(h * HD, (h + 1) * HD)
+            one = slice(h, h + 1)
+            scores = dot_nt(k[:, lanes], q[:, lanes]) * scale2
+            if extra is not None:
+                scores = scores + extra[...]
+            old = peak[one, :]
+            new = jnp.maximum(old, jnp.max(scores, axis=0, keepdims=True))
+            weights = jnp.exp2(scores - new)
+            factor = jnp.exp2(old - new)
+            peak[one, :] = new
+            total[one, :] = total[one, :] * factor + jnp.sum(weights, axis=0, keepdims=True)
+            acc[lanes, :] = acc[lanes, :] * factor + dot_tn(v[:, lanes], weights.astype(bf16))
 
     needs = (kb == rank) | (reach > kb * block)
 
+    @pl.when(kb <= rank)
+    def _():
+        take(step, keys, k)
+        take(step, values, v)
+
     @pl.when((kb <= rank) & jnp.logical_not(needs))
     def _():
-        update(dot_nt(k[...], q[...]) * scale2)
+        update(None)
 
     @pl.when((kb <= rank) & needs)
     def _():
-        scores = dot_nt(k[...], q[...]) * scale2
-        update(masked(scores, kb, block, span[0:1, :], span[1:2, :]))
-
-    @pl.when(kb == pl.num_programs(1) - 1)
-    def _():
-        out[...] = jnp.transpose(acc[...] / total[...]).astype(bf16)
-        lse[...] = (peak[...] + jnp.log2(total[...]))[None]
-
-
-def attend(q, k_all, v_all, info, kslot, vslot, span, blocks):
+        hide(kb, block, span, bias)
+        update(bias)
+
+    @pl.when(step == pl.num_programs(0) - 1)
+    def _():
+        for h in range(heads):
+            lanes = slice(h * HD, (h + 1) * HD)
+            one = slice(h, h + 1)
+            out[:, lanes] = jnp.transpose(acc[lanes, :] / total[one, :]).astype(bf16)
+            lse[one, :] = peak[one, :] + jnp.log2(total[one, :])
+
+
+def attend(q, keys, values, info, offsets, span):
     rows, local = q.shape
     heads = local // HD
-    block = k_all.shape[0] // blocks
+    block = keys[0].shape[0]
+    blocks = len(keys)
     scale2 = HD ** (-0.5) * log2e
+    fixed = lambda shape: pl.BlockSpec(shape, lambda b, info, at: (0, 0))
     grid_spec = pltpu.PrefetchScalarGridSpec(
-        num_scalar_prefetch=3,
-        grid=(heads, blocks),
-        in_specs=[
-            pl.BlockSpec((rows, HD), lambda h, b, info, ks, vs: (0, h)),
-            pl.BlockSpec((block, HD), lambda h, b, info, ks, vs: (ks[jnp.minimum(b, info[0])], h)),
-            pl.BlockSpec((block, HD), lambda h, b, info, ks, vs: (vs[jnp.minimum(b, info[0])], h)),
-            pl.BlockSpec((8, rows), lambda h, b, info, ks, vs: (0, 0)),
+        num_scalar_prefetch=2,
+        grid=(blocks,),
+        in_specs=[fixed((rows, local)), fixed((8, rows))] + [fixed((block, local))] * (2 * blocks),
+        out_specs=[fixed((rows, local)), fixed((8, rows))],
+        scratch_shapes=[
+            pltpu.VMEM((8, rows), f32),
+            pltpu.VMEM((8, rows), f32),
+            pltpu.VMEM((local, rows), f32),
+            pltpu.VMEM((block, rows), f32),
+            pltpu.VMEM((block, local), bf16),
+            pltpu.VMEM((block, local), bf16),
         ],
-        out_specs=[
-            pl.BlockSpec((rows, HD), lambda h, b, info, ks, vs: (0, h)),
-            pl.BlockSpec((1, 1, rows), lambda h, b, info, ks, vs: (h, 0, 0)),
-        ],
-        scratch_shapes=[
-            pltpu.VMEM((1, rows), f32),
-            pltpu.VMEM((1, rows), f32),
-            pltpu.VMEM((HD, rows), f32),
-        ],
     )
     return pl.pallas_call(
-        functools.partial(attend_kernel, scale2),
+        functools.partial(attend_kernel, scale2, heads, blocks),
         grid_spec=grid_spec,
         out_shape=(
             jax.ShapeDtypeStruct((rows, local), bf16),
-            jax.ShapeDtypeStruct((heads, 1, rows), f32),
+            jax.ShapeDtypeStruct((8, rows), f32),
         ),
-        compiler_params=params(32),
-        cost_estimate=pl.CostEstimate(
-            flops=8 * rows * block * blocks * local, bytes_accessed=8 * MIB, transcendentals=0
-        ),
+        compiler_params=params(56),
+        cost_estimate=small_cost,
         name="attend",
-    )(info, kslot, vslot, q, k_all, v_all, span)
-
-
-def attend_back_kernel(
-    scale, scale2, info, kslot, vslot, q, k, v, do, o, lse, span, same, down, up, gq, gk, gv, delta, acc
-):
-    kb = pl.program_id(1)
+    )(info, offsets, q, span, *keys, *values)
+
+
+def attend_back_kernel(scale, scale2, heads, blocks, *refs):
+    info, offsets, _, _ = refs[:4]
+    q, do, o, lse, span, same, down, up = refs[4:12]
+    keys, values = refs[12 : 12 + blocks], refs[12 + blocks : 12 + 2 * blocks]
+    gq, gk_hi, gk_lo, gv_hi, gv_lo, delta, acc, bias, k, v = refs[12 + 2 * blocks :]
+    step = pl.program_id(0)
     rank, reach = info[0], info[1]
+    kb = offsets[step]
     block = k.shape[0]
 
-    @pl.when(kb == 0)
-    def _():
-        both = do[...].astype(f32) * o[...].astype(f32)
-        delta[...] = jnp.sum(jnp.transpose(both), axis=0, keepdims=True)
+    @pl.when(step == 0)
+    def _():
+        for h in range(heads):
+            lanes = slice(h * HD, (h + 1) * HD)
+            both = do[:, lanes].astype(f32) * o[:, lanes].astype(f32)
+            delta[h : h + 1, :] = jnp.sum(jnp.transpose(both), axis=0, keepdims=True)
         acc[...] = jnp.zeros_like(acc)
 
-    def update(scores):
-        weights = jnp.exp2(scores - lse[0])
-        gv[...] = dot(weights.astype(bf16), do[...]).astype(bf16)
-        grad_weights = dot_nt(v[...], do[...])
-        grad_scores = (weights * (grad_weights - delta[...])).astype(bf16)
-        gk[...] = (dot(grad_scores, q[...]) * scale).astype(bf16)
-        acc[...] += dot_tn(k[...], grad_scores)
+    def update(extra, gk, gv):
+        for h in range(heads):
+            lanes = slice(h * HD, (h + 1) * HD)
+            one = slice(h, h + 1)
+            scores = dot_nt(k[:, lanes], q[:, lanes]) * scale2
+            if extra is not None:
+                scores = scores + extra[...]
+            weights = jnp.exp2(scores - lse[one, :])
+            gv[:, lanes] = dot(weights.astype(bf16), do[:, lanes]).astype(bf16)
+            grad_weights = dot_nt(v[:, lanes], do[:, lanes])
+            grad_scores = (weights * (grad_weights - delta[one, :])).astype(bf16)
+            gk[:, lanes] = (dot(grad_scores, q[:, lanes]) * scale).astype(bf16)
+            acc[lanes, :] += dot_tn(k[:, lanes], grad_scores)
 
     needs = (kb == rank) | (reach > kb * block)
 
-    @pl.when((kb <= rank) & jnp.logical_not(needs))
-    def _():
-        update(dot_nt(k[...], q[...]) * scale2)
-
-    @pl.when((kb <= rank) & needs)
-    def _():
-        scores = dot_nt(k[...], q[...]) * scale2
-        update(masked(scores, kb, block, span[0:1, :], span[1:2, :]))
-
-    @pl.when(kb > rank)
-    def _():
-        gk[...] = jnp.zeros_like(gk)
-        gv[...] = jnp.zeros_like(gv)
-
-    @pl.when(kb == pl.num_programs(1) - 1)
-    def _():
-        x = jnp.transpose(acc[...]) * scale
-        gq[...] = turn(x, same[...], -down[...], -up[...]).astype(bf16)
-
-
-def attend_back(q, k_all, v_all, do, o, lse, info, kslot, vslot, span, tables, blocks):
+    @pl.when(kb <= rank)
+    def _():
+        take(step, keys, k)
+        take(step, values, v)
+
+    for high, gk, gv in ((True, gk_hi, gv_hi), (False, gk_lo, gv_lo)):
+        here = (step < blocks // 2) if high else (step >= blocks // 2)
+
+        @pl.when(here & (kb <= rank) & jnp.logical_not(needs))
+        def _(gk=gk, gv=gv):
+            update(None, gk, gv)
+
+        @pl.when(here & (kb <= rank) & needs)
+        def _(gk=gk, gv=gv):
+            hide(kb, block, span, bias)
+            update(bias, gk, gv)
+
+        @pl.when(here & (kb > rank))
+        def _(gk=gk, gv=gv):
+            gk[...] = jnp.zeros_like(gk)
+            gv[...] = jnp.zeros_like(gv)
+
+    @pl.when(step == pl.num_programs(0) - 1)
+    def _():
+        for h in range(heads):
+            lanes = slice(h * HD, (h + 1) * HD)
+            x = jnp.transpose(acc[lanes, :]) * scale
+            gq[:, lanes] = turn(x, same[...], -down[...], -up[...]).astype(bf16)
+
+
+def attend_back(q, keys, values, do, o, lse, info, offsets, key_at, value_at, span, tables):
     rows, local = q.shape
     heads = local // HD
-    block = k_all.shape[0] // blocks
+    block = keys[0].shape[0]
+    blocks = len(keys)
+    half = blocks // 2
     scale = HD ** (-0.5)
-    at_query = pl.BlockSpec((rows, HD), lambda h, b, info, ks, vs: (0, h))
-    table = pl.BlockSpec((rows, HD), lambda h, b, info, ks, vs: (0, 0))
+    fixed = lambda shape: pl.BlockSpec(shape, lambda b, info, at, ks, vs: (0, 0))
+    high = lambda pick: pl.BlockSpec(
+        (block, local), lambda b, info, at, ks, vs: ((ks, vs)[pick][jnp.minimum(b, half - 1)] - half, 0)
+    )
+    low = lambda pick: pl.BlockSpec(
+        (block, local), lambda b, info, at, ks, vs: ((ks, vs)[pick][jnp.maximum(b, half)], 0)
+    )
     grid_spec = pltpu.PrefetchScalarGridSpec(
-        num_scalar_prefetch=3,
-        grid=(heads, blocks),
-        in_specs=[
-            at_query,
-            pl.BlockSpec((block, HD), lambda h, b, info, ks, vs: (ks[jnp.minimum(b, info[0])], h)),
-            pl.BlockSpec((block, HD), lambda h, b, info, ks, vs: (vs[jnp.minimum(b, info[0])], h)),
-            at_query,
-            at_query,
-            pl.BlockSpec((1, 1, rows), lambda h, b, info, ks, vs: (h, 0, 0)),
-            pl.BlockSpec((8, rows), lambda h, b, info, ks, vs: (0, 0)),
-            table,
-            table,
-            table,
+        num_scalar_prefetch=4,
+        grid=(blocks,),
+        in_specs=[fixed((rows, local))] * 3
+        + [fixed((8, rows))] * 2
+        + [fixed((rows, HD))] * 3
+        + [fixed((block, local))] * (2 * blocks),
+        out_specs=[fixed((rows, local)), high(0), low(0), high(1), low(1)],
+        scratch_shapes=[
+            pltpu.VMEM((8, rows), f32),
+            pltpu.VMEM((local, rows), f32),
+            pltpu.VMEM((block, rows), f32),
+            pltpu.VMEM((block, local), bf16),
+            pltpu.VMEM((block, local), bf16),
         ],
-        out_specs=[
-            at_query,
-            pl.BlockSpec((block, HD), lambda h, b, info, ks, vs: (ks[b], h)),
-            pl.BlockSpec((block, HD), lambda h, b, info, ks, vs: (vs[b], h)),
-        ],
-        scratch_shapes=[pltpu.VMEM((1, rows), f32), pltpu.VMEM((HD, rows), f32)],
-    )
+    )
+    part = jax.ShapeDtypeStruct((half * block, local), bf16)
     return pl.pallas_call(
-        functools.partial(attend_back_kernel, scale, scale * log2e),
+        functools.partial(attend_back_kernel, scale, scale * log2e, heads, blocks),
         grid_spec=grid_spec,
+        out_shape=(jax.ShapeDtypeStruct((rows, local), bf16), part, part, part, part),
+        compiler_params=params(60),
+        cost_estimate=small_cost,
+        name="attend_back",
+    )(info, offsets, key_at, value_at, q, do, o, lse, span, *tables, *keys, *values)
+
+
+def key_value_back_kernel(terms, *refs):
+    gk_parts, gv_parts = refs[:terms], refs[terms : 2 * terms]
+    wk, wv, same, down, up, gk, gv, gn = refs[2 * terms :]
+    width = wk.shape[0]
+    add = lambda parts: functools.reduce(lambda a, b: a + b, [p[...].astype(f32) for p in parts])
+    gk[...] = rotated(add(gk_parts), same[...], -down[...], -up[...])
+    gv[...] = add(gv_parts).astype(bf16)
+    gn[:, 0:width] = dot_nt(gk[...], wk[...]).astype(bf16)
+    gn[:, width : 2 * width] = dot_nt(gv[...], wv[...]).astype(bf16)
+
+
+def key_value_back(gk_parts, gv_parts, wk, wv, tables):
+    rows = tables[0].shape[0]
+    local = gk_parts[0].shape[1]
+    width = wk.shape[0]
+    block = min(256, rows)
+    spec = lambda cols: pl.BlockSpec((block, cols), lambda i: (i, 0))
+    whole = pl.BlockSpec((width, local), lambda i: (0, 0))
+    return pl.pallas_call(
+        functools.partial(key_value_back_kernel, len(gk_parts)),
+        grid=(rows // block,),
         out_shape=(
             jax.ShapeDtypeStruct((rows, local), bf16),
-            jax.ShapeDtypeStruct(k_all.shape, bf16),
-            jax.ShapeDtypeStruct(v_all.shape, bf16),
+            jax.ShapeDtypeStruct((rows, local), bf16),
+            jax.ShapeDtypeStruct((rows, 2 * width), bf16),
         ),
+        in_specs=[spec(local)] * (2 * len(gk_parts)) + [whole] * 2 + [spec(HD)] * 3,
+        out_specs=[spec(local), spec(local), spec(2 * width)],
+        compiler_params=params(48),
+        cost_estimate=small_cost,
+        name="key_value_back",
+    )(*gk_parts, *gv_parts, wk, wv, *tables)
+
+
+def weight_grad_kernel(half, core, nq, nk, nv, cot, gq, gk, gv, att, send_a, own_a, send_b, own_b):
+    step = pl.program_id(0)
+    local = gq.shape[1]
+
+    def fill(a, b):
+        a[:, 0:local] = dot_tn(nq[...], gq[...]).astype(bf16)
+        a[:, local : 2 * local] = dot_tn(nk[...], gk[...]).astype(bf16)
+        b[:, 0:local] = dot_tn(nv[...], gv[...]).astype(bf16)
+        b[:, local : 2 * local] = dot_tn(cot[...], att[...]).astype(bf16)
+
+    @pl.when(step < half)
+    def _():
+        fill(send_a, send_b)
+
+    @pl.when(step >= half)
+    def _():
+        fill(own_a, own_b)
+
+
+def weight_grads(core, nq, nkv, cot, gq, gk, gv, att):
+    rows, width = nq.shape
+    local = gq.shape[1]
+    block = 256
+    steps = width // block
+    half = steps // 2
+    column = lambda i, core: jnp.where(i < half, (1 - core[0]) * half + i, core[0] * half + i - half)
+    lhs = lambda shift: pl.BlockSpec((rows, block), lambda i, core: (0, column(i, core) + shift))
+    rhs = pl.BlockSpec((rows, local), lambda i, core: (0, 0))
+    out = jax.ShapeDtypeStruct((width // 2, 2 * local), bf16)
+    first = pl.BlockSpec((block, 2 * local), lambda i, core: (jnp.minimum(i, half - 1), 0))
+    second = pl.BlockSpec((block, 2 * local), lambda i, core: (jnp.maximum(i - half, 0), 0))
+    grid_spec = pltpu.PrefetchScalarGridSpec(
+        num_scalar_prefetch=1,
+        grid=(steps,),
+        in_specs=[lhs(0), lhs(0), lhs(steps), lhs(0)] + [rhs] * 4,
+        out_specs=[first, second, first, second],
+    )
+    return pl.pallas_call(
+        functools.partial(weight_grad_kernel, half),
+        grid_spec=grid_spec,
+        out_shape=(out, out, out, out),
+        compiler_params=params(48),
+        cost_estimate=small_cost,
+        name="weight_grads",
+    )(core, nq, nkv, nkv, cot, gq, gk, gv, att)
+
+
+def assemble_kernel(half, local, a_slot, b_slot, a_lo, a_hi, b_lo, b_hi, gwq, gwk, gwv, gwo):
+    r = pl.program_id(0)
+
+    @pl.when(a_slot[r] < half)
+    def _():
+        gwq[...] = a_lo[:, 0:local].astype(f32)
+        gwk[...] = a_lo[:, local : 2 * local].astype(f32)
+
+    @pl.when(a_slot[r] >= half)
+    def _():
+        gwq[...] = a_hi[:, 0:local].astype(f32)
+        gwk[...] = a_hi[:, local : 2 * local].astype(f32)
+
+    @pl.when(b_slot[r] < half)
+    def _():
+        gwv[...] = b_lo[:, 0:local].astype(f32)
+        gwo[...] = jnp.transpose(b_lo[:, local : 2 * local].astype(f32))
+
+    @pl.when(b_slot[r] >= half)
+    def _():
+        gwv[...] = b_hi[:, 0:local].astype(f32)
+        gwo[...] = jnp.transpose(b_hi[:, local : 2 * local].astype(f32))
+
+
+def assemble(a_slot, b_slot, a_lo, a_hi, b_lo, b_hi, pieces):
+    half = pieces // 2
+    piece = a_lo.shape[0] // half
+    local = a_lo.shape[1] // 2
+    width = pieces * piece
+    low = lambda pick: pl.BlockSpec(
+        (piece, 2 * local), lambda i, a, b: (jnp.minimum((a, b)[pick][i], half - 1), 0)
+    )
+    high = lambda pick: pl.BlockSpec(
+        (piece, 2 * local), lambda i, a, b: (jnp.maximum((a, b)[pick][i] - half, 0), 0)
+    )
+    rowed = pl.BlockSpec((piece, local), lambda i, a, b: (i, 0))
+    tall = jax.ShapeDtypeStruct((width, local), f32)
+    grid_spec = pltpu.PrefetchScalarGridSpec(
+        num_scalar_prefetch=2,
+        grid=(pieces,),
+        in_specs=[low(0), high(0), low(1), high(1)],
+        out_specs=[rowed, rowed, rowed, pl.BlockSpec((local, piece), lambda i, a, b: (0, i))],
+    )
+    return pl.pallas_call(
+        functools.partial(assemble_kernel, half, local),
+        grid_spec=grid_spec,
+        out_shape=(tall, tall, tall, jax.ShapeDtypeStruct((local, width), f32)),
         compiler_params=params(32),
-        cost_estimate=pl.CostEstimate(
-            flops=20 * rows * block * blocks * local, bytes_accessed=20 * MIB, transcendentals=0
-        ),
-        name="attend_back",
-    )(info, kslot, vslot, q, k_all, v_all, do, o, lse, span, *tables)
-
-
-def flipped(x, axis, bit):
+        name="assemble",
+    )(a_slot, b_slot, a_lo, a_hi, b_lo, b_hi)
+
+
+def flipped(x, axis, bit, sender=None):
     count = lax.axis_size(axis)
-    return lax.ppermute(x, axis, [(i, i ^ bit) for i in range(count)])
+    sends = [i for i in range(count) if sender is None or bool(i & bit) == sender]
+    return lax.ppermute(x, axis, [(i, i ^ bit) for i in sends])
+
+
+def top(bit):
+    return 2 * bit == lax.axis_size("seq")
 
 
 def bits_of(count):
@@ -546,37 +761,83 @@
     return order
 
 
-def slots_for(bits, rank, count):
-    order = slot_order(bits)
+def collect(block, bits):
+    held = {0: block}
+    for bit in bits:
+        sender = False if top(bit) else None
+        held.update({m | bit: flipped(x, "seq", bit, sender) for m, x in held.items()})
+    return held
+
+
+def summed(a, b):
+    return (a.astype(f32) + b.astype(f32)).astype(bf16)
+
+
+def disperse(low, high, bits):
+    terms = [low, flipped(high, "seq", bits[-1], True if top(bits[-1]) else None)]
+    half = low.shape[0] // 2
+    for bit in reversed(bits[:-1]):
+        total = functools.reduce(lambda a, b: a + b, [t[half : 2 * half].astype(f32) for t in terms])
+        terms.append(flipped(total.astype(bf16), "seq", bit, True if top(bit) else None))
+        half = half // 2
+    return terms
+
+
+def reduced(own, got, bits, rank):
+    for bit in bits:
+        half = own.shape[0] // 2
+        side = (rank & bit) // bit
+        cut = lambda x, at: lax.dynamic_slice_in_dim(x, at * half, half)
+        send = summed(cut(own, 1 - side), cut(got, 1 - side))
+        own = summed(cut(own, side), cut(got, side))
+        got = flipped(send, "seq", bit)
+    return summed(own, got)
+
+
+def spread(piece, bits):
+    held = piece
+    for bit in bits[:-1]:
+        held = jnp.concatenate([held, flipped(held, "seq", bit)], axis=0)
+    return held, flipped(held, "seq", bits[-1])
+
+
+def piece_slots(bits, rank, count):
+    order = slot_order(bits[::-1])
     table = [0] * count
     for slot, m in enumerate(order):
         table[m] = slot
-    return jnp.take(jnp.array(table, jnp.int32), jnp.arange(count, dtype=jnp.int32) ^ rank)
-
-
-def collect(block, bits):
-    pieces = [block]
-    held = block
-    for bit in bits:
-        got = flipped(held, "seq", bit)
-        pieces.append(got)
-        held = jnp.concatenate([held, got], axis=0)
-    return held
-
-
-def summed(a, b):
-    return (a.astype(f32) + b.astype(f32)).astype(bf16)
-
-
-def disperse(parts, bits):
-    held = parts
-    for at, bit in enumerate(reversed(bits)):
-        half = held.shape[0] // 2
-        got = flipped(held[half:], "seq", bit)
-        if at == len(bits) - 1:
-            return held[:half].astype(f32) + got.astype(f32)
-        held = summed(held[:half], got)
-    return held.astype(f32)
+    owners = []
+    for r in range(count):
+        owner = 0
+        for at, bit in enumerate(bits):
+            if (r >> (len(bits) - 1 - at)) & 1:
+                owner |= bit
+        owners.append(owner)
+    return jnp.take(jnp.array(table, jnp.int32), jnp.array(owners, jnp.int32) ^ rank)
+
+
+def ring(x, axis):
+    count = lax.axis_size(axis)
+    from_below, from_above = [], []
+    up = down = x
+    for k in range(1, count):
+        up = lax.ppermute(up, axis, [(i, i + 1) for i in range(k - 1, count - 1)])
+        down = lax.ppermute(down, axis, [(i, i - 1) for i in range(1, count - k + 1)])
+        from_below.append(up)
+        from_above.append(down)
+    return from_below + from_above
+
+
+def after(x, *earlier):
+    anywhere = pl.BlockSpec(memory_space=pl.ANY)
+    return pl.pallas_call(
+        lambda *refs: None,
+        out_shape=jax.ShapeDtypeStruct(x.shape, x.dtype),
+        in_specs=[anywhere] * (1 + len(earlier)),
+        out_specs=anywhere,
+        input_output_aliases={0: 0},
+        name="after",
+    )(x, *earlier)
 
 
 def small_sum(x):
@@ -625,54 +886,84 @@
     bits = bits_of(seq_count)
     key_bits = bits[1:] + bits[:1]
     value_bits = bits[1:][::-1] + bits[:1]
-    key_slots = slots_for(key_bits, rank, seq_count)
-    value_slots = slots_for(value_bits, rank, seq_count)
-
-    cot_full = gather(cotangent)
+    key_order = slot_order(key_bits)
+    value_order = slot_order(value_bits)
+    half = seq_count // 2
+    order = key_order[half:] + key_order[:half]
+    offsets = jnp.array(order, jnp.int32) ^ rank
+    key_at = jnp.array([key_order.index(m) for m in order], jnp.int32)
+    value_at = jnp.array([value_order.index(m) for m in order], jnp.int32)
+    same, down, up = tables
+    core = (rank & 1)[None].astype(jnp.int32)
+    cot_pieces = [cotangent] + ring(cotangent, "head")
     n3, nkv, nq, streams, coef, mix_pre = mix_forward(
         histories, norm_gains, mix_in, mix_out, mix_bias[None, :]
     )
-    n3_full = gather(n3)
-    nkv_full = gather(nkv)
+    n3_pieces = [n3] + ring(n3, "head")
+    nkv_full = gather(after(nkv, *n3_pieces[1:], *cot_pieces[1:]))
     nq_full = gather(nq)
-    ff_out, gn3_part, gw_up, gw_down = feed_forward(n3_full, cot_full, w_up, w_down)
+    ff_out, gn3_part, gw_up, gw_down, cot_full = feed_forward(
+        lax.axis_index("head")[None], n3_pieces, cot_pieces, w_up, w_down
+    )
     gn3 = scatter(gn3_part)
-    key, value = project(key_value_kernel, nkv_full, (w_key, w_value), tables, 2, "project_kv")
+    gw_up, gw_down = lax.psum((gw_up, gw_down), "seq")
+    key, value = project(
+        key_value_kernel, nkv_full, (w_key, w_value), (after(same, gn3_part), down, up), 2, "project_kv"
+    )
     (query,) = project(query_kernel, nq_full, (w_query,), tables, 1, "project_q")
-    k_all = collect(key, key_bits)
-    v_all = collect(value, value_bits)
-    attended, lse = attend(query, k_all, v_all, info, key_slots, value_slots, span, seq_count)
+    keys = collect(key, key_bits)
+    values = collect(value, value_bits)
+    keys, values = [keys[m] for m in order], [values[m] for m in order]
+    attended, lse = attend(query, keys, values, info, offsets, span)
     branch = scatter((ff_out + dot(attended, w_out)).astype(bf16))
     layer_out = (streams[3] + branch.astype(f32)).astype(bf16)
     do = dot_nt(cot_full, w_out).astype(bf16)
-    gw_out = dot_tn(attended, cot_full).astype(bf16)
-    gq, gk_parts, gv_parts = attend_back(
-        query, k_all, v_all, do, attended, lse, info, key_slots, value_slots, span, tables, seq_count
+    gq, gk_hi, gk_lo, gv_hi, gv_lo = attend_back(
+        query,
+        keys,
+        values,
+        do,
+        attended,
+        lse,
+        info,
+        offsets,
+        key_at,
+        value_at,
+        span,
+        tables,
     )
     gnq = scatter(dot_nt(gq, w_query).astype(bf16))
-    gk_wide = disperse(gk_parts, key_bits)
-    gv = disperse(gv_parts, value_bits).astype(bf16)
-    same, down, up = tables
-    heads = gk_wide.shape[1] // HD
-    gk3 = gk_wide.reshape(block_rows, heads, HD)
-    cos, sin = same[:, None, :HALF], -down[:, None, :HALF]
-    a, b = gk3[..., :HALF], gk3[..., HALF:ROT]
-    gk = (
-        jnp.concatenate([a * cos + b * sin, b * cos - a * sin, gk3[..., ROT:]], axis=-1)
-        .reshape(gk_wide.shape)
-        .astype(bf16)
-    )
-    gnkv = scatter(jnp.concatenate([dot_nt(gk, w_key), dot_nt(gv, w_value)], axis=1).astype(bf16))
-    gw_query = dot_tn(nq_full, gq).astype(bf16)
-    gw_key = dot_tn(nkv_full[:, :width], gk).astype(bf16)
-    gw_value = dot_tn(nkv_full[:, width:], gv).astype(bf16)
+    gk, gv, gnkv_part = key_value_back(
+        disperse(gk_lo, gk_hi, key_bits),
+        disperse(gv_lo, gv_hi, value_bits),
+        w_key,
+        w_value,
+        tables,
+    )
+    gnkv = scatter(gnkv_part)
+    gw_up, gw_down = gw_up.astype(f32), gw_down.astype(f32)
+    send_a, own_a, send_b, own_b = weight_grads(
+        core, nq_full, nkv_full, cot_full, gq, gk, gv, attended
+    )
+    got_a = flipped(send_a, "seq", 1)
+    got_b = flipped(send_b, "seq", 1)
+    a_bits = bits[1:]
+    b_bits = bits[1:][::-1]
+    a_lo, a_hi = spread(reduced(own_a, got_a, a_bits, rank), a_bits[::-1] + bits[:1])
+    b_lo, b_hi = spread(reduced(own_b, got_b, b_bits, rank), b_bits[::-1] + bits[:1])
+    gwq, gwk, gwv, gwo = assemble(
+        piece_slots(bits[:1] + a_bits, rank, seq_count),
+        piece_slots(bits[:1] + b_bits, rank, seq_count),
+        a_lo,
+        a_hi,
+        b_lo,
+        b_hi,
+        seq_count,
+    )
+    coef = after(coef, gw_up, gw_down)
     ghist, pack = unmix(
         histories, streams, gn3, gnkv, gnq, cotangent, coef, mix_pre, norm_gains, mix_in, mix_out
     )
-    big = lax.psum((gw_up, gw_down), "seq")
-    tied = lax.optimization_barrier((gw_query, gw_key, gw_value, gw_out) + big)
-    rest = lax.psum(tied[:4], "seq")
-    big = tied[4:]
     pack = small_sum(pack)
     return (
         layer_out,
@@ -681,12 +972,12 @@
         jnp.transpose(pack[:units, :width]),
         pack[:units, width : width + mixes],
         pack[units, width : width + mixes],
-        rest[0].astype(f32),
-        rest[1].astype(f32),
-        rest[2].astype(f32),
-        rest[3].astype(f32),
-        big[0].astype(f32),
-        big[1].astype(f32),
+        gwq,
+        gwk,
+        gwv,
+        gwo,
+        gw_up,
+        gw_down,
     )
 
 

time: 867 us -> 626 us (0.72)
  waiting for transfers between devices: 555 us -> 283 us
  Pallas kernels: 88.7 us -> 136 us
  matrix products: 25.7 us -> 7.75 us
  starting transfers between devices: 68.2 us -> 82.7 us
  local copies, waits for them, and re-layouts: 41.6 us -> 29.8 us
    psum x2 -> x1, waiting for transfers between devices: 180 us -> 0.02 us  [body(): gw_up, gw_down = lax.psum((gw_up, gw_down), 'seq')]
    reduce_scatter x4, waiting for transfers between devices: 171 us -> 0.06 us  [scatter(): return lax.psum_scatter(x, 'head', scatter_dimension=0, tiled=True)]
    ppermute x17 -> x49, waiting for transfers between devices: 82.1 us -> 246 us  [the longest x37 190 us: flipped(): return lax.ppermute(x, axis, [(i, i ^ bit) for i in sends])]
    all_gather x4 -> x2, waiting for transfers between devices: 120 us -> 34.6 us  [gather(): return lax.all_gather(x, 'head', axis=0, tiled=True)]
    pallas_call x2 -> x8, Pallas kernels: 45.2 us -> 78.1 us  [the longest x1 40.4 us: feed_forward(): pl.pallas_call(functools.partial(ff_kernel, count), grid_spec=grid_spec,...]
    ppermute x17 -> x49, starting transfers between devices: 67.2 us -> 82.1 us  [the longest x37 62.1 us: flipped(): return lax.ppermute(x, axis, [(i, i ^ bit) for i in sends])]
    pallas_call x1, Pallas kernels: 12 us -> 26 us  [attend_back(): pl.pallas_call(functools.partial(attend_back_kernel, scale, scale * log2e...]
    dot_general x4 -> x0, matrix products: 13.5 us -> none  [dot_tn(): lax.dot_general(a, b, (((0,), (0,)), ((), ())), preferred_element_type=f32)]
  transfers between devices with their start and end apart: 27 -> 56, of which waited for: 15 -> 25; matrix products, arithmetic and copies ran while one was open for 12% -> 12% of each run, Pallas kernels for 10% -> 20%
where the time goes in v2:
time: 626 us; the launch traced here: 617 us
  waiting for transfers between devices  283 us (45%)
  Pallas kernels  136 us (22%)
  starting transfers between devices  82.7 us (13%)
  other arithmetic  61.5 us (10%)
  local copies, waits for them, and re-layouts  29.8 us (5%)
  between operations  16.7 us (3%)
  matrix products  7.75 us (1%)
    ppermute x37, waiting for transfers between devices, flipped(): return lax.ppermute(x, axis, [(i, i ^ bit) for i in sends])  190 us
    ppermute x37, starting transfers between devices, flipped(): return lax.ppermute(x, axis, [(i, i ^ bit) for i in sends])  62.1 us
    ppermute x6, waiting for transfers between devices, ring(): lax.ppermute(down, axis, [(i, i - 1) for i in range(1, count - k + 1)])  46.8 us
    pallas_call x1, Pallas kernels, feed_forward(): pl.pallas_call(functools.partial(ff_kernel, count), grid_spec=grid_spec,...  40.4 us
    all_gather x2, waiting for transfers between devices, gather(): return lax.all_gather(x, 'head', axis=0, tiled=True)  34.6 us
    pallas_call x1, Pallas kernels, attend_back(): pl.pallas_call(functools.partial(attend_back_kernel, scale, scale * log2e...  26 us
    unnamed x136, local copies, waits for them, and re-layouts  25.8 us
    convert_element_type x2, other arithmetic, body(): gw_up, gw_down = (gw_up.astype(f32), gw_down.astype(f32))  23.5 us
  transfers between devices with their start and end apart: 56, of which 25 were waited for; matrix products, arithmetic and copies ran while one was open for 12% of the time, Pallas kernels for 20%

profile of v2, /device:TPU:0, one launch (start us, length us, event | category | flops | bytes accessed | tf_op | source)
XLA Modules:
  0.0 616.7 jit_solution(7307327768678493407)
XLA Ops:
  11.5 9.9 %mix_forward.1 = (bf16[128,2048]{1,0:T(8,128)(2,1)S(1)}, bf16[128,4096]{1,0:T(8,128)(2,1)S(1)}, bf16[128,2048]{1,0:T(8,128)(2,1)}, f32[4,128,2048]{2,1,0:T(8,128...) custom-call(bf16[9,128,2048]{2,1,0:T(8,128)(2,1)} %hist.3, f32[4,2048]{1,0:T(4,128)S(1)} %copy-done.33, ...), custom_call_target="tpu_custom_call" | custom-call | tf_op jit(solution)/shard_map/mix_forward/pallas_call | solution.py:104
  23.0 4.9 collective-permute-start
  35.2 5.1 collective-permute-done.refs_1_
  51.0 4.9 collective-permute-done.9.refs_11_.refs_10_
  58.0 9.2 %collective-permute-done.4.refs_5_ = bf16[128,2048]{1,0:T(8,128)(2,1)S(1)} collective-permute-done((bf16[128,2048]{1,0:T(8,128)(2,1)S(1)}, bf16[128,2048]{1,0:T(8,128)(2,1)S(1)}, u32[]{:S(2)}, u32[]{:S(2)}) %collective-permute-start.4) | collective-permute-done | bytes 524320 | tf_op jit(solution)/shard_map/ppermute | solution.py:825
  69.2 9.2 %collective-permute-done.10.refs_12_.refs_11_ = bf16[128,2048]{1,0:T(8,128)(2,1)S(1)} collective-permute-done((bf16[128,2048]{1,0:T(8,128)(2,1)S(1)}, bf16[128,2048]{1,0:T(8,128)(2,1)S(1)}, u32[]{:S(2)}, u32[]{:S(2)}) %collective-permute-start.10) | collective-permute-done | bytes 524320 | tf_op jit(solution)/shard_map/ppermute | solution.py:825
  79.8 9.9 %collective-permute-done.5.refs_6_ = bf16[128,2048]{1,0:T(8,128)(2,1)S(1)} collective-permute-done((bf16[128,2048]{1,0:T(8,128)(2,1)S(1)}, bf16[128,2048]{1,0:T(8,128)(2,1)S(1)}, u32[]{:S(2)}, u32[]{:S(2)}) %collective-permute-start.5) | collective-permute-done | bytes 524320 | tf_op jit(solution)/shard_map/ppermute | solution.py:825
  89.7 9.7 %collective-permute-done.11.refs_13_.refs_12_ = bf16[128,2048]{1,0:T(8,128)(2,1)S(1)} collective-permute-done((bf16[128,2048]{1,0:T(8,128)(2,1)S(1)}, bf16[128,2048]{1,0:T(8,128)(2,1)S(1)}, u32[]{:S(2)}, u32[]{:S(2)}) %collective-permute-start.11) | collective-permute-done | bytes 524320 | tf_op jit(solution)/shard_map/ppermute | solution.py:825
  101.1 40.4 %feed_forward.1 = (f32[512,2048]{1,0:T(8,128)}, bf16[512,2048]{1,0:T(8,128)(2,1)}, bf16[2048,2048]{1,0:T(8,128)(2,1)}, bf16[2048,2048]{1,0:T(8,128)(2,1)}, bf16[512,2048]{1,0:T(8,128)(2,1)}) custom-call(s32[1]{0:T(128)} %bitcast.2.rank_ref, bf16[128,2048]{1,0:T(8,128)(2,1)} %copy-done.30, bf16[128,2048]{1,0:T(8,128)(2,1)} %copy-done.52, ...), custom_call_target="tpu_custom_call" | custom-call | flops 1048576 | bytes 1048576 | tf_op jit(solution)/shard_map/feed_forward/pallas_call | solution.py:331
  145.5 34.6 %all-gather.5.cloned.1.call-done.n.nk.nv = bf16[512,4096]{1,0:T(8,128)(2,1)} async-done(((bf16[128,4096]{1,0:T(8,128)(2,1)}), bf16[512,4096]{1,0:T(8,128)(2,1)}) %all-gather.5.cloned.1.call-update) | async-done | bytes 4194320 | tf_op jit(solution)/shard_map/all_gather | solution.py:876
  197.3 17.4 %collective-permute-done.13.refs_5_.refs_17_ = bf16[512,512]{1,0:T(8,128)(2,1)S(1)} collective-permute-done((bf16[512,512]{1,0:T(8,128)(2,1)S(1)}, bf16[512,512]{1,0:T(8,128)(2,1)S(1)}, u32[]{:S(2)}, u32[]{:S(2)}) %collective-permute-start.13) | collective-permute-done | bytes 524320 | tf_op jit(solution)/shard_map/ppermute | solution.py:743
  217.2 5.3 collective-permute-start.17
  222.4 13.7 %collective-permute-done.22.refs_14_.refs_26_ = bf16[512,512]{1,0:T(8,128)(2,1)} collective-permute-done((bf16[512,512]{1,0:T(8,128)(2,1)S(1)}, bf16[512,512]{1,0:T(8,128)(2,1)}, u32[]{:S(2)}, u32[]{:S(2)}) %collective-permute-start.22) | collective-permute-done | bytes 524320 | tf_op jit(solution)/shard_map/ppermute | solution.py:743
  239.3 10.0 %collective-permute-done.17.refs_7_.refs_19_ = bf16[512,512]{1,0:T(8,128)(2,1)} collective-permute-done((bf16[512,512]{1,0:T(8,128)(2,1)S(1)}, bf16[512,512]{1,0:T(8,128)(2,1)}, u32[]{:S(2)}, u32[]{:S(2)}) %collective-permute-start.17) | collective-permute-done | bytes 524320 | tf_op jit(solution)/shard_map/ppermute | solution.py:743
  249.3 5.0 collective-permute-done.24.refs_15_.refs_27_
  264.2 8.3 %attend.1 = (bf16[512,512]{1,0:T(8,128)(2,1)}, f32[8,512]{1,0:T(8,128)}) custom-call(s32[2]{0:T(128)} %pad_add_fusion.info.refs_0_, s32[8]{0:T(128)} %broadcast_xor_fusion.offsets.refs_1_, bf16[512,512]{1,0:T(8,128)(2,1)} %copy-done.14, s32[8,512]{1,0:T(8,128)} %add_add_fusion.span.refs_8_, bf16[512,512]{1,0:T(8,128)(2,1)} %copy-done.46, ...), custom_call_target="tpu_custom_call" | custom-call | flops 1048576 | bytes 1048576 | tf_op jit(solution)/shard_map/attend/pallas_call | solution.py:489
  272.6 26.0 %attend_back.1 = (bf16[512,512]{1,0:T(8,128)(2,1)}, bf16[2048,512]{1,0:T(8,128)(2,1)}, bf16[2048,512]{1,0:T(8,128)(2,1)}, bf16[2048,512]{1,0:T(8,128)(2,1)}, bf16[2048,512]{1,0:T(8,128)(2,1)}) custom-call(s32[2]{0:T(128)} %pad_add_fusion.info.refs_0_, s32[8]{0:T(128)} %broadcast_xor_fusion.offsets.refs_1_, s32[8]{0:T(128)} %constant.86.clone.refs_2_, ...), custom_call_target="tpu_custom_call" | custom-call | flops 1048576 | bytes 1048576 | tf_op jit(solution)/shard_map/attend_back/pallas_call | solution.py:597
  298.6 6.3 %collective-permute-start.26 = (bf16[2048,512]{1,0:T(8,128)(2,1)}, bf16[2048,512]{1,0:T(8,128)(2,1)}, u32[]{:S(2)}, u32[]{:S(2)}) collective-permute-start(bf16[2048,512]{1,0:T(8,128)(2,1)} %get-tuple-element.58), channel_id=1, source_target_pairs={{0,4},{4,0},{8,12},{12,8},{16,20},{20,16},{24,28},{28,24},{1,5},{5... | collective-permute-start | bytes 6291464 | tf_op jit(solution)/shard_map/ppermute | solution.py:743
  314.5 12.0 %collective-permute-start.30 = (bf16[1024,512]{1,0:T(8,128)(2,1)S(1)}, bf16[1024,512]{1,0:T(8,128)(2,1)S(1)}, u32[]{:S(2)}, u32[]{:S(2)}) collective-permute-start(bf16[1024,512]{1,0:T(8,128)(2,1)S(1)} %add_convert_fusion.5), channel_id=1, source_target_pairs={{0,8},{4,12},{8,0},{12,4},{16,24},{20,28},{24,16},{28,20},{1,9},{5... | collective-permute-start | bytes 3145736 | tf_op jit(solution)/shard_map/ppermute | solution.py:743
  326.5 55.4 %collective-permute-done.27.refs_2_ = bf16[1024,512]{1,0:T(8,128)(2,1)S(1)} collective-permute-done((bf16[1024,512]{1,0:T(8,128)(2,1)S(1)}, bf16[1024,512]{1,0:T(8,128)(2,1)S(1)}, u32[]{:S(2)}, u32[]{:S(2)}) %collective-permute-start.27) | collective-permute-done | bytes 1048608 | tf_op jit(solution)/shard_map/ppermute | solution.py:743
  383.3 12.0 %collective-permute-start.28 = (bf16[512,512]{1,0:T(8,128)(2,1)S(1)}, bf16[512,512]{1,0:T(8,128)(2,1)S(1)}, u32[]{:S(2)}, u32[]{:S(2)}) collective-permute-start(bf16[512,512]{1,0:T(8,128)(2,1)S(1)} %add_convert_fusion.14), channel_id=1, source_target_pairs={{0,8},{4,12},{8,0},{12,4},{16,24},{20,28},{24,16},{28,20},{1,9},{5... | collective-permute-start | bytes 1572872 | tf_op jit(solution)/shard_map/ppermute | solution.py:743
  397.9 20.0 %collective-permute-done.28.refs_3_ = bf16[512,512]{1,0:T(8,128)(2,1)S(1)} collective-permute-done((bf16[512,512]{1,0:T(8,128)(2,1)S(1)}, bf16[512,512]{1,0:T(8,128)(2,1)S(1)}, u32[]{:S(2)}, u32[]{:S(2)}) %collective-permute-start.28) | collective-permute-done | bytes 524320 | tf_op jit(solution)/shard_map/ppermute | solution.py:743
  418.1 6.9 %key_value_back.1 = (bf16[512,512]{1,0:T(8,128)(2,1)S(1)}, bf16[512,512]{1,0:T(8,128)(2,1)S(1)}, bf16[512,4096]{1,0:T(8,128)(2,1)}) custom-call(bf16[2048,512]{1,0:T(8,128)(2,1)} %get-tuple-element.57.refs_0_, bf16[2048,512]{1,0:T(8,128)(2,1)} %collective-permute-done.26.refs_1_, bf16[1024,512]{1,0:T(8,128)(2,1)S(1)} %collective-permute-done.27.refs_2_, ...), custom_call_target="tpu_custom_call" | custom-call | flops 1048576 | bytes 1048576 | tf_op jit(solution)/shard_map/key_value_back/pallas_call | solution.py:625
  430.8 11.4 %weight_grads.1 = (bf16[1024,1024]{1,0:T(8,128)(2,1)}, bf16[1024,1024]{1,0:T(8,128)(2,1)}, bf16[1024,1024]{1,0:T(8,128)(2,1)}, bf16[1024,1024]{1,0:T(8,128)(2,1)}) custom-call(s32[1]{0:T(128)} %bitcast.8.core, bf16[512,2048]{1,0:T(8,128)(2,1)} %all-gather.3.cloned.1.call-done.n.nq, bf16[512,4096]{1,0:T(8,128)(2,1)} %all-gather.5.cloned.1.call-done.n.nk.nv, ...), custom_call_target="tpu_custom_call" | custom-call | flops 1048576 | bytes 1048576 | tf_op jit(solution)/shard_map/weight_grads/pallas_call | solution.py:678
  458.3 18.7 %collective-permute-done.38 = bf16[512,1024]{1,0:T(8,128)(2,1)} collective-permute-done((bf16[512,1024]{1,0:T(8,128)(2,1)}, bf16[512,1024]{1,0:T(8,128)(2,1)}, u32[]{:S(2)}, u32[]{:S(2)}) %collective-permute-start.38) | collective-permute-done | bytes 1048608 | tf_op jit(solution)/shard_map/ppermute | solution.py:743
  487.5 5.8 collective-permute-done.39
  501.2 11.8 %convert_element_type.227.refs_1_ = f32[2048,2048]{1,0:T(8,128)} convert(bf16[2048,2048]{1,0:T(8,128)(2,1)} %get-tuple-element.79) | non-fusion elementwise | flops 4194304 | bytes 25165824 | tf_op jit(solution)/shard_map/convert_element_type | solution.py:944
  512.9 11.7 %convert_element_type.228.refs_2_ = f32[2048,2048]{1,0:T(8,128)} convert(bf16[2048,2048]{1,0:T(8,128)(2,1)} %get-tuple-element.80) | non-fusion elementwise | flops 4194304 | bytes 25165824 | tf_op jit(solution)/shard_map/convert_element_type | solution.py:944
  529.8 15.3 %unmix.1 = (bf16[9,128,2048]{2,1,0:T(8,128)(2,1)}, f32[48,2176]{1,0:T(8,128)S(1)}) custom-call(bf16[9,128,2048]{2,1,0:T(8,128)(2,1)} %hist.3, f32[4,128,2048]{2,1,0:T(8,128)} %get-tuple-element.46.streams, bf16[128,2048]{1,0:T(8,128)(2,1)S(1)} %copy-done.23, bf16[128,4096]{1,0:T(8,128)(2,1)S(1)} %copy-done.22, bf16[128,2048]{1,0:T(8,128)(2,1)S(1)} %copy-done.24, ...), custom_call_target="tpu_custom_call" | custom-call | tf_op jit(solution)/shard_map/unmix/pallas_call | solution.py:206
  551.1 25.4 %collective-permute-done.33 = bf16[48,2176]{1,0:T(8,128)(2,1)S(1)} collective-permute-done((bf16[48,2176]{1,0:T(8,128)(2,1)S(1)}, bf16[48,2176]{1,0:T(8,128)(2,1)S(1)}, u32[]{:S(2)}, u32[]{:S(2)}) %collective-permute-start.33) | collective-permute-done | bytes 208928 | tf_op jit(solution)/shard_map/ppermute | solution.py:743
  585.2 5.1 collective-permute-done.35
  595.3 11.0 %assemble.1 = (f32[2048,512]{1,0:T(8,128)}, f32[2048,512]{1,0:T(8,128)}, f32[2048,512]{1,0:T(8,128)}, f32[512,2048]{1,0:T(8,128)}) custom-call(s32[8]{0:T(128)S(1)} %and_select_fusion.1.a_slot, s32[8]{0:T(128)S(1)} %and_select_fusion.b_slot, bf16[1024,1024]{1,0:T(8,128)(2,1)S(1)} %copy-done.3, bf16[1024,1024]{1,0:T(8,128)(2,1)} %collective-permute-done.42.a_hi, ...), custom_call_target="tpu_custom_call" | custom-call | tf_op jit(solution)/shard_map/assemble/pallas_call | solution.py:731
  (291 shorter events, 147.2 us)
Async XLA Ops:
  8.0 172.1 %all-gather.5.cloned.1.call-start = ((), (), s32[]{:S(2)}) async-start(), calls=%async_computation.5 | async-start | bytes 5242880 | tf_op jit(solution)/shard_map/all_gather | solution.py:876
  33.9 22.1 %collective-permute-start.9 = (bf16[128,2048]{1,0:T(8,128)(2,1)S(1)}, bf16[128,2048]{1,0:T(8,128)(2,1)S(1)}, u32[]{:S(2)}, u32[]{:S(2)}) collective-permute-start(bf16[128,2048]{1,0:T(8,128)(2,1)S(1)} %copy-done.20), channel_id=1, source_target_pairs={{1,0},{2,1},{3,2},{5,4},{6,5},{7,6},{9,8},{10,9},{11,10},{13,12},{... | collective-permute-start | bytes 1572872 | tf_op jit(solution)/shard_map/ppermute | solution.py:825
  44.7 22.5 %collective-permute-start.4 = (bf16[128,2048]{1,0:T(8,128)(2,1)S(1)}, bf16[128,2048]{1,0:T(8,128)(2,1)S(1)}, u32[]{:S(2)}, u32[]{:S(2)}) collective-permute-start(bf16[128,2048]{1,0:T(8,128)(2,1)S(1)} %collective-permute-done.3.refs_4_), channel_id=1, source_target_pairs={{1,0},{2,1},{5,4},{6,5},{9,8},{10,9},{13,12},{14,13},{17,16},{18,1... | collective-permute-start | bytes 1572872 | tf_op jit(solution)/shard_map/ppermute | solution.py:825
  56.0 22.5 %collective-permute-start.10 = (bf16[128,2048]{1,0:T(8,128)(2,1)S(1)}, bf16[128,2048]{1,0:T(8,128)(2,1)S(1)}, u32[]{:S(2)}, u32[]{:S(2)}) collective-permute-start(bf16[128,2048]{1,0:T(8,128)(2,1)S(1)} %collective-permute-done.9.refs_11_.refs_10_), channel_id=1, source_target_pairs={{1,0},{2,1},{5,4},{6,5},{9,8},{10,9},{13,12},{14,13},{17,16},{18,1... | collective-permute-start | bytes 1572872 | tf_op jit(solution)/shard_map/ppermute | solution.py:825
  57.3 22.4 %collective-permute-start.2 = (bf16[128,2048]{1,0:T(8,128)(2,1)S(1)}, bf16[128,2048]{1,0:T(8,128)(2,1)S(1)}, u32[]{:S(2)}, u32[]{:S(2)}) collective-permute-start(bf16[128,2048]{1,0:T(8,128)(2,1)S(1)} %collective-permute-done.1.refs_2_), channel_id=1, source_target_pairs={{2,3},{6,7},{10,11},{14,15},{18,19},{22,23},{26,27},{30,31}} | collective-permute-start | bytes 1572872 | tf_op jit(solution)/shard_map/ppermute | solution.py:824
  67.2 22.5 %collective-permute-start.5 = (bf16[128,2048]{1,0:T(8,128)(2,1)S(1)}, bf16[128,2048]{1,0:T(8,128)(2,1)S(1)}, u32[]{:S(2)}, u32[]{:S(2)}) collective-permute-start(bf16[128,2048]{1,0:T(8,128)(2,1)S(1)} %collective-permute-done.4.refs_5_), channel_id=1, source_target_pairs={{1,0},{5,4},{9,8},{13,12},{17,16},{21,20},{25,24},{29,28}} | collective-permute-start | bytes 1572872 | tf_op jit(solution)/shard_map/ppermute | solution.py:825
  100.3 157.9 %all-gather.3.cloned.1.call-start = ((), (), s32[]{:S(2)}) async-start(), calls=%async_computation.4 | async-start | bytes 2621440 | tf_op jit(solution)/shard_map/all_gather | solution.py:876
  101.1 400.1 %all-reduce.4.cloned.1.call-start = ((), (), s32[]{:S(2)}) async-start(), calls=%async_computation.10 | async-start | bytes 33554432 | tf_op jit(solution)/shard_map/psum | solution.py:909
  141.6 383.1 %reduce-scatter.7.cloned.1.call-start = ((), (), s32[]{:S(2)}) async-start(), calls=%async_computation.7 | async-start | bytes 2621440 | tf_op jit(solution)/shard_map/reduce_scatter | solution.py:879
  142.3 382.4 %reduce-scatter.11.cloned.1.call-start = ((), (), s32[]{:S(2)}) async-start(), calls=%async_computation.9 | async-start | bytes 2621440 | tf_op jit(solution)/shard_map/reduce_scatter | solution.py:879
  188.7 26.1 %collective-permute-start.13 = (bf16[512,512]{1,0:T(8,128)(2,1)S(1)}, bf16[512,512]{1,0:T(8,128)(2,1)S(1)}, u32[]{:S(2)}, u32[]{:S(2)}) collective-permute-start(bf16[512,512]{1,0:T(8,128)(2,1)S(1)} %get-tuple-element.52.refs_4_.refs_16_), channel_id=1, source_target_pairs={{0,8},{4,12},{8,0},{12,4},{16,24},{20,28},{24,16},{28,20},{1,9},{5... | collective-permute-start | bytes 1572872 | tf_op jit(solution)/shard_map/ppermute | solution.py:743
  190.2 26.9 %collective-permute-start.15 = (bf16[512,512]{1,0:T(8,128)(2,1)S(1)}, bf16[512,512]{1,0:T(8,128)(2,1)}, u32[]{:S(2)}, u32[]{:S(2)}) collective-permute-start(bf16[512,512]{1,0:T(8,128)(2,1)S(1)} %get-tuple-element.52.refs_4_.refs_16_), channel_id=1, source_target_pairs={{0,16},{4,20},{8,24},{12,28},{1,17},{5,21},{9,25},{13,29},{2,18},{... | collective-permute-start | bytes 1572872 | tf_op jit(solution)/shard_map/ppermute | solution.py:743
  194.5 41.6 %collective-permute-start.22 = (bf16[512,512]{1,0:T(8,128)(2,1)S(1)}, bf16[512,512]{1,0:T(8,128)(2,1)}, u32[]{:S(2)}, u32[]{:S(2)}) collective-permute-start(bf16[512,512]{1,0:T(8,128)(2,1)S(1)} %get-tuple-element.53.refs_12_.refs_24_), channel_id=1, source_target_pairs={{0,16},{4,20},{8,24},{12,28},{1,17},{5,21},{9,25},{13,29},{2,18},{... | collective-permute-start | bytes 1572872 | tf_op jit(solution)/shard_map/ppermute | solution.py:743
  196.6 42.1 %collective-permute-start.19 = (bf16[512,512]{1,0:T(8,128)(2,1)S(1)}, bf16[512,512]{1,0:T(8,128)(2,1)S(1)}, u32[]{:S(2)}, u32[]{:S(2)}) collective-permute-start(bf16[512,512]{1,0:T(8,128)(2,1)S(1)} %get-tuple-element.53.refs_12_.refs_24_), channel_id=1, source_target_pairs={{0,4},{4,0},{8,12},{12,8},{16,20},{20,16},{24,28},{28,24},{1,5},{5... | collective-permute-start | bytes 1572872 | tf_op jit(solution)/shard_map/ppermute | solution.py:743
  196.6 42.1 %collective-permute-start.20 = (bf16[512,512]{1,0:T(8,128)(2,1)S(1)}, bf16[512,512]{1,0:T(8,128)(2,1)}, u32[]{:S(2)}, u32[]{:S(2)}) collective-permute-start(bf16[512,512]{1,0:T(8,128)(2,1)S(1)} %get-tuple-element.53.refs_12_.refs_24_), channel_id=1, source_target_pairs={{0,8},{4,12},{8,0},{12,4},{16,24},{20,28},{24,16},{28,20},{1,9},{5... | collective-permute-start | bytes 1572872 | tf_op jit(solution)/shard_map/ppermute | solution.py:743
  214.8 24.4 %collective-permute-start.14 = (bf16[512,512]{1,0:T(8,128)(2,1)S(1)}, bf16[512,512]{1,0:T(8,128)(2,1)S(1)}, u32[]{:S(2)}, u32[]{:S(2)}) collective-permute-start(bf16[512,512]{1,0:T(8,128)(2,1)S(1)} %collective-permute-done.13.refs_5_.refs_17_), channel_id=1, source_target_pairs={{0,4},{4,0},{8,12},{12,8},{16,20},{20,16},{24,28},{28,24},{1,5},{5... | collective-permute-start | bytes 1572872 | tf_op jit(solution)/shard_map/ppermute | solution.py:743
  217.2 32.2 %collective-permute-start.17 = (bf16[512,512]{1,0:T(8,128)(2,1)S(1)}, bf16[512,512]{1,0:T(8,128)(2,1)}, u32[]{:S(2)}, u32[]{:S(2)}) collective-permute-start(bf16[512,512]{1,0:T(8,128)(2,1)S(1)} %collective-permute-done.13.refs_5_.refs_17_), channel_id=1, source_target_pairs={{0,16},{4,20},{8,24},{12,28},{1,17},{5,21},{9,25},{13,29},{2,18},{... | collective-permute-start | bytes 1572872 | tf_op jit(solution)/shard_map/ppermute | solution.py:743
  238.7 25.6 %collective-permute-start.23 = (bf16[512,512]{1,0:T(8,128)(2,1)}, bf16[512,512]{1,0:T(8,128)(2,1)}, u32[]{:S(2)}, u32[]{:S(2)}) collective-permute-start(bf16[512,512]{1,0:T(8,128)(2,1)} %collective-permute-done.22.refs_14_.refs_26_), channel_id=1, source_target_pairs={{0,4},{4,0},{8,12},{12,8},{16,20},{20,16},{24,28},{28,24},{1,5},{5... | collective-permute-start | bytes 1572872 | tf_op jit(solution)/shard_map/ppermute | solution.py:743
  238.7 25.5 %collective-permute-start.16 = (bf16[512,512]{1,0:T(8,128)(2,1)}, bf16[512,512]{1,0:T(8,128)(2,1)}, u32[]{:S(2)}, u32[]{:S(2)}) collective-permute-start(bf16[512,512]{1,0:T(8,128)(2,1)} %collective-permute-done.15.refs_6_.refs_18_), channel_id=1, source_target_pairs={{0,4},{4,0},{8,12},{12,8},{16,20},{20,16},{24,28},{28,24},{1,5},{5... | collective-permute-start | bytes 1572872 | tf_op jit(solution)/shard_map/ppermute | solution.py:743
  239.2 25.0 %collective-permute-start.21 = (bf16[512,512]{1,0:T(8,128)(2,1)}, bf16[512,512]{1,0:T(8,128)(2,1)}, u32[]{:S(2)}, u32[]{:S(2)}) collective-permute-start(bf16[512,512]{1,0:T(8,128)(2,1)} %collective-permute-done.20.refs_13_.refs_25_), channel_id=1, source_target_pairs={{0,4},{4,0},{8,12},{12,8},{16,20},{20,16},{24,28},{28,24},{1,5},{5... | collective-permute-start | bytes 1572872 | tf_op jit(solution)/shard_map/ppermute | solution.py:743
  309.5 215.2 %reduce-scatter.9.cloned.1.call-start = ((), (), s32[]{:S(2)}) async-start(), calls=%async_computation.8 | async-start | bytes 5242880 | tf_op jit(solution)/shard_map/reduce_scatter | solution.py:879
  311.5 70.4 %collective-permute-start.27 = (bf16[1024,512]{1,0:T(8,128)(2,1)S(1)}, bf16[1024,512]{1,0:T(8,128)(2,1)S(1)}, u32[]{:S(2)}, u32[]{:S(2)}) collective-permute-start(bf16[1024,512]{1,0:T(8,128)(2,1)S(1)} %add_convert_fusion.6), channel_id=1, source_target_pairs={{16,0},{20,4},{24,8},{28,12},{17,1},{21,5},{25,9},{29,13},{18,2},{... | collective-permute-start | bytes 3145736 | tf_op jit(solution)/shard_map/ppermute | solution.py:743
  314.5 80.8 %collective-permute-start.30 = (bf16[1024,512]{1,0:T(8,128)(2,1)S(1)}, bf16[1024,512]{1,0:T(8,128)(2,1)S(1)}, u32[]{:S(2)}, u32[]{:S(2)}) collective-permute-start(bf16[1024,512]{1,0:T(8,128)(2,1)S(1)} %add_convert_fusion.5), channel_id=1, source_target_pairs={{0,8},{4,12},{8,0},{12,4},{16,24},{20,28},{24,16},{28,20},{1,9},{5... | collective-permute-start | bytes 3145736 | tf_op jit(solution)/shard_map/ppermute | solution.py:743
  383.3 34.6 %collective-permute-start.28 = (bf16[512,512]{1,0:T(8,128)(2,1)S(1)}, bf16[512,512]{1,0:T(8,128)(2,1)S(1)}, u32[]{:S(2)}, u32[]{:S(2)}) collective-permute-start(bf16[512,512]{1,0:T(8,128)(2,1)S(1)} %add_convert_fusion.14), channel_id=1, source_target_pairs={{0,8},{4,12},{8,0},{12,4},{16,24},{20,28},{24,16},{28,20},{1,9},{5... | collective-permute-start | bytes 1572872 | tf_op jit(solution)/shard_map/ppermute | solution.py:743
  426.7 166.2 %reduce-scatter.5.cloned.1.call-start = ((), (), s32[]{:S(2)}) async-start(), calls=%async_computation.6 | async-start | bytes 2621440 | tf_op jit(solution)/shard_map/reduce_scatter | solution.py:879
  451.5 25.5 %collective-permute-start.38 = (bf16[512,1024]{1,0:T(8,128)(2,1)}, bf16[512,1024]{1,0:T(8,128)(2,1)}, u32[]{:S(2)}, u32[]{:S(2)}) collective-permute-start(bf16[512,1024]{1,0:T(8,128)(2,1)} %get-tuple-element.86), channel_id=1, source_target_pairs={{0,8},{4,12},{8,0},{12,4},{16,24},{20,28},{24,16},{28,20},{1,9},{5... | collective-permute-start | bytes 3145736 | tf_op jit(solution)/shard_map/ppermute | solution.py:743
  457.0 26.4 %collective-permute-start.44 = (bf16[512,1024]{1,0:T(8,128)(2,1)}, bf16[512,1024]{1,0:T(8,128)(2,1)}, u32[]{:S(2)}, u32[]{:S(2)}) collective-permute-start(bf16[512,1024]{1,0:T(8,128)(2,1)} %get-tuple-element.84), channel_id=1, source_target_pairs={{0,16},{4,20},{8,24},{12,28},{16,0},{20,4},{24,8},{28,12},{1,17},{... | collective-permute-start | bytes 3145736 | tf_op jit(solution)/shard_map/ppermute | solution.py:743
  494.8 50.5 %collective-permute-start.40 = (bf16[256,1024]{1,0:T(8,128)(2,1)S(1)}, bf16[256,1024]{1,0:T(8,128)(2,1)}, u32[]{:S(2)}, u32[]{:S(2)}) collective-permute-start(bf16[256,1024]{1,0:T(8,128)(2,1)S(1)} %add_convert_fusion.10), channel_id=1, source_target_pairs={{0,16},{4,20},{8,24},{12,28},{16,0},{20,4},{24,8},{28,12},{1,17},{... | collective-permute-start | bytes 1572872 | tf_op jit(solution)/shard_map/ppermute | solution.py:743
  499.2 48.8 %collective-permute-start.46 = (bf16[256,1024]{1,0:T(8,128)(2,1)}, bf16[256,1024]{1,0:T(8,128)(2,1)}, u32[]{:S(2)}, u32[]{:S(2)}) collective-permute-start(bf16[256,1024]{1,0:T(8,128)(2,1)} %add_convert_fusion.7), channel_id=1, source_target_pairs={{0,8},{4,12},{8,0},{12,4},{16,24},{20,28},{24,16},{28,20},{1,9},{5... | collective-permute-start | bytes 1572872 | tf_op jit(solution)/shard_map/ppermute | solution.py:743
  546.4 31.3 %collective-permute-start.41 = (bf16[512,1024]{1,0:T(8,128)(2,1)S(1)}, bf16[512,1024]{1,0:T(8,128)(2,1)S(1)}, u32[]{:S(2)}, u32[]{:S(2)}) collective-permute-start(bf16[512,1024]{1,0:T(8,128)(2,1)S(1)} %pad_maximum_fusion.2), channel_id=1, source_target_pairs={{0,8},{4,12},{8,0},{12,4},{16,24},{20,28},{24,16},{28,20},{1,9},{5... | collective-permute-start | bytes 3145736 | tf_op jit(solution)/shard_map/ppermute | solution.py:743
  549.3 29.8 %collective-permute-start.47 = (bf16[512,1024]{1,0:T(8,128)(2,1)S(1)}, bf16[512,1024]{1,0:T(8,128)(2,1)S(1)}, u32[]{:S(2)}, u32[]{:S(2)}) collective-permute-start(bf16[512,1024]{1,0:T(8,128)(2,1)S(1)} %pad_maximum_fusion.3), channel_id=1, source_target_pairs={{0,16},{4,20},{8,24},{12,28},{16,0},{20,4},{24,8},{28,12},{1,17},{... | collective-permute-start | bytes 3145736 | tf_op jit(solution)/shard_map/ppermute | solution.py:743
  550.2 26.3 %collective-permute-start.33 = (bf16[48,2176]{1,0:T(8,128)(2,1)S(1)}, bf16[48,2176]{1,0:T(8,128)(2,1)S(1)}, u32[]{:S(2)}, u32[]{:S(2)}) collective-permute-start(bf16[48,2176]{1,0:T(8,128)(2,1)S(1)} %add_convert_fusion.19), channel_id=1, source_target_pairs={{0,8},{4,12},{8,0},{12,4},{16,24},{20,28},{24,16},{28,20},{1,9},{5... | collective-permute-start | bytes 626696 | tf_op jit(solution)/shard_map/ppermute | solution.py:743
  (91 other events, 1930.5 us)
Sparse Core Ops, SparseCore 0:
  100.4 79.5 all-gather.4
  182.2 44.4 all-gather.2
  229.6 42.5 reduce-scatter.6
  309.6 76.1 reduce-scatter.10
  426.8 76.7 reduce-scatter.8
  506.4 44.3 reduce-scatter.4
Sparse Core Ops, SparseCore 1:
  141.7 275.8 all-reduce.3

commit v3 on v2

--- a/solution.py
+++ b/solution.py
@@ -783,12 +783,14 @@
     return terms
 
 
-def reduced(own, got, bits, rank):
-    for bit in bits:
+def reduced(own, got, bits, rank, midway):
+    for at, bit in enumerate(bits):
         half = own.shape[0] // 2
         side = (rank & bit) // bit
         cut = lambda x, at: lax.dynamic_slice_in_dim(x, at * half, half)
         send = summed(cut(own, 1 - side), cut(got, 1 - side))
+        if at == len(bits) - 1:
+            send = after(send, midway)
         own = summed(cut(own, side), cut(got, side))
         got = flipped(send, "seq", bit)
     return summed(own, got)
@@ -842,7 +844,7 @@
 
 def small_sum(x):
     x = x.astype(bf16)
-    for axis in ("seq", "head"):
+    for axis in ("head", "seq"):
         for bit in bits_of(lax.axis_size(axis)):
             x = summed(x, flipped(x, axis, bit))
     return x.astype(f32)
@@ -938,19 +940,21 @@
         disperse(gv_lo, gv_hi, value_bits),
         w_key,
         w_value,
-        tables,
+        (after(same, gn3), down, up),
     )
     gnkv = scatter(gnkv_part)
-    gw_up, gw_down = gw_up.astype(f32), gw_down.astype(f32)
     send_a, own_a, send_b, own_b = weight_grads(
-        core, nq_full, nkv_full, cot_full, gq, gk, gv, attended
+        core, nq_full, nkv_full, cot_full, gq, gk, after(gv, gw_up, gw_down), attended
     )
     got_a = flipped(send_a, "seq", 1)
     got_b = flipped(send_b, "seq", 1)
     a_bits = bits[1:]
     b_bits = bits[1:][::-1]
-    a_lo, a_hi = spread(reduced(own_a, got_a, a_bits, rank), a_bits[::-1] + bits[:1])
-    b_lo, b_hi = spread(reduced(own_b, got_b, b_bits, rank), b_bits[::-1] + bits[:1])
+    gw_up, gw_down = gw_up.astype(f32), gw_down.astype(f32)
+    piece_a = reduced(own_a, got_a, a_bits, rank, gw_up)
+    piece_b = after(reduced(own_b, got_b, b_bits, rank, gw_up), gw_down)
+    a_lo, a_hi = spread(piece_a, a_bits[::-1] + bits[:1])
+    b_lo, b_hi = spread(piece_b, b_bits[::-1] + bits[:1])
     gwq, gwk, gwv, gwo = assemble(
         piece_slots(bits[:1] + a_bits, rank, seq_count),
         piece_slots(bits[:1] + b_bits, rank, seq_count),
@@ -960,7 +964,7 @@
         b_hi,
         seq_count,
     )
-    coef = after(coef, gw_up, gw_down)
+    coef = after(coef, layer_out)
     ghist, pack = unmix(
         histories, streams, gn3, gnkv, gnq, cotangent, coef, mix_pre, norm_gains, mix_in, mix_out
     )

time: 626 us -> 601 us (0.960)
  waiting for transfers between devices: 283 us -> 258 us
    ppermute x37, waiting for transfers between devices: 190 us -> 171 us  [flipped(): return lax.ppermute(x, axis, [(i, i ^ bit) for i in sends])]
    ppermute x6, waiting for transfers between devices: 9.43 us -> 0.02 us  [ring(): up = lax.ppermute(up, axis, [(i, i + 1) for i in range(k - 1, count - 1)])]
    ppermute x37, starting transfers between devices: 62.1 us -> 54.4 us  [flipped(): return lax.ppermute(x, axis, [(i, i ^ bit) for i in sends])]
    unnamed x136 -> x126, local copies, waits for them, and re-layouts: 25.8 us -> 27 us
  transfers between devices with their start and end apart: 56 -> 56, of which waited for: 25 -> 24; matrix products, arithmetic and copies ran while one was open for 12% -> 13% of each run, Pallas kernels for 20% -> 23%
where the time goes in v3:
time: 601 us; the launch traced here: 592 us
  waiting for transfers between devices  258 us (43%)
  Pallas kernels  135 us (22%)
  starting transfers between devices  76.5 us (13%)
  other arithmetic  65.1 us (11%)
  local copies, waits for them, and re-layouts  31 us (5%)
  between operations  16.8 us (3%)
  matrix products  9.86 us (2%)
    ppermute x37, waiting for transfers between devices, flipped(): return lax.ppermute(x, axis, [(i, i ^ bit) for i in sends])  171 us
    ppermute x37, starting transfers between devices, flipped(): return lax.ppermute(x, axis, [(i, i ^ bit) for i in sends])  54.4 us
    ppermute x6, waiting for transfers between devices, ring(): lax.ppermute(down, axis, [(i, i - 1) for i in range(1, count - k + 1)])  46.2 us
    pallas_call x1, Pallas kernels, feed_forward(): pl.pallas_call(functools.partial(ff_kernel, count), grid_spec=grid_spec,...  40.3 us
    all_gather x2, waiting for transfers between devices, gather(): return lax.all_gather(x, 'head', axis=0, tiled=True)  38.8 us
    unnamed x126, local copies, waits for them, and re-layouts  27 us
    pallas_call x1, Pallas kernels, attend_back(): pl.pallas_call(functools.partial(attend_back_kernel, scale, scale * log2e...  25.3 us
    convert_element_type x2, other arithmetic, body(): gw_up, gw_down = (gw_up.astype(f32), gw_down.astype(f32))  23.4 us
  transfers between devices with their start and end apart: 56, of which 24 were waited for; matrix products, arithmetic and copies ran while one was open for 13% of the time, Pallas kernels for 23%

profile of v3, /device:TPU:0, one launch (start us, length us, event | category | flops | bytes accessed | tf_op | source)
XLA Modules:
  0.0 592.0 jit_solution(4822581725977400696)
XLA Ops:
  9.5 6.4 %collective-permute-start.6 = (bf16[128,2048]{1,0:T(8,128)(2,1)}, bf16[128,2048]{1,0:T(8,128)(2,1)}, u32[]{:S(2)}, u32[]{:S(2)}) collective-permute-start(bf16[128,2048]{1,0:T(8,128)(2,1)} %cot.1), channel_id=1, source_target_pairs={{0,1},{1,2},{2,3},{4,5},{5,6},{6,7},{8,9},{9,10},{10,11},{12,13},{... | collective-permute-start | bytes 1572872 | tf_op jit(solution)/shard_map/ppermute | solution.py:826
  19.2 9.8 %mix_forward.1 = (bf16[128,2048]{1,0:T(8,128)(2,1)S(1)}, bf16[128,4096]{1,0:T(8,128)(2,1)S(1)}, bf16[128,2048]{1,0:T(8,128)(2,1)}, f32[4,128,2048]{2,1,0:T(8,128...) custom-call(bf16[9,128,2048]{2,1,0:T(8,128)(2,1)} %hist.3, f32[4,2048]{1,0:T(4,128)S(1)} %copy-done.33, ...), custom_call_target="tpu_custom_call" | custom-call | tf_op jit(solution)/shard_map/mix_forward/pallas_call | solution.py:104
  31.9 4.6 collective-permute-start
  38.5 8.8 %collective-permute-done.3.refs_4_ = bf16[128,2048]{1,0:T(8,128)(2,1)S(1)} collective-permute-done((bf16[128,2048]{1,0:T(8,128)(2,1)S(1)}, bf16[128,2048]{1,0:T(8,128)(2,1)S(1)}, u32[]{:S(2)}, u32[]{:S(2)}) %collective-permute-start.3) | collective-permute-done | bytes 524320 | tf_op jit(solution)/shard_map/ppermute | solution.py:827
  49.4 9.2 %collective-permute-done.10.refs_12_.refs_11_ = bf16[128,2048]{1,0:T(8,128)(2,1)S(1)} collective-permute-done((bf16[128,2048]{1,0:T(8,128)(2,1)}, bf16[128,2048]{1,0:T(8,128)(2,1)S(1)}, u32[]{:S(2)}, u32[]{:S(2)}) %collective-permute-start.10) | collective-permute-done | bytes 524320 | tf_op jit(solution)/shard_map/ppermute | solution.py:827
  60.6 9.2 %collective-permute-done.4.refs_5_ = bf16[128,2048]{1,0:T(8,128)(2,1)S(1)} collective-permute-done((bf16[128,2048]{1,0:T(8,128)(2,1)S(1)}, bf16[128,2048]{1,0:T(8,128)(2,1)S(1)}, u32[]{:S(2)}, u32[]{:S(2)}) %collective-permute-start.4) | collective-permute-done | bytes 524320 | tf_op jit(solution)/shard_map/ppermute | solution.py:827
  71.8 9.2 %collective-permute-done.11.refs_13_.refs_12_ = bf16[128,2048]{1,0:T(8,128)(2,1)S(1)} collective-permute-done((bf16[128,2048]{1,0:T(8,128)(2,1)S(1)}, bf16[128,2048]{1,0:T(8,128)(2,1)S(1)}, u32[]{:S(2)}, u32[]{:S(2)}) %collective-permute-start.11) | collective-permute-done | bytes 524320 | tf_op jit(solution)/shard_map/ppermute | solution.py:827
  81.1 9.7 %collective-permute-done.5.refs_6_ = bf16[128,2048]{1,0:T(8,128)(2,1)S(1)} collective-permute-done((bf16[128,2048]{1,0:T(8,128)(2,1)S(1)}, bf16[128,2048]{1,0:T(8,128)(2,1)S(1)}, u32[]{:S(2)}, u32[]{:S(2)}) %collective-permute-start.5) | collective-permute-done | bytes 524320 | tf_op jit(solution)/shard_map/ppermute | solution.py:827
  93.3 40.3 %feed_forward.1 = (f32[512,2048]{1,0:T(8,128)}, bf16[512,2048]{1,0:T(8,128)(2,1)}, bf16[2048,2048]{1,0:T(8,128)(2,1)}, bf16[2048,2048]{1,0:T(8,128)(2,1)}, bf16[512,2048]{1,0:T(8,128)(2,1)}) custom-call(s32[1]{0:T(128)} %bitcast.2.rank_ref, bf16[128,2048]{1,0:T(8,128)(2,1)} %copy-done.30, bf16[128,2048]{1,0:T(8,128)(2,1)} %copy-done.50, ...), custom_call_target="tpu_custom_call" | custom-call | flops 1048576 | bytes 1048576 | tf_op jit(solution)/shard_map/feed_forward/pallas_call | solution.py:331
  137.4 38.8 %all-gather.5.cloned.1.call-done.n.nk.nv = bf16[512,4096]{1,0:T(8,128)(2,1)} async-done(((bf16[128,4096]{1,0:T(8,128)(2,1)}), bf16[512,4096]{1,0:T(8,128)(2,1)}) %all-gather.5.cloned.1.call-update) | async-done | bytes 4194320 | tf_op jit(solution)/shard_map/all_gather | solution.py:878
  192.2 19.3 %collective-permute-done.15.refs_6_.refs_18_ = bf16[512,512]{1,0:T(8,128)(2,1)S(1)} collective-permute-done((bf16[512,512]{1,0:T(8,128)(2,1)S(1)}, bf16[512,512]{1,0:T(8,128)(2,1)S(1)}, u32[]{:S(2)}, u32[]{:S(2)}) %collective-permute-start.15) | collective-permute-done | bytes 524320 | tf_op jit(solution)/shard_map/ppermute | solution.py:743
  217.2 16.8 %collective-permute-done.22.refs_14_.refs_26_ = bf16[512,512]{1,0:T(8,128)(2,1)} collective-permute-done((bf16[512,512]{1,0:T(8,128)(2,1)S(1)}, bf16[512,512]{1,0:T(8,128)(2,1)}, u32[]{:S(2)}, u32[]{:S(2)}) %collective-permute-start.22) | collective-permute-done | bytes 524320 | tf_op jit(solution)/shard_map/ppermute | solution.py:743
  237.4 10.9 %collective-permute-done.17.refs_7_.refs_19_ = bf16[512,512]{1,0:T(8,128)(2,1)} collective-permute-done((bf16[512,512]{1,0:T(8,128)(2,1)}, bf16[512,512]{1,0:T(8,128)(2,1)}, u32[]{:S(2)}, u32[]{:S(2)}) %collective-permute-start.17) | collective-permute-done | bytes 524320 | tf_op jit(solution)/shard_map/ppermute | solution.py:743
  259.3 8.5 %attend.1 = (bf16[512,512]{1,0:T(8,128)(2,1)}, f32[8,512]{1,0:T(8,128)}) custom-call(s32[2]{0:T(128)} %pad_add_fusion.info.refs_0_, s32[8]{0:T(128)} %broadcast_xor_fusion.offsets.refs_1_, bf16[512,512]{1,0:T(8,128)(2,1)} %copy-done.14, s32[8,512]{1,0:T(8,128)} %add_add_fusion.span.refs_8_, bf16[512,512]{1,0:T(8,128)(2,1)} %copy-done.45, ...), custom_call_target="tpu_custom_call" | custom-call | flops 1048576 | bytes 1048576 | tf_op jit(solution)/shard_map/attend/pallas_call | solution.py:489
  276.1 25.3 %attend_back.1 = (bf16[512,512]{1,0:T(8,128)(2,1)}, bf16[2048,512]{1,0:T(8,128)(2,1)}, bf16[2048,512]{1,0:T(8,128)(2,1)}, bf16[2048,512]{1,0:T(8,128)(2,1)}, bf16[2048,512]{1,0:T(8,128)(2,1)}) custom-call(s32[2]{0:T(128)} %pad_add_fusion.info.refs_0_, s32[8]{0:T(128)} %broadcast_xor_fusion.offsets.refs_1_, s32[8]{0:T(128)} %constant.86.clone.refs_2_, ...), custom_call_target="tpu_custom_call" | custom-call | flops 1048576 | bytes 1048576 | tf_op jit(solution)/shard_map/attend_back/pallas_call | solution.py:597
  301.4 6.3 %collective-permute-start.26 = (bf16[2048,512]{1,0:T(8,128)(2,1)}, bf16[2048,512]{1,0:T(8,128)(2,1)}, u32[]{:S(2)}, u32[]{:S(2)}) collective-permute-start(bf16[2048,512]{1,0:T(8,128)(2,1)} %get-tuple-element.58), channel_id=1, source_target_pairs={{0,4},{4,0},{8,12},{12,8},{16,20},{20,16},{24,28},{28,24},{1,5},{5... | collective-permute-start | bytes 6291464 | tf_op jit(solution)/shard_map/ppermute | solution.py:743
  317.6 9.8 %collective-permute-start.30 = (bf16[1024,512]{1,0:T(8,128)(2,1)S(1)}, bf16[1024,512]{1,0:T(8,128)(2,1)S(1)}, u32[]{:S(2)}, u32[]{:S(2)}) collective-permute-start(bf16[1024,512]{1,0:T(8,128)(2,1)S(1)} %add_convert_fusion.5), channel_id=1, source_target_pairs={{0,8},{4,12},{8,0},{12,4},{16,24},{20,28},{24,16},{28,20},{1,9},{5... | collective-permute-start | bytes 3145736 | tf_op jit(solution)/shard_map/ppermute | solution.py:743
  327.3 55.7 %collective-permute-done.27.refs_2_ = bf16[1024,512]{1,0:T(8,128)(2,1)S(1)} collective-permute-done((bf16[1024,512]{1,0:T(8,128)(2,1)S(1)}, bf16[1024,512]{1,0:T(8,128)(2,1)S(1)}, u32[]{:S(2)}, u32[]{:S(2)}) %collective-permute-start.27) | collective-permute-done | bytes 1048608 | tf_op jit(solution)/shard_map/ppermute | solution.py:743
  385.4 9.7 %collective-permute-start.28 = (bf16[512,512]{1,0:T(8,128)(2,1)}, bf16[512,512]{1,0:T(8,128)(2,1)}, u32[]{:S(2)}, u32[]{:S(2)}) collective-permute-start(bf16[512,512]{1,0:T(8,128)(2,1)} %add_convert_fusion.14), channel_id=1, source_target_pairs={{0,8},{4,12},{8,0},{12,4},{16,24},{20,28},{24,16},{28,20},{1,9},{5... | collective-permute-start | bytes 1572872 | tf_op jit(solution)/shard_map/ppermute | solution.py:743
  398.5 20.7 %collective-permute-done.28.refs_3_ = bf16[512,512]{1,0:T(8,128)(2,1)} collective-permute-done((bf16[512,512]{1,0:T(8,128)(2,1)}, bf16[512,512]{1,0:T(8,128)(2,1)}, u32[]{:S(2)}, u32[]{:S(2)}) %collective-permute-start.28) | collective-permute-done | bytes 524320 | tf_op jit(solution)/shard_map/ppermute | solution.py:743
  421.9 7.4 %key_value_back.1 = (bf16[512,512]{1,0:T(8,128)(2,1)S(1)}, bf16[512,512]{1,0:T(8,128)(2,1)S(1)}, bf16[512,4096]{1,0:T(8,128)(2,1)}) custom-call(bf16[2048,512]{1,0:T(8,128)(2,1)} %get-tuple-element.57.refs_0_, bf16[2048,512]{1,0:T(8,128)(2,1)} %collective-permute-done.26.refs_1_, bf16[1024,512]{1,0:T(8,128)(2,1)S(1)} %collective-permute-done.27.refs_2_, ...), custom_call_target="tpu_custom_call" | custom-call | flops 1048576 | bytes 1048576 | tf_op jit(solution)/shard_map/key_value_back/pallas_call | solution.py:625
  433.4 11.3 %weight_grads.1 = (bf16[1024,1024]{1,0:T(8,128)(2,1)}, bf16[1024,1024]{1,0:T(8,128)(2,1)}, bf16[1024,1024]{1,0:T(8,128)(2,1)}, bf16[1024,1024]{1,0:T(8,128)(2,1)}) custom-call(s32[1]{0:T(128)} %bitcast.8.core, bf16[512,2048]{1,0:T(8,128)(2,1)} %all-gather.3.cloned.1.call-done.n.nq, bf16[512,4096]{1,0:T(8,128)(2,1)} %all-gather.5.cloned.1.call-done.n.nk.nv, ...), custom_call_target="tpu_custom_call" | custom-call | flops 1048576 | bytes 1048576 | tf_op jit(solution)/shard_map/weight_grads/pallas_call | solution.py:678
  445.2 6.1 %collective-permute-done.37 = bf16[1024,1024]{1,0:T(8,128)(2,1)S(1)} collective-permute-done((bf16[1024,1024]{1,0:T(8,128)(2,1)}, bf16[1024,1024]{1,0:T(8,128)(2,1)S(1)}, u32[]{:S(2)}, u32[]{:S(2)}) %collective-permute-start.37) | collective-permute-done | bytes 2097184 | tf_op jit(solution)/shard_map/ppermute | solution.py:743
  462.4 11.7 %convert_element_type.257.refs_1_ = f32[2048,2048]{1,0:T(8,128)} convert(bf16[2048,2048]{1,0:T(8,128)(2,1)} %get-tuple-element.79.refs_1_) | non-fusion elementwise | flops 4194304 | bytes 25165824 | tf_op jit(solution)/shard_map/convert_element_type | solution.py:953
  474.1 8.2 %collective-permute-done.38 = bf16[512,1024]{1,0:T(8,128)(2,1)} collective-permute-done((bf16[512,1024]{1,0:T(8,128)(2,1)}, bf16[512,1024]{1,0:T(8,128)(2,1)}, u32[]{:S(2)}, u32[]{:S(2)}) %collective-permute-start.38) | collective-permute-done | bytes 1048608 | tf_op jit(solution)/shard_map/ppermute | solution.py:743
  484.3 4.3 collective-permute-done.44
  490.7 11.7 %convert_element_type.275.refs_1_ = f32[2048,2048]{1,0:T(8,128)} convert(bf16[2048,2048]{1,0:T(8,128)(2,1)} %get-tuple-element.80.refs_2_) | non-fusion elementwise | flops 4194304 | bytes 25165824 | tf_op jit(solution)/shard_map/convert_element_type | solution.py:953
  510.8 5.4 collective-permute-done.40
  525.6 15.4 %unmix.1 = (bf16[9,128,2048]{2,1,0:T(8,128)(2,1)}, f32[48,2176]{1,0:T(8,128)S(1)}) custom-call(bf16[9,128,2048]{2,1,0:T(8,128)(2,1)} %hist.3, f32[4,128,2048]{2,1,0:T(8,128)} %get-tuple-element.46.streams, bf16[128,2048]{1,0:T(8,128)(2,1)S(1)} %copy-done.21, bf16[128,4096]{1,0:T(8,128)(2,1)S(1)} %copy-done.25, bf16[128,2048]{1,0:T(8,128)(2,1)S(1)} %copy-done.26, ...), custom_call_target="tpu_custom_call" | custom-call | tf_op jit(solution)/shard_map/unmix/pallas_call | solution.py:206
  542.5 6.4 %collective-permute-done.32 = bf16[48,2176]{1,0:T(8,128)(2,1)S(1)} collective-permute-done((bf16[48,2176]{1,0:T(8,128)(2,1)S(1)}, bf16[48,2176]{1,0:T(8,128)(2,1)S(1)}, u32[]{:S(2)}, u32[]{:S(2)}) %collective-permute-start.32) | collective-permute-done | bytes 208928 | tf_op jit(solution)/shard_map/ppermute | solution.py:743
  562.5 6.1 %collective-permute-done.35 = bf16[48,2176]{1,0:T(8,128)(2,1)S(1)} collective-permute-done((bf16[48,2176]{1,0:T(8,128)(2,1)S(1)}, bf16[48,2176]{1,0:T(8,128)(2,1)S(1)}, u32[]{:S(2)}, u32[]{:S(2)}) %collective-permute-start.35) | collective-permute-done | bytes 208928 | tf_op jit(solution)/shard_map/ppermute | solution.py:743
  570.6 11.0 %assemble.1 = (f32[2048,512]{1,0:T(8,128)}, f32[2048,512]{1,0:T(8,128)}, f32[2048,512]{1,0:T(8,128)}, f32[512,2048]{1,0:T(8,128)}) custom-call(s32[8]{0:T(128)S(1)} %and_select_fusion.1.a_slot, s32[8]{0:T(128)S(1)} %and_select_fusion.b_slot, bf16[1024,1024]{1,0:T(8,128)(2,1)S(1)} %copy-done.5, bf16[1024,1024]{1,0:T(8,128)(2,1)} %collective-permute-done.42.a_hi, ...), custom_call_target="tpu_custom_call" | custom-call | tf_op jit(solution)/shard_map/assemble/pallas_call | solution.py:731
  (286 shorter events, 141.1 us)
Async XLA Ops:
  8.0 168.1 %all-gather.5.cloned.1.call-start = ((), (), s32[]{:S(2)}) async-start(), calls=%async_computation.5 | async-start | bytes 5242880 | tf_op jit(solution)/shard_map/all_gather | solution.py:878
  8.1 28.4 %collective-permute-start.9 = (bf16[128,2048]{1,0:T(8,128)(2,1)}, bf16[128,2048]{1,0:T(8,128)(2,1)}, u32[]{:S(2)}, u32[]{:S(2)}) collective-permute-start(bf16[128,2048]{1,0:T(8,128)(2,1)} %cot.1), channel_id=1, source_target_pairs={{1,0},{2,1},{3,2},{5,4},{6,5},{7,6},{9,8},{10,9},{11,10},{13,12},{... | collective-permute-start | bytes 1572872 | tf_op jit(solution)/shard_map/ppermute | solution.py:827
  9.5 28.3 %collective-permute-start.6 = (bf16[128,2048]{1,0:T(8,128)(2,1)}, bf16[128,2048]{1,0:T(8,128)(2,1)}, u32[]{:S(2)}, u32[]{:S(2)}) collective-permute-start(bf16[128,2048]{1,0:T(8,128)(2,1)} %cot.1), channel_id=1, source_target_pairs={{0,1},{1,2},{2,3},{4,5},{5,6},{6,7},{8,9},{9,10},{10,11},{12,13},{... | collective-permute-start | bytes 1572872 | tf_op jit(solution)/shard_map/ppermute | solution.py:826
  36.5 22.1 %collective-permute-start.10 = (bf16[128,2048]{1,0:T(8,128)(2,1)}, bf16[128,2048]{1,0:T(8,128)(2,1)S(1)}, u32[]{:S(2)}, u32[]{:S(2)}) collective-permute-start(bf16[128,2048]{1,0:T(8,128)(2,1)} %collective-permute-done.9.refs_11_.refs_10_), channel_id=1, source_target_pairs={{1,0},{2,1},{5,4},{6,5},{9,8},{10,9},{13,12},{14,13},{17,16},{18,1... | collective-permute-start | bytes 1572872 | tf_op jit(solution)/shard_map/ppermute | solution.py:827
  47.4 22.5 %collective-permute-start.4 = (bf16[128,2048]{1,0:T(8,128)(2,1)S(1)}, bf16[128,2048]{1,0:T(8,128)(2,1)S(1)}, u32[]{:S(2)}, u32[]{:S(2)}) collective-permute-start(bf16[128,2048]{1,0:T(8,128)(2,1)S(1)} %collective-permute-done.3.refs_4_), channel_id=1, source_target_pairs={{1,0},{2,1},{5,4},{6,5},{9,8},{10,9},{13,12},{14,13},{17,16},{18,1... | collective-permute-start | bytes 1572872 | tf_op jit(solution)/shard_map/ppermute | solution.py:827
  48.7 22.4 %collective-permute-start.1 = (bf16[128,2048]{1,0:T(8,128)(2,1)S(1)}, bf16[128,2048]{1,0:T(8,128)(2,1)S(1)}, u32[]{:S(2)}, u32[]{:S(2)}) collective-permute-start(bf16[128,2048]{1,0:T(8,128)(2,1)S(1)} %collective-permute-done.refs_1_), channel_id=1, source_target_pairs={{1,2},{2,3},{5,6},{6,7},{9,10},{10,11},{13,14},{14,15},{17,18},{18... | collective-permute-start | bytes 1572872 | tf_op jit(solution)/shard_map/ppermute | solution.py:826
  58.6 22.5 %collective-permute-start.11 = (bf16[128,2048]{1,0:T(8,128)(2,1)S(1)}, bf16[128,2048]{1,0:T(8,128)(2,1)S(1)}, u32[]{:S(2)}, u32[]{:S(2)}) collective-permute-start(bf16[128,2048]{1,0:T(8,128)(2,1)S(1)} %collective-permute-done.10.refs_12_.refs_11_), channel_id=1, source_target_pairs={{1,0},{5,4},{9,8},{13,12},{17,16},{21,20},{25,24},{29,28}} | collective-permute-start | bytes 1572872 | tf_op jit(solution)/shard_map/ppermute | solution.py:827
  92.5 160.8 %all-gather.3.cloned.1.call-start = ((), (), s32[]{:S(2)}) async-start(), calls=%async_computation.4 | async-start | bytes 2621440 | tf_op jit(solution)/shard_map/all_gather | solution.py:878
  93.2 305.3 %reduce-scatter.7.cloned.1.call-start = ((), (), s32[]{:S(2)}) async-start(), calls=%async_computation.7 | async-start | bytes 2621440 | tf_op jit(solution)/shard_map/reduce_scatter | solution.py:881
  133.6 297.3 %all-reduce.4.cloned.1.call-start = ((), (), s32[]{:S(2)}) async-start(), calls=%async_computation.10 | async-start | bytes 33554432 | tf_op jit(solution)/shard_map/psum | solution.py:911
  134.2 374.1 %reduce-scatter.5.cloned.1.call-start = ((), (), s32[]{:S(2)}) async-start(), calls=%async_computation.6 | async-start | bytes 2621440 | tf_op jit(solution)/shard_map/reduce_scatter | solution.py:881
  184.6 27.0 %collective-permute-start.15 = (bf16[512,512]{1,0:T(8,128)(2,1)S(1)}, bf16[512,512]{1,0:T(8,128)(2,1)S(1)}, u32[]{:S(2)}, u32[]{:S(2)}) collective-permute-start(bf16[512,512]{1,0:T(8,128)(2,1)S(1)} %get-tuple-element.52.refs_4_.refs_16_), channel_id=1, source_target_pairs={{0,16},{4,20},{8,24},{12,28},{1,17},{5,21},{9,25},{13,29},{2,18},{... | collective-permute-start | bytes 1572872 | tf_op jit(solution)/shard_map/ppermute | solution.py:743
  188.1 26.3 %collective-permute-start.13 = (bf16[512,512]{1,0:T(8,128)(2,1)S(1)}, bf16[512,512]{1,0:T(8,128)(2,1)}, u32[]{:S(2)}, u32[]{:S(2)}) collective-permute-start(bf16[512,512]{1,0:T(8,128)(2,1)S(1)} %get-tuple-element.52.refs_4_.refs_16_), channel_id=1, source_target_pairs={{0,8},{4,12},{8,0},{12,4},{16,24},{20,28},{24,16},{28,20},{1,9},{5... | collective-permute-start | bytes 1572872 | tf_op jit(solution)/shard_map/ppermute | solution.py:743
  189.6 24.8 %collective-permute-start.12 = (bf16[512,512]{1,0:T(8,128)(2,1)S(1)}, bf16[512,512]{1,0:T(8,128)(2,1)S(1)}, u32[]{:S(2)}, u32[]{:S(2)}) collective-permute-start(bf16[512,512]{1,0:T(8,128)(2,1)S(1)} %get-tuple-element.52.refs_4_.refs_16_), channel_id=1, source_target_pairs={{0,4},{4,0},{8,12},{12,8},{16,20},{20,16},{24,28},{28,24},{1,5},{5... | collective-permute-start | bytes 1572872 | tf_op jit(solution)/shard_map/ppermute | solution.py:743
  189.6 44.4 %collective-permute-start.22 = (bf16[512,512]{1,0:T(8,128)(2,1)S(1)}, bf16[512,512]{1,0:T(8,128)(2,1)}, u32[]{:S(2)}, u32[]{:S(2)}) collective-permute-start(bf16[512,512]{1,0:T(8,128)(2,1)S(1)} %get-tuple-element.53.refs_12_.refs_24_), channel_id=1, source_target_pairs={{0,16},{4,20},{8,24},{12,28},{1,17},{5,21},{9,25},{13,29},{2,18},{... | collective-permute-start | bytes 1572872 | tf_op jit(solution)/shard_map/ppermute | solution.py:743
  191.7 44.9 %collective-permute-start.20 = (bf16[512,512]{1,0:T(8,128)(2,1)S(1)}, bf16[512,512]{1,0:T(8,128)(2,1)}, u32[]{:S(2)}, u32[]{:S(2)}) collective-permute-start(bf16[512,512]{1,0:T(8,128)(2,1)S(1)} %get-tuple-element.53.refs_12_.refs_24_), channel_id=1, source_target_pairs={{0,8},{4,12},{8,0},{12,4},{16,24},{20,28},{24,16},{28,20},{1,9},{5... | collective-permute-start | bytes 1572872 | tf_op jit(solution)/shard_map/ppermute | solution.py:743
  211.6 25.0 %collective-permute-start.19 = (bf16[512,512]{1,0:T(8,128)(2,1)S(1)}, bf16[512,512]{1,0:T(8,128)(2,1)S(1)}, u32[]{:S(2)}, u32[]{:S(2)}) collective-permute-start(bf16[512,512]{1,0:T(8,128)(2,1)S(1)} %get-tuple-element.53.refs_12_.refs_24_), channel_id=1, source_target_pairs={{0,4},{4,0},{8,12},{12,8},{16,20},{20,16},{24,28},{28,24},{1,5},{5... | collective-permute-start | bytes 1572872 | tf_op jit(solution)/shard_map/ppermute | solution.py:743
  214.4 22.7 %collective-permute-start.16 = (bf16[512,512]{1,0:T(8,128)(2,1)S(1)}, bf16[512,512]{1,0:T(8,128)(2,1)S(1)}, u32[]{:S(2)}, u32[]{:S(2)}) collective-permute-start(bf16[512,512]{1,0:T(8,128)(2,1)S(1)} %collective-permute-done.15.refs_6_.refs_18_), channel_id=1, source_target_pairs={{0,4},{4,0},{8,12},{12,8},{16,20},{20,16},{24,28},{28,24},{1,5},{5... | collective-permute-start | bytes 1572872 | tf_op jit(solution)/shard_map/ppermute | solution.py:743
  214.4 33.9 %collective-permute-start.17 = (bf16[512,512]{1,0:T(8,128)(2,1)}, bf16[512,512]{1,0:T(8,128)(2,1)}, u32[]{:S(2)}, u32[]{:S(2)}) collective-permute-start(bf16[512,512]{1,0:T(8,128)(2,1)} %collective-permute-done.13.refs_5_.refs_17_), channel_id=1, source_target_pairs={{0,16},{4,20},{8,24},{12,28},{1,17},{5,21},{9,25},{13,29},{2,18},{... | collective-permute-start | bytes 1572872 | tf_op jit(solution)/shard_map/ppermute | solution.py:743
  236.5 22.7 %collective-permute-start.14 = (bf16[512,512]{1,0:T(8,128)(2,1)}, bf16[512,512]{1,0:T(8,128)(2,1)}, u32[]{:S(2)}, u32[]{:S(2)}) collective-permute-start(bf16[512,512]{1,0:T(8,128)(2,1)} %collective-permute-done.13.refs_5_.refs_17_), channel_id=1, source_target_pairs={{0,4},{4,0},{8,12},{12,8},{16,20},{20,16},{24,28},{28,24},{1,5},{5... | collective-permute-start | bytes 1572872 | tf_op jit(solution)/shard_map/ppermute | solution.py:743
  236.6 22.7 %collective-permute-start.23 = (bf16[512,512]{1,0:T(8,128)(2,1)}, bf16[512,512]{1,0:T(8,128)(2,1)}, u32[]{:S(2)}, u32[]{:S(2)}) collective-permute-start(bf16[512,512]{1,0:T(8,128)(2,1)} %collective-permute-done.22.refs_14_.refs_26_), channel_id=1, source_target_pairs={{0,4},{4,0},{8,12},{12,8},{16,20},{20,16},{24,28},{28,24},{1,5},{5... | collective-permute-start | bytes 1572872 | tf_op jit(solution)/shard_map/ppermute | solution.py:743
  237.1 22.1 %collective-permute-start.21 = (bf16[512,512]{1,0:T(8,128)(2,1)}, bf16[512,512]{1,0:T(8,128)(2,1)}, u32[]{:S(2)}, u32[]{:S(2)}) collective-permute-start(bf16[512,512]{1,0:T(8,128)(2,1)} %collective-permute-done.20.refs_13_.refs_25_), channel_id=1, source_target_pairs={{0,4},{4,0},{8,12},{12,8},{16,20},{20,16},{24,28},{28,24},{1,5},{5... | collective-permute-start | bytes 1572872 | tf_op jit(solution)/shard_map/ppermute | solution.py:743
  272.3 251.0 %reduce-scatter.11.cloned.1.call-start = ((), (), s32[]{:S(2)}) async-start(), calls=%async_computation.9 | async-start | bytes 2621440 | tf_op jit(solution)/shard_map/reduce_scatter | solution.py:881
  311.5 211.7 %reduce-scatter.9.cloned.1.call-start = ((), (), s32[]{:S(2)}) async-start(), calls=%async_computation.8 | async-start | bytes 5242880 | tf_op jit(solution)/shard_map/reduce_scatter | solution.py:881
  314.6 68.4 %collective-permute-start.27 = (bf16[1024,512]{1,0:T(8,128)(2,1)S(1)}, bf16[1024,512]{1,0:T(8,128)(2,1)S(1)}, u32[]{:S(2)}, u32[]{:S(2)}) collective-permute-start(bf16[1024,512]{1,0:T(8,128)(2,1)S(1)} %add_convert_fusion.6), channel_id=1, source_target_pairs={{16,0},{20,4},{24,8},{28,12},{17,1},{21,5},{25,9},{29,13},{18,2},{... | collective-permute-start | bytes 3145736 | tf_op jit(solution)/shard_map/ppermute | solution.py:743
  317.6 77.6 %collective-permute-start.30 = (bf16[1024,512]{1,0:T(8,128)(2,1)S(1)}, bf16[1024,512]{1,0:T(8,128)(2,1)S(1)}, u32[]{:S(2)}, u32[]{:S(2)}) collective-permute-start(bf16[1024,512]{1,0:T(8,128)(2,1)S(1)} %add_convert_fusion.5), channel_id=1, source_target_pairs={{0,8},{4,12},{8,0},{12,4},{16,24},{20,28},{24,16},{28,20},{1,9},{5... | collective-permute-start | bytes 3145736 | tf_op jit(solution)/shard_map/ppermute | solution.py:743
  385.4 33.8 %collective-permute-start.28 = (bf16[512,512]{1,0:T(8,128)(2,1)}, bf16[512,512]{1,0:T(8,128)(2,1)}, u32[]{:S(2)}, u32[]{:S(2)}) collective-permute-start(bf16[512,512]{1,0:T(8,128)(2,1)} %add_convert_fusion.14), channel_id=1, source_target_pairs={{0,8},{4,12},{8,0},{12,4},{16,24},{20,28},{24,16},{28,20},{1,9},{5... | collective-permute-start | bytes 1572872 | tf_op jit(solution)/shard_map/ppermute | solution.py:743
  397.2 23.8 %collective-permute-start.31 = (bf16[512,512]{1,0:T(8,128)(2,1)}, bf16[512,512]{1,0:T(8,128)(2,1)}, u32[]{:S(2)}, u32[]{:S(2)}) collective-permute-start(bf16[512,512]{1,0:T(8,128)(2,1)} %add_convert_fusion.13), channel_id=1, source_target_pairs={{16,0},{20,4},{24,8},{28,12},{17,1},{21,5},{25,9},{29,13},{18,2},{... | collective-permute-start | bytes 1572872 | tf_op jit(solution)/shard_map/ppermute | solution.py:743
  456.8 25.5 %collective-permute-start.38 = (bf16[512,1024]{1,0:T(8,128)(2,1)}, bf16[512,1024]{1,0:T(8,128)(2,1)}, u32[]{:S(2)}, u32[]{:S(2)}) collective-permute-start(bf16[512,1024]{1,0:T(8,128)(2,1)} %get-tuple-element.86), channel_id=1, source_target_pairs={{0,8},{4,12},{8,0},{12,4},{16,24},{20,28},{24,16},{28,20},{1,9},{5... | collective-permute-start | bytes 3145736 | tf_op jit(solution)/shard_map/ppermute | solution.py:743
  462.4 26.2 %collective-permute-start.44 = (bf16[512,1024]{1,0:T(8,128)(2,1)}, bf16[512,1024]{1,0:T(8,128)(2,1)}, u32[]{:S(2)}, u32[]{:S(2)}) collective-permute-start(bf16[512,1024]{1,0:T(8,128)(2,1)} %get-tuple-element.84), channel_id=1, source_target_pairs={{0,16},{4,20},{8,24},{12,28},{16,0},{20,4},{24,8},{28,12},{1,17},{... | collective-permute-start | bytes 3145736 | tf_op jit(solution)/shard_map/ppermute | solution.py:743
  518.2 33.4 %collective-permute-start.41 = (bf16[512,1024]{1,0:T(8,128)(2,1)}, bf16[512,1024]{1,0:T(8,128)(2,1)}, u32[]{:S(2)}, u32[]{:S(2)}) collective-permute-start(bf16[512,1024]{1,0:T(8,128)(2,1)} %pad_maximum_fusion.2), channel_id=1, source_target_pairs={{0,8},{4,12},{8,0},{12,4},{16,24},{20,28},{24,16},{28,20},{1,9},{5... | collective-permute-start | bytes 3145736 | tf_op jit(solution)/shard_map/ppermute | solution.py:743
  521.8 31.5 %collective-permute-start.47 = (bf16[512,1024]{1,0:T(8,128)(2,1)}, bf16[512,1024]{1,0:T(8,128)(2,1)}, u32[]{:S(2)}, u32[]{:S(2)}) collective-permute-start(bf16[512,1024]{1,0:T(8,128)(2,1)} %pad_maximum_fusion.3), channel_id=1, source_target_pairs={{0,16},{4,20},{8,24},{12,28},{16,0},{20,4},{24,8},{28,12},{1,17},{... | collective-permute-start | bytes 3145736 | tf_op jit(solution)/shard_map/ppermute | solution.py:743
  (86 other events, 1531.6 us)
Sparse Core Ops, SparseCore 0:
  92.6 83.5 all-gather.4
  178.3 44.3 all-gather.2
  225.6 42.5 reduce-scatter.6
  272.4 60.2 reduce-scatter.4
  334.8 49.2 reduce-scatter.10
  431.1 76.7 reduce-scatter.8
Sparse Core Ops, SparseCore 1:
  138.7 282.4 all-reduce.3

commit v4 on v3

--- a/solution.py
+++ b/solution.py
@@ -30,7 +30,7 @@
 
 
 def params(mib, **more):
-    return pltpu.CompilerParams(vmem_limit_bytes=mib * MIB, **more)
+    return pltpu.CompilerParams(vmem_limit_bytes=60 * MIB, **more)
 
 
 def cdf(x):
@@ -201,7 +201,7 @@
     count = norm_gains.shape[0]
     units = mix_in.shape[1]
     mixes = count * hist_count
-    tile = 16
+    tile = 32
     whole = lambda shape: pl.BlockSpec(shape, lambda i: (0, 0))
     return pl.pallas_call(
         unmix_kernel,
@@ -242,9 +242,8 @@
 def ff_kernel(count, rank_ref, *refs):
     pieces = 2 * count - 1
     sources = (refs[:pieces], refs[pieces : 2 * pieces])
-    w_up, w_down, ff_out, gn3, gw_up, gw_down, cot, n3, gn_acc, sems = refs[2 * pieces :]
+    w_up, w_down, act, grad, gw_up, gw_down, cot, n3, sems = refs[2 * pieces :]
     step = pl.program_id(0)
-    last = pl.num_programs(0) - 1
 
     @pl.when(step == 0)
     def _():
@@ -276,27 +275,11 @@
 
     pre = dot(n3[...], w_up[...])
     phi = cdf(pre)
-    act = (pre * phi).astype(bf16)
+    act[...] = (pre * phi).astype(bf16)
     slope = phi + pre * pdf(pre)
-    grad = (dot_nt(cot[...], w_down[...]) * slope).astype(bf16)
-    gw_down[...] = dot_tn(act, cot[...]).astype(bf16)
-    gw_up[...] = dot_tn(n3[...], grad).astype(bf16)
-    part_out = dot(act, w_down[...])
-    part_gn = dot_nt(grad, w_up[...])
-
-    @pl.when(step == 0)
-    def _():
-        ff_out[...] = part_out
-        gn_acc[...] = part_gn
-
-    @pl.when(step > 0)
-    def _():
-        ff_out[...] += part_out
-        gn_acc[...] += part_gn
-
-    @pl.when(step == last)
-    def _():
-        gn3[...] = gn_acc[...].astype(bf16)
+    grad[...] = (dot_nt(cot[...], w_down[...]) * slope).astype(bf16)
+    gw_down[...] = dot_tn(act[...], cot[...]).astype(bf16)
+    gw_up[...] = dot_tn(n3[...], grad[...]).astype(bf16)
 
 
 def feed_forward(rank, n3_pieces, cot_pieces, w_up, w_down):
@@ -316,15 +299,14 @@
             pl.BlockSpec((block, width), lambda i, r: (i, 0)),
         ],
         out_specs=[
-            fixed,
-            fixed,
+            pl.BlockSpec((rows, block), lambda i, r: (0, i)),
+            pl.BlockSpec((rows, block), lambda i, r: (0, i)),
             pl.BlockSpec((width, block), lambda i, r: (0, i)),
             pl.BlockSpec((block, width), lambda i, r: (i, 0)),
             fixed,
         ],
         scratch_shapes=[
             pltpu.VMEM((rows, width), bf16),
-            pltpu.VMEM((rows, width), f32),
             pltpu.SemaphoreType.DMA((2, len(n3_pieces))),
         ],
     )
@@ -332,8 +314,8 @@
         functools.partial(ff_kernel, count),
         grid_spec=grid_spec,
         out_shape=(
-            jax.ShapeDtypeStruct((rows, width), f32),
-            jax.ShapeDtypeStruct((rows, width), bf16),
+            jax.ShapeDtypeStruct((rows, hidden), bf16),
+            jax.ShapeDtypeStruct((rows, hidden), bf16),
             jax.ShapeDtypeStruct((width, hidden), bf16),
             jax.ShapeDtypeStruct((hidden, width), bf16),
             jax.ShapeDtypeStruct((rows, width), bf16),
@@ -342,6 +324,37 @@
         cost_estimate=small_cost,
         name="feed_forward",
     )(rank, *n3_pieces, *cot_pieces, w_up, w_down)
+
+
+def ff_sums_kernel(act, grad, w_up, w_down, ff_out, gn3):
+    ff_out[...] = dot(act[...], w_down[...])
+    gn3[...] = dot_nt(grad[...], w_up[...]).astype(bf16)
+
+
+def feed_forward_sums(act, grad, w_up, w_down):
+    rows, hidden = act.shape
+    width = w_up.shape[0]
+    block = min(512, width)
+    fixed = pl.BlockSpec((rows, hidden), lambda i: (0, 0))
+    out = pl.BlockSpec((rows, block), lambda i: (0, i))
+    return pl.pallas_call(
+        ff_sums_kernel,
+        grid=(width // block,),
+        out_shape=(
+            jax.ShapeDtypeStruct((rows, width), f32),
+            jax.ShapeDtypeStruct((rows, width), bf16),
+        ),
+        in_specs=[
+            fixed,
+            fixed,
+            pl.BlockSpec((block, hidden), lambda i: (i, 0)),
+            pl.BlockSpec((hidden, block), lambda i: (0, i)),
+        ],
+        out_specs=[out, out],
+        compiler_params=params(56),
+        cost_estimate=small_cost,
+        name="feed_forward_sums",
+    )(act, grad, w_up, w_down)
 
 
 def turn(x, same, down, up):
@@ -783,17 +796,70 @@
     return terms
 
 
-def reduced(own, got, bits, rank, midway):
-    for at, bit in enumerate(bits):
-        half = own.shape[0] // 2
-        side = (rank & bit) // bit
-        cut = lambda x, at: lax.dynamic_slice_in_dim(x, at * half, half)
-        send = summed(cut(own, 1 - side), cut(got, 1 - side))
-        if at == len(bits) - 1:
-            send = after(send, midway)
-        own = summed(cut(own, side), cut(got, side))
-        got = flipped(send, "seq", bit)
-    return summed(own, got)
+def merge_kernel(count, blocks, sides, *refs):
+    step = pl.program_id(0)
+    ins, outs = refs[: 2 * count], refs[2 * count :]
+
+    @pl.when(step < blocks)
+    def _():
+        for i in range(count):
+            outs[2 * i][...] = summed(ins[2 * i][...], ins[2 * i + 1][...])
+
+    @pl.when(step >= blocks)
+    def _():
+        for i in range(count):
+            outs[2 * i + 1][...] = summed(ins[2 * i][...], ins[2 * i + 1][...])
+
+
+def reduce_level(pairs, bits, rank, midway=None):
+    sides = jnp.stack([(rank & bit) // bit for bit in bits]).astype(jnp.int32)
+    blocks = 2
+    in_specs, out_specs, out_shape = [], [], []
+    for at, (own, _) in enumerate(pairs):
+        half, cols = own.shape[0] // 2, own.shape[1]
+        block = half // blocks
+
+        def pick(i, sides, at=at):
+            side = sides[at]
+            return (jnp.where(i < blocks, (1 - side) * blocks + i, side * blocks + i - blocks), 0)
+
+        in_specs += [pl.BlockSpec((block, cols), pick)] * 2
+        out_specs.append(pl.BlockSpec((block, cols), lambda i, sides: (jnp.minimum(i, blocks - 1), 0)))
+        out_specs.append(pl.BlockSpec((block, cols), lambda i, sides: (jnp.maximum(i - blocks, 0), 0)))
+        out_shape += [jax.ShapeDtypeStruct((half, cols), bf16)] * 2
+    outs = pl.pallas_call(
+        functools.partial(merge_kernel, len(pairs), blocks),
+        grid_spec=pltpu.PrefetchScalarGridSpec(
+            num_scalar_prefetch=1, grid=(2 * blocks,), in_specs=in_specs, out_specs=out_specs
+        ),
+        out_shape=out_shape,
+        compiler_params=params(32),
+        cost_estimate=small_cost,
+        name="merge",
+    )(sides, *[x for pair in pairs for x in pair])
+    pairs = []
+    for i, bit in enumerate(bits):
+        send = outs[2 * i] if midway is None else after(outs[2 * i], midway)
+        pairs.append((outs[2 * i + 1], flipped(send, "seq", bit)))
+    return pairs
+
+
+def widen_kernel(x, out):
+    out[...] = x[...].astype(f32)
+
+
+def widened(x):
+    rows, cols = x.shape
+    spec = pl.BlockSpec((min(512, rows), cols), lambda i: (i, 0))
+    return pl.pallas_call(
+        widen_kernel,
+        grid=(rows // min(512, rows),),
+        out_shape=jax.ShapeDtypeStruct(x.shape, f32),
+        in_specs=[spec],
+        out_specs=spec,
+        compiler_params=params(48),
+        name="widen",
+    )(x)
 
 
 def spread(piece, bits):
@@ -842,9 +908,11 @@
     )(x, *earlier)
 
 
-def small_sum(x):
+def small_sum(x, midway):
     x = x.astype(bf16)
-    for axis in ("head", "seq"):
+    for axis in ("seq", "head"):
+        if axis == "head":
+            x = after(x, midway)
         for bit in bits_of(lax.axis_size(axis)):
             x = summed(x, flipped(x, axis, bit))
     return x.astype(f32)
@@ -904,22 +972,19 @@
     n3_pieces = [n3] + ring(n3, "head")
     nkv_full = gather(after(nkv, *n3_pieces[1:], *cot_pieces[1:]))
     nq_full = gather(nq)
-    ff_out, gn3_part, gw_up, gw_down, cot_full = feed_forward(
+    act, ff_grad, gw_up, gw_down, cot_full = feed_forward(
         lax.axis_index("head")[None], n3_pieces, cot_pieces, w_up, w_down
     )
-    gn3 = scatter(gn3_part)
     gw_up, gw_down = lax.psum((gw_up, gw_down), "seq")
     key, value = project(
-        key_value_kernel, nkv_full, (w_key, w_value), (after(same, gn3_part), down, up), 2, "project_kv"
+        key_value_kernel, nkv_full, (w_key, w_value), (after(same, act), down, up), 2, "project_kv"
     )
     (query,) = project(query_kernel, nq_full, (w_query,), tables, 1, "project_q")
     keys = collect(key, key_bits)
     values = collect(value, value_bits)
     keys, values = [keys[m] for m in order], [values[m] for m in order]
-    attended, lse = attend(query, keys, values, info, offsets, span)
-    branch = scatter((ff_out + dot(attended, w_out)).astype(bf16))
-    layer_out = (streams[3] + branch.astype(f32)).astype(bf16)
     do = dot_nt(cot_full, w_out).astype(bf16)
+    attended, lse = attend(query, keys, values, info, offsets, after(span, do))
     gq, gk_hi, gk_lo, gv_hi, gv_lo = attend_back(
         query,
         keys,
@@ -935,24 +1000,30 @@
         tables,
     )
     gnq = scatter(dot_nt(gq, w_query).astype(bf16))
+    ff_out, gn3_part = feed_forward_sums(after(act, gq), ff_grad, w_up, w_down)
+    gn3 = scatter(gn3_part)
+    branch_part = (ff_out + dot(attended, w_out)).astype(bf16)
+    branch = scatter(branch_part)
+    layer_out = (streams[3] + branch.astype(f32)).astype(bf16)
     gk, gv, gnkv_part = key_value_back(
         disperse(gk_lo, gk_hi, key_bits),
         disperse(gv_lo, gv_hi, value_bits),
         w_key,
         w_value,
-        (after(same, gn3), down, up),
+        (after(same, gn3_part, branch_part), down, up),
     )
     gnkv = scatter(gnkv_part)
     send_a, own_a, send_b, own_b = weight_grads(
         core, nq_full, nkv_full, cot_full, gq, gk, after(gv, gw_up, gw_down), attended
     )
-    got_a = flipped(send_a, "seq", 1)
-    got_b = flipped(send_b, "seq", 1)
+    pairs = [(own_a, flipped(send_a, "seq", 1)), (own_b, flipped(send_b, "seq", 1))]
     a_bits = bits[1:]
     b_bits = bits[1:][::-1]
-    gw_up, gw_down = gw_up.astype(f32), gw_down.astype(f32)
-    piece_a = reduced(own_a, got_a, a_bits, rank, gw_up)
-    piece_b = after(reduced(own_b, got_b, b_bits, rank, gw_up), gw_down)
+    gw_up, gw_down = widened(gw_up), widened(gw_down)
+    for level in range(len(a_bits)):
+        last = level == len(a_bits) - 1
+        pairs = reduce_level(pairs, (a_bits[level], b_bits[level]), rank, gw_up if last else None)
+    piece_a, piece_b = summed(*pairs[0]), summed(*pairs[1])
     a_lo, a_hi = spread(piece_a, a_bits[::-1] + bits[:1])
     b_lo, b_hi = spread(piece_b, b_bits[::-1] + bits[:1])
     gwq, gwk, gwv, gwo = assemble(
@@ -964,11 +1035,10 @@
         b_hi,
         seq_count,
     )
-    coef = after(coef, layer_out)
     ghist, pack = unmix(
         histories, streams, gn3, gnkv, gnq, cotangent, coef, mix_pre, norm_gains, mix_in, mix_out
     )
-    pack = small_sum(pack)
+    pack = small_sum(pack, gw_down)
     return (
         layer_out,
         ghist,

time: 601 us -> 587 us (0.977)
  other arithmetic: 65.1 us -> 28.2 us
  Pallas kernels: 135 us -> 163 us
  local copies, waits for them, and re-layouts: 31 us -> 12.6 us
  waiting for transfers between devices: 258 us -> 268 us
    pallas_call x0 -> x5, Pallas kernels: none -> 46.1 us  [the longest x2 19.1 us: widened(): pl.pallas_call(widen_kernel, grid=(rows // min(512, rows),), out_shape=ja...]
    convert_element_type x3 -> x1, other arithmetic: 25.3 us -> 1.95 us  [body(): branch_part = (ff_out + dot(attended, w_out)).astype(bf16)]
    unnamed x126 -> x87, local copies, waits for them, and re-layouts: 27 us -> 7.82 us
    pallas_call x1, Pallas kernels: 40.3 us -> 25.5 us  [feed_forward(): pl.pallas_call(functools.partial(ff_kernel, count), grid_spec=grid_spec,...]
    convert_element_type x10 -> x6, other arithmetic: 16.3 us -> 2.21 us  [summed(): return (a.astype(f32) + b.astype(f32)).astype(bf16)]
    all_gather x2, waiting for transfers between devices: 38.8 us -> 52.7 us  [gather(): return lax.all_gather(x, 'head', axis=0, tiled=True)]
    pallas_call x1, Pallas kernels: 25.3 us -> 15 us  [attend_back(): pl.pallas_call(functools.partial(attend_back_kernel, scale, scale * log2e...]
  transfers between devices with their start and end apart: 56 -> 56, of which waited for: 24 -> 23; matrix products, arithmetic and copies ran while one was open for 13% -> 7% of each run, Pallas kernels for 23% -> 28%
where the time goes in v4:
time: 587 us; the launch traced here: 579 us
  waiting for transfers between devices  268 us (46%)
  Pallas kernels  163 us (28%)
  starting transfers between devices  80.6 us (14%)
  other arithmetic  28.2 us (5%)
  between operations  16.6 us (3%)
  local copies, waits for them, and re-layouts  12.6 us (2%)
  matrix products  9.39 us (2%)
    ppermute x37, waiting for transfers between devices, flipped(): return lax.ppermute(x, axis, [(i, i ^ bit) for i in sends])  168 us
    ppermute x37, starting transfers between devices, flipped(): return lax.ppermute(x, axis, [(i, i ^ bit) for i in sends])  59.5 us
    all_gather x2, waiting for transfers between devices, gather(): return lax.all_gather(x, 'head', axis=0, tiled=True)  52.7 us
    ppermute x6, waiting for transfers between devices, ring(): lax.ppermute(down, axis, [(i, i - 1) for i in range(1, count - k + 1)])  46.4 us
    pallas_call x1, Pallas kernels, feed_forward(): pl.pallas_call(functools.partial(ff_kernel, count), grid_spec=grid_spec,...  25.5 us
    pallas_call x2, Pallas kernels, widened(): pl.pallas_call(widen_kernel, grid=(rows // min(512, rows),), out_shape=ja...  19.1 us
    pallas_call x1, Pallas kernels, feed_forward_sums(): pl.pallas_call(ff_sums_kernel, grid=(width // block,), out_shape=(jax.Sha...  15.2 us
    pallas_call x1, Pallas kernels, attend_back(): pl.pallas_call(functools.partial(attend_back_kernel, scale, scale * log2e...  15 us
  transfers between devices with their start and end apart: 56, of which 23 were waited for; matrix products, arithmetic and copies ran while one was open for 7% of the time, Pallas kernels for 28%

profile of v4, /device:TPU:0, one launch (start us, length us, event | category | flops | bytes accessed | tf_op | source)
XLA Modules:
  0.0 578.5 jit_solution(11706975194794273039)
XLA Ops:
  9.5 5.6 collective-permute-start.6
  17.0 10.4 %mix_forward.1 = (bf16[128,2048]{1,0:T(8,128)(2,1)}, bf16[128,4096]{1,0:T(8,128)(2,1)}, bf16[128,2048]{1,0:T(8,128)(2,1)}, f32[4,128,2048]{2,1,0:T(8,128)}, f32[128,36]{1,0:T(8,128)}, /*index=5*/f32[128,40]{1,0:T(8,128)}) custom-call(bf16[9,128,2048]{2,1,0:T(8,128)(2,1)} %hist.3, f32[4,2048]{1,0:T(4,128)} %gains.3, bf16[2048,40]{1,0:T(8,128)(2,1)} %copy.45.mix_in, ...), custom_call_target="tpu_custom_call" | custom-call | tf_op jit(solution)/shard_map/mix_forward/pallas_call | solution.py:104
  35.4 9.0 %collective-permute-done.3.refs_4_ = bf16[128,2048]{1,0:T(8,128)(2,1)S(1)} collective-permute-done((bf16[128,2048]{1,0:T(8,128)(2,1)}, bf16[128,2048]{1,0:T(8,128)(2,1)S(1)}, u32[]{:S(2)}, u32[]{:S(2)}) %collective-permute-start.3) | collective-permute-done | bytes 524320 | tf_op jit(solution)/shard_map/ppermute | solution.py:893
  46.4 9.2 %collective-permute-done.10.refs_12_.refs_11_ = bf16[128,2048]{1,0:T(8,128)(2,1)S(1)} collective-permute-done((bf16[128,2048]{1,0:T(8,128)(2,1)S(1)}, bf16[128,2048]{1,0:T(8,128)(2,1)S(1)}, u32[]{:S(2)}, u32[]{:S(2)}) %collective-permute-start.10) | collective-permute-done | bytes 524320 | tf_op jit(solution)/shard_map/ppermute | solution.py:893
  57.7 9.2 %collective-permute-done.4.refs_5_ = bf16[128,2048]{1,0:T(8,128)(2,1)S(1)} collective-permute-done((bf16[128,2048]{1,0:T(8,128)(2,1)S(1)}, bf16[128,2048]{1,0:T(8,128)(2,1)S(1)}, u32[]{:S(2)}, u32[]{:S(2)}) %collective-permute-start.4) | collective-permute-done | bytes 524320 | tf_op jit(solution)/shard_map/ppermute | solution.py:893
  68.9 9.2 %collective-permute-done.11.refs_13_.refs_12_ = bf16[128,2048]{1,0:T(8,128)(2,1)S(1)} collective-permute-done((bf16[128,2048]{1,0:T(8,128)(2,1)S(1)}, bf16[128,2048]{1,0:T(8,128)(2,1)S(1)}, u32[]{:S(2)}, u32[]{:S(2)}) %collective-permute-start.11) | collective-permute-done | bytes 524320 | tf_op jit(solution)/shard_map/ppermute | solution.py:893
  78.1 9.7 %collective-permute-done.5.refs_6_ = bf16[128,2048]{1,0:T(8,128)(2,1)S(1)} collective-permute-done((bf16[128,2048]{1,0:T(8,128)(2,1)S(1)}, bf16[128,2048]{1,0:T(8,128)(2,1)S(1)}, u32[]{:S(2)}, u32[]{:S(2)}) %collective-permute-start.5) | collective-permute-done | bytes 524320 | tf_op jit(solution)/shard_map/ppermute | solution.py:893
  90.3 25.5 %feed_forward.1 = (bf16[512,2048]{1,0:T(8,128)(2,1)}, bf16[512,2048]{1,0:T(8,128)(2,1)}, bf16[2048,2048]{1,0:T(8,128)(2,1)}, bf16[2048,2048]{1,0:T(8,128)(2,1)}, bf16[512,2048]{1,0:T(8,128)(2,1)}) custom-call(s32[1]{0:T(128)} %bitcast.2.rank_ref, bf16[128,2048]{1,0:T(8,128)(2,1)} %get-tuple-element.57.refs_0_, bf16[128,2048]{1,0:T(8,128)(2,1)} %copy-done.22, ...), custom_call_target="tpu_custom_call" | custom-call | flops 1048576 | bytes 1048576 | tf_op jit(solution)/shard_map/feed_forward/pallas_call | solution.py:313
  120.5 52.7 %all-gather.5.cloned.1.call-done.n.nk.nv = bf16[512,4096]{1,0:T(8,128)(2,1)} async-done(((bf16[128,4096]{1,0:T(8,128)(2,1)}), bf16[512,4096]{1,0:T(8,128)(2,1)}) %all-gather.5.cloned.1.call-update) | async-done | bytes 4194320 | tf_op jit(solution)/shard_map/all_gather | solution.py:946
  173.2 6.5 %project_kv.1 = (bf16[512,512]{1,0:T(8,128)(2,1)}, bf16[512,512]{1,0:T(8,128)(2,1)}) custom-call(bf16[512,4096]{1,0:T(8,128)(2,1)} %all-gather.5.cloned.1.call-done.n.nk.nv, bf16[2048,512]{1,0:T(8,128)(2,1)} %refs_8_.1, bf16[2048,512]{1,0:T(8,128)(2,1)} %refs_9_.1, f32[512,128]{1,0:T(8,128)} %after.11.same, f32[512,128]{1,0:T(8,128)} %concatenate.27.down.refs_10_.refs_11_, ...), custom_call_target="tpu_custom_call" | custom-call | flops 1048576 | bytes 1048576 | tf_op jit(solution)/shard_map/project_kv/pallas_call | solution.py:386
  187.4 15.9 %collective-permute-done.15.refs_6_.refs_18_ = bf16[512,512]{1,0:T(8,128)(2,1)S(1)} collective-permute-done((bf16[512,512]{1,0:T(8,128)(2,1)}, bf16[512,512]{1,0:T(8,128)(2,1)S(1)}, u32[]{:S(2)}, u32[]{:S(2)}) %collective-permute-start.15) | collective-permute-done | bytes 524320 | tf_op jit(solution)/shard_map/ppermute | solution.py:756
  210.1 5.7 collective-permute-done.22.refs_14_.refs_26_
  219.4 18.5 %collective-permute-done.17.refs_7_.refs_19_ = bf16[512,512]{1,0:T(8,128)(2,1)} collective-permute-done((bf16[512,512]{1,0:T(8,128)(2,1)S(1)}, bf16[512,512]{1,0:T(8,128)(2,1)}, u32[]{:S(2)}, u32[]{:S(2)}) %collective-permute-start.17) | collective-permute-done | bytes 524320 | tf_op jit(solution)/shard_map/ppermute | solution.py:756
  252.6 8.2 %attend.1 = (bf16[512,512]{1,0:T(8,128)(2,1)}, f32[8,512]{1,0:T(8,128)}) custom-call(s32[2]{0:T(128)} %pad_add_fusion.info.refs_0_, s32[8]{0:T(128)} %broadcast_xor_fusion.offsets.refs_1_, bf16[512,512]{1,0:T(8,128)(2,1)} %project_q.1.q.refs_4_, s32[8,512]{1,0:T(8,128)} %after.9.span, bf16[512,512]{1,0:T(8,128)(2,1)} %collective-permute-done.12.refs_0_.refs_12_, ...), custom_call_target="tpu_custom_call" | custom-call | flops 1048576 | bytes 1048576 | tf_op jit(solution)/shard_map/attend/pallas_call | solution.py:502
  260.8 15.0 %attend_back.1 = (bf16[512,512]{1,0:T(8,128)(2,1)}, bf16[2048,512]{1,0:T(8,128)(2,1)}, bf16[2048,512]{1,0:T(8,128)(2,1)}, bf16[2048,512]{1,0:T(8,128)(2,1)}, bf16[2048,512]{1,0:T(8,128)(2,1)}) custom-call(s32[2]{0:T(128)} %pad_add_fusion.info.refs_0_, s32[8]{0:T(128)} %broadcast_xor_fusion.offsets.refs_1_, s32[8]{0:T(128)} %constant.81.clone.refs_2_, ...), custom_call_target="tpu_custom_call" | custom-call | flops 1048576 | bytes 1048576 | tf_op jit(solution)/shard_map/attend_back/pallas_call | solution.py:610
  280.4 6.0 %collective-permute-start.26 = (bf16[2048,512]{1,0:T(8,128)(2,1)}, bf16[2048,512]{1,0:T(8,128)(2,1)}, u32[]{:S(2)}, u32[]{:S(2)}) collective-permute-start(bf16[2048,512]{1,0:T(8,128)(2,1)} %get-tuple-element.71), channel_id=1, source_target_pairs={{0,4},{4,0},{8,12},{12,8},{16,20},{20,16},{24,28},{28,24},{1,5},{5... | collective-permute-start | bytes 6291464 | tf_op jit(solution)/shard_map/ppermute | solution.py:756
  286.5 15.2 %feed_forward_sums.1 = (f32[512,2048]{1,0:T(8,128)}, bf16[512,2048]{1,0:T(8,128)(2,1)}) custom-call(bf16[512,2048]{1,0:T(8,128)(2,1)} %after.12.act, bf16[512,2048]{1,0:T(8,128)(2,1)} %get-tuple-element.67.grad, bf16[2048,2048]{1,0:T(8,128)(2,1)} %w_up.1, bf16[2048,2048]{1,0:T(8,128)(2,1)} %w_down.1), custom_call_target="tpu_custom_call" | custom-call | flops 1048576 | bytes 1048576 | tf_op jit(solution)/shard_map/feed_forward_sums/pallas_call | solution.py:340
  306.8 11.4 %collective-permute-start.30 = (bf16[1024,512]{1,0:T(8,128)(2,1)S(1)}, bf16[1024,512]{1,0:T(8,128)(2,1)S(1)}, u32[]{:S(2)}, u32[]{:S(2)}) collective-permute-start(bf16[1024,512]{1,0:T(8,128)(2,1)S(1)} %add_convert_fusion.1), channel_id=1, source_target_pairs={{0,8},{4,12},{8,0},{12,4},{16,24},{20,28},{24,16},{28,20},{1,9},{5... | collective-permute-start | bytes 3145736 | tf_op jit(solution)/shard_map/ppermute | solution.py:756
  319.5 54.2 %collective-permute-done.27.refs_2_ = bf16[1024,512]{1,0:T(8,128)(2,1)S(1)} collective-permute-done((bf16[1024,512]{1,0:T(8,128)(2,1)S(1)}, bf16[1024,512]{1,0:T(8,128)(2,1)S(1)}, u32[]{:S(2)}, u32[]{:S(2)}) %collective-permute-start.27) | collective-permute-done | bytes 1048608 | tf_op jit(solution)/shard_map/ppermute | solution.py:756
  375.5 10.9 %collective-permute-start.28 = (bf16[512,512]{1,0:T(8,128)(2,1)S(1)}, bf16[512,512]{1,0:T(8,128)(2,1)S(1)}, u32[]{:S(2)}, u32[]{:S(2)}) collective-permute-start(bf16[512,512]{1,0:T(8,128)(2,1)S(1)} %add_convert_fusion.6), channel_id=1, source_target_pairs={{0,8},{4,12},{8,0},{12,4},{16,24},{20,28},{24,16},{28,20},{1,9},{5... | collective-permute-start | bytes 1572872 | tf_op jit(solution)/shard_map/ppermute | solution.py:756
  391.3 7.1 %collective-permute-done.28.refs_3_ = bf16[512,512]{1,0:T(8,128)(2,1)S(1)} collective-permute-done((bf16[512,512]{1,0:T(8,128)(2,1)S(1)}, bf16[512,512]{1,0:T(8,128)(2,1)S(1)}, u32[]{:S(2)}, u32[]{:S(2)}) %collective-permute-start.28) | collective-permute-done | bytes 524320 | tf_op jit(solution)/shard_map/ppermute | solution.py:756
  404.2 7.7 %key_value_back.1 = (bf16[512,512]{1,0:T(8,128)(2,1)}, bf16[512,512]{1,0:T(8,128)(2,1)}, bf16[512,4096]{1,0:T(8,128)(2,1)}) custom-call(bf16[2048,512]{1,0:T(8,128)(2,1)} %get-tuple-element.70.refs_0_, bf16[2048,512]{1,0:T(8,128)(2,1)} %collective-permute-done.26.refs_1_, bf16[1024,512]{1,0:T(8,128)(2,1)} %copy-done.9, bf16[512,512]{1,0:T(8,128)(2,1)} %copy-done.35, ...), custom_call_target="tpu_custom_call" | custom-call | flops 1048576 | bytes 1048576 | tf_op jit(solution)/shard_map/key_value_back/pallas_call | solution.py:638
  412.0 12.3 %weight_grads.1 = (bf16[1024,1024]{1,0:T(8,128)(2,1)}, bf16[1024,1024]{1,0:T(8,128)(2,1)}, bf16[1024,1024]{1,0:T(8,128)(2,1)}, bf16[1024,1024]{1,0:T(8,128)(2,1)}) custom-call(s32[1]{0:T(128)} %bitcast.10.core, bf16[512,2048]{1,0:T(8,128)(2,1)} %all-gather.3.cloned.1.call-done.n.nq, bf16[512,4096]{1,0:T(8,128)(2,1)} %all-gather.5.cloned.1.call-done.n.nk.nv, ...), custom_call_target="tpu_custom_call" | custom-call | flops 1048576 | bytes 1048576 | tf_op jit(solution)/shard_map/weight_grads/pallas_call | solution.py:691
  425.5 5.5 collective-permute-done.37.refs_1_
  432.3 6.7 %merge.2 = (bf16[512,1024]{1,0:T(8,128)(2,1)}, bf16[512,1024]{1,0:T(8,128)(2,1)}, bf16[512,1024]{1,0:T(8,128)(2,1)}, bf16[512,1024]{1,0:T(8,128)(2,1)}) custom-call(s32[2]{0:T(128)} %pad_add_fusion.2.sides, bf16[1024,1024]{1,0:T(8,128)(2,1)} %get-tuple-element.83.refs_0_, bf16[1024,1024]{1,0:T(8,128)(2,1)} %copy-done.15, ...), custom_call_target="tpu_custom_call" | custom-call | flops 1048576 | bytes 1048576 | tf_op jit(solution)/shard_map/merge/pallas_call | solution.py:830
  440.0 9.5 %widen.3.refs_1_ = f32[2048,2048]{1,0:T(8,128)} custom-call(bf16[2048,2048]{1,0:T(8,128)(2,1)} %get-tuple-element.100.refs_1_.x), custom_call_target="tpu_custom_call" | custom-call | tf_op jit(solution)/shard_map/widen/pallas_call | solution.py:854
  449.5 14.9 %collective-permute-done.39.refs_1_ = bf16[512,1024]{1,0:T(8,128)(2,1)S(1)} collective-permute-done((bf16[512,1024]{1,0:T(8,128)(2,1)}, bf16[512,1024]{1,0:T(8,128)(2,1)S(1)}, u32[]{:S(2)}, u32[]{:S(2)}) %collective-permute-start.39) | collective-permute-done | bytes 1048608 | tf_op jit(solution)/shard_map/ppermute | solution.py:756
  472.7 11.7 %collective-permute-done.41 = bf16[256,1024]{1,0:T(8,128)(2,1)S(1)} collective-permute-done((bf16[256,1024]{1,0:T(8,128)(2,1)}, bf16[256,1024]{1,0:T(8,128)(2,1)S(1)}, u32[]{:S(2)}, u32[]{:S(2)}) %collective-permute-start.41) | collective-permute-done | bytes 524320 | tf_op jit(solution)/shard_map/ppermute | solution.py:756
  488.0 14.4 %unmix.1 = (bf16[9,128,2048]{2,1,0:T(8,128)(2,1)}, f32[48,2176]{1,0:T(8,128)}) custom-call(bf16[9,128,2048]{2,1,0:T(8,128)(2,1)} %hist.3, f32[4,128,2048]{2,1,0:T(8,128)} %get-tuple-element.56.streams, bf16[128,2048]{1,0:T(8,128)(2,1)} %reduce-scatter.7.cloned.1.call-done.gn3, bf16[128,4096]{1,0:T(8,128)(2,1)} %reduce-scatter.9.cloned.1.call-done.gnkv, ...), custom_call_target="tpu_custom_call" | custom-call | tf_op jit(solution)/shard_map/unmix/pallas_call | solution.py:206
  509.8 9.6 %widen.2.refs_1_ = f32[2048,2048]{1,0:T(8,128)} custom-call(bf16[2048,2048]{1,0:T(8,128)(2,1)} %get-tuple-element.99.x.refs_2_), custom_call_target="tpu_custom_call" | custom-call | tf_op jit(solution)/shard_map/widen/pallas_call | solution.py:854
  519.4 15.5 %collective-permute-done.33 = bf16[48,2176]{1,0:T(8,128)(2,1)S(1)} collective-permute-done((bf16[48,2176]{1,0:T(8,128)(2,1)S(1)}, bf16[48,2176]{1,0:T(8,128)(2,1)S(1)}, u32[]{:S(2)}, u32[]{:S(2)}) %collective-permute-start.33) | collective-permute-done | bytes 208928 | tf_op jit(solution)/shard_map/ppermute | solution.py:756
  556.3 12.0 %assemble.1 = (f32[2048,512]{1,0:T(8,128)}, f32[2048,512]{1,0:T(8,128)}, f32[2048,512]{1,0:T(8,128)}, f32[512,2048]{1,0:T(8,128)}) custom-call(s32[8]{0:T(128)} %and_select_fusion.1.a_slot, s32[8]{0:T(128)} %and_select_fusion.b_slot, bf16[1024,1024]{1,0:T(8,128)(2,1)} %pad_maximum_fusion.a_lo, bf16[1024,1024]{1,0:T(8,128)(2,1)} %collective-permute-done.44.a_hi, ...), custom_call_target="tpu_custom_call" | custom-call | tf_op jit(solution)/shard_map/assemble/pallas_call | solution.py:744
  (249 shorter events, 126.9 us)
Async XLA Ops:
  8.0 165.2 %all-gather.5.cloned.1.call-start = ((), (), s32[]{:S(2)}) async-start(), calls=%async_computation.5 | async-start | bytes 5242880 | tf_op jit(solution)/shard_map/all_gather | solution.py:946
  8.1 25.3 %collective-permute-start.9 = (bf16[128,2048]{1,0:T(8,128)(2,1)}, bf16[128,2048]{1,0:T(8,128)(2,1)S(1)}, u32[]{:S(2)}, u32[]{:S(2)}) collective-permute-start(bf16[128,2048]{1,0:T(8,128)(2,1)} %cot.1), channel_id=1, source_target_pairs={{1,0},{2,1},{3,2},{5,4},{6,5},{7,6},{9,8},{10,9},{11,10},{13,12},{... | collective-permute-start | bytes 1572872 | tf_op jit(solution)/shard_map/ppermute | solution.py:893
  9.5 25.2 %collective-permute-start.6 = (bf16[128,2048]{1,0:T(8,128)(2,1)}, bf16[128,2048]{1,0:T(8,128)(2,1)S(1)}, u32[]{:S(2)}, u32[]{:S(2)}) collective-permute-start(bf16[128,2048]{1,0:T(8,128)(2,1)} %cot.1), channel_id=1, source_target_pairs={{0,1},{1,2},{2,3},{4,5},{5,6},{6,7},{8,9},{9,10},{10,11},{12,13},{... | collective-permute-start | bytes 1572872 | tf_op jit(solution)/shard_map/ppermute | solution.py:892
  33.4 22.3 %collective-permute-start.10 = (bf16[128,2048]{1,0:T(8,128)(2,1)S(1)}, bf16[128,2048]{1,0:T(8,128)(2,1)S(1)}, u32[]{:S(2)}, u32[]{:S(2)}) collective-permute-start(bf16[128,2048]{1,0:T(8,128)(2,1)S(1)} %collective-permute-done.9.refs_11_.refs_10_), channel_id=1, source_target_pairs={{1,0},{2,1},{5,4},{6,5},{9,8},{10,9},{13,12},{14,13},{17,16},{18,1... | collective-permute-start | bytes 1572872 | tf_op jit(solution)/shard_map/ppermute | solution.py:893
  34.7 22.3 %collective-permute-start.7 = (bf16[128,2048]{1,0:T(8,128)(2,1)S(1)}, bf16[128,2048]{1,0:T(8,128)(2,1)S(1)}, u32[]{:S(2)}, u32[]{:S(2)}) collective-permute-start(bf16[128,2048]{1,0:T(8,128)(2,1)S(1)} %collective-permute-done.6.refs_8_.refs_7_), channel_id=1, source_target_pairs={{1,2},{2,3},{5,6},{6,7},{9,10},{10,11},{13,14},{14,15},{17,18},{18... | collective-permute-start | bytes 1572872 | tf_op jit(solution)/shard_map/ppermute | solution.py:892
  44.4 22.5 %collective-permute-start.4 = (bf16[128,2048]{1,0:T(8,128)(2,1)S(1)}, bf16[128,2048]{1,0:T(8,128)(2,1)S(1)}, u32[]{:S(2)}, u32[]{:S(2)}) collective-permute-start(bf16[128,2048]{1,0:T(8,128)(2,1)S(1)} %collective-permute-done.3.refs_4_), channel_id=1, source_target_pairs={{1,0},{2,1},{5,4},{6,5},{9,8},{10,9},{13,12},{14,13},{17,16},{18,1... | collective-permute-start | bytes 1572872 | tf_op jit(solution)/shard_map/ppermute | solution.py:893
  45.7 22.5 %collective-permute-start.1 = (bf16[128,2048]{1,0:T(8,128)(2,1)S(1)}, bf16[128,2048]{1,0:T(8,128)(2,1)S(1)}, u32[]{:S(2)}, u32[]{:S(2)}) collective-permute-start(bf16[128,2048]{1,0:T(8,128)(2,1)S(1)} %collective-permute-done.refs_1_), channel_id=1, source_target_pairs={{1,2},{2,3},{5,6},{6,7},{9,10},{10,11},{13,14},{14,15},{17,18},{18... | collective-permute-start | bytes 1572872 | tf_op jit(solution)/shard_map/ppermute | solution.py:892
  55.6 22.5 %collective-permute-start.11 = (bf16[128,2048]{1,0:T(8,128)(2,1)S(1)}, bf16[128,2048]{1,0:T(8,128)(2,1)S(1)}, u32[]{:S(2)}, u32[]{:S(2)}) collective-permute-start(bf16[128,2048]{1,0:T(8,128)(2,1)S(1)} %collective-permute-done.10.refs_12_.refs_11_), channel_id=1, source_target_pairs={{1,0},{5,4},{9,8},{13,12},{17,16},{21,20},{25,24},{29,28}} | collective-permute-start | bytes 1572872 | tf_op jit(solution)/shard_map/ppermute | solution.py:893
  89.5 158.1 %all-gather.3.cloned.1.call-start = ((), (), s32[]{:S(2)}) async-start(), calls=%async_computation.4 | async-start | bytes 2621440 | tf_op jit(solution)/shard_map/all_gather | solution.py:946
  90.3 321.8 %all-reduce.4.cloned.1.call-start = ((), (), s32[]{:S(2)}) async-start(), calls=%async_computation.10 | async-start | bytes 33554432 | tf_op jit(solution)/shard_map/psum | solution.py:978
  115.8 372.1 %reduce-scatter.11.cloned.1.call-start = ((), (), s32[]{:S(2)}) async-start(), calls=%async_computation.9 | async-start | bytes 2621440 | tf_op jit(solution)/shard_map/reduce_scatter | solution.py:949
  179.7 23.6 %collective-permute-start.15 = (bf16[512,512]{1,0:T(8,128)(2,1)}, bf16[512,512]{1,0:T(8,128)(2,1)S(1)}, u32[]{:S(2)}, u32[]{:S(2)}) collective-permute-start(bf16[512,512]{1,0:T(8,128)(2,1)} %get-tuple-element.62.refs_4_.refs_16_), channel_id=1, source_target_pairs={{0,16},{4,20},{8,24},{12,28},{1,17},{5,21},{9,25},{13,29},{2,18},{... | collective-permute-start | bytes 1572872 | tf_op jit(solution)/shard_map/ppermute | solution.py:756
  183.1 22.7 %collective-permute-start.13 = (bf16[512,512]{1,0:T(8,128)(2,1)}, bf16[512,512]{1,0:T(8,128)(2,1)S(1)}, u32[]{:S(2)}, u32[]{:S(2)}) collective-permute-start(bf16[512,512]{1,0:T(8,128)(2,1)} %get-tuple-element.62.refs_4_.refs_16_), channel_id=1, source_target_pairs={{0,8},{4,12},{8,0},{12,4},{16,24},{20,28},{24,16},{28,20},{1,9},{5... | collective-permute-start | bytes 1572872 | tf_op jit(solution)/shard_map/ppermute | solution.py:756
  184.6 31.2 %collective-permute-start.22 = (bf16[512,512]{1,0:T(8,128)(2,1)}, bf16[512,512]{1,0:T(8,128)(2,1)}, u32[]{:S(2)}, u32[]{:S(2)}) collective-permute-start(bf16[512,512]{1,0:T(8,128)(2,1)} %get-tuple-element.63.refs_12_.refs_24_), channel_id=1, source_target_pairs={{0,16},{4,20},{8,24},{12,28},{1,17},{5,21},{9,25},{13,29},{2,18},{... | collective-permute-start | bytes 1572872 | tf_op jit(solution)/shard_map/ppermute | solution.py:756
  186.8 32.0 %collective-permute-start.20 = (bf16[512,512]{1,0:T(8,128)(2,1)}, bf16[512,512]{1,0:T(8,128)(2,1)}, u32[]{:S(2)}, u32[]{:S(2)}) collective-permute-start(bf16[512,512]{1,0:T(8,128)(2,1)} %get-tuple-element.63.refs_12_.refs_24_), channel_id=1, source_target_pairs={{0,8},{4,12},{8,0},{12,4},{16,24},{20,28},{24,16},{28,20},{1,9},{5... | collective-permute-start | bytes 1572872 | tf_op jit(solution)/shard_map/ppermute | solution.py:756
  205.9 32.0 %collective-permute-start.17 = (bf16[512,512]{1,0:T(8,128)(2,1)S(1)}, bf16[512,512]{1,0:T(8,128)(2,1)}, u32[]{:S(2)}, u32[]{:S(2)}) collective-permute-start(bf16[512,512]{1,0:T(8,128)(2,1)S(1)} %collective-permute-done.13.refs_5_.refs_17_), channel_id=1, source_target_pairs={{0,16},{4,20},{8,24},{12,28},{1,17},{5,21},{9,25},{13,29},{2,18},{... | collective-permute-start | bytes 1572872 | tf_op jit(solution)/shard_map/ppermute | solution.py:756
  215.8 25.7 %collective-permute-start.24 = (bf16[512,512]{1,0:T(8,128)(2,1)}, bf16[512,512]{1,0:T(8,128)(2,1)}, u32[]{:S(2)}, u32[]{:S(2)}) collective-permute-start(bf16[512,512]{1,0:T(8,128)(2,1)} %collective-permute-done.22.refs_14_.refs_26_), channel_id=1, source_target_pairs={{0,8},{4,12},{8,0},{12,4},{16,24},{20,28},{24,16},{28,20},{1,9},{5... | collective-permute-start | bytes 1572872 | tf_op jit(solution)/shard_map/ppermute | solution.py:756
  218.8 33.8 %collective-permute-start.14 = (bf16[512,512]{1,0:T(8,128)(2,1)S(1)}, bf16[512,512]{1,0:T(8,128)(2,1)}, u32[]{:S(2)}, u32[]{:S(2)}) collective-permute-start(bf16[512,512]{1,0:T(8,128)(2,1)S(1)} %collective-permute-done.13.refs_5_.refs_17_), channel_id=1, source_target_pairs={{0,4},{4,0},{8,12},{12,8},{16,20},{20,16},{24,28},{28,24},{1,5},{5... | collective-permute-start | bytes 1572872 | tf_op jit(solution)/shard_map/ppermute | solution.py:756
  218.8 33.8 %collective-permute-start.23 = (bf16[512,512]{1,0:T(8,128)(2,1)}, bf16[512,512]{1,0:T(8,128)(2,1)}, u32[]{:S(2)}, u32[]{:S(2)}) collective-permute-start(bf16[512,512]{1,0:T(8,128)(2,1)} %collective-permute-done.22.refs_14_.refs_26_), channel_id=1, source_target_pairs={{0,4},{4,0},{8,12},{12,8},{16,20},{20,16},{24,28},{28,24},{1,5},{5... | collective-permute-start | bytes 1572872 | tf_op jit(solution)/shard_map/ppermute | solution.py:756
  219.3 33.3 %collective-permute-start.21 = (bf16[512,512]{1,0:T(8,128)(2,1)}, bf16[512,512]{1,0:T(8,128)(2,1)}, u32[]{:S(2)}, u32[]{:S(2)}) collective-permute-start(bf16[512,512]{1,0:T(8,128)(2,1)} %collective-permute-done.20.refs_13_.refs_25_), channel_id=1, source_target_pairs={{0,4},{4,0},{8,12},{12,8},{16,20},{20,16},{24,28},{28,24},{1,5},{5... | collective-permute-start | bytes 1572872 | tf_op jit(solution)/shard_map/ppermute | solution.py:756
  280.4 207.6 %reduce-scatter.7.cloned.1.call-start = ((), (), s32[]{:S(2)}) async-start(), calls=%async_computation.7 | async-start | bytes 2621440 | tf_op jit(solution)/shard_map/reduce_scatter | solution.py:949
  280.4 21.4 %collective-permute-start.26 = (bf16[2048,512]{1,0:T(8,128)(2,1)}, bf16[2048,512]{1,0:T(8,128)(2,1)}, u32[]{:S(2)}, u32[]{:S(2)}) collective-permute-start(bf16[2048,512]{1,0:T(8,128)(2,1)} %get-tuple-element.71), channel_id=1, source_target_pairs={{0,4},{4,0},{8,12},{12,8},{16,20},{20,16},{24,28},{28,24},{1,5},{5... | collective-permute-start | bytes 6291464 | tf_op jit(solution)/shard_map/ppermute | solution.py:756
  301.7 186.3 %reduce-scatter.9.cloned.1.call-start = ((), (), s32[]{:S(2)}) async-start(), calls=%async_computation.8 | async-start | bytes 5242880 | tf_op jit(solution)/shard_map/reduce_scatter | solution.py:949
  303.8 69.9 %collective-permute-start.27 = (bf16[1024,512]{1,0:T(8,128)(2,1)S(1)}, bf16[1024,512]{1,0:T(8,128)(2,1)S(1)}, u32[]{:S(2)}, u32[]{:S(2)}) collective-permute-start(bf16[1024,512]{1,0:T(8,128)(2,1)S(1)} %add_convert_fusion.2), channel_id=1, source_target_pairs={{16,0},{20,4},{24,8},{28,12},{17,1},{21,5},{25,9},{29,13},{18,2},{... | collective-permute-start | bytes 3145736 | tf_op jit(solution)/shard_map/ppermute | solution.py:756
  306.8 79.6 %collective-permute-start.30 = (bf16[1024,512]{1,0:T(8,128)(2,1)S(1)}, bf16[1024,512]{1,0:T(8,128)(2,1)S(1)}, u32[]{:S(2)}, u32[]{:S(2)}) collective-permute-start(bf16[1024,512]{1,0:T(8,128)(2,1)S(1)} %add_convert_fusion.1), channel_id=1, source_target_pairs={{0,8},{4,12},{8,0},{12,4},{16,24},{20,28},{24,16},{28,20},{1,9},{5... | collective-permute-start | bytes 3145736 | tf_op jit(solution)/shard_map/ppermute | solution.py:756
  375.5 22.9 %collective-permute-start.28 = (bf16[512,512]{1,0:T(8,128)(2,1)S(1)}, bf16[512,512]{1,0:T(8,128)(2,1)S(1)}, u32[]{:S(2)}, u32[]{:S(2)}) collective-permute-start(bf16[512,512]{1,0:T(8,128)(2,1)S(1)} %add_convert_fusion.6), channel_id=1, source_target_pairs={{0,8},{4,12},{8,0},{12,4},{16,24},{20,28},{24,16},{28,20},{1,9},{5... | collective-permute-start | bytes 1572872 | tf_op jit(solution)/shard_map/ppermute | solution.py:756
  411.9 142.1 %reduce-scatter.5.cloned.1.call-start = ((), (), s32[]{:S(2)}) async-start(), calls=%async_computation.6 | async-start | bytes 2621440 | tf_op jit(solution)/shard_map/reduce_scatter | solution.py:949
  439.0 25.4 %collective-permute-start.39 = (bf16[512,1024]{1,0:T(8,128)(2,1)}, bf16[512,1024]{1,0:T(8,128)(2,1)S(1)}, u32[]{:S(2)}, u32[]{:S(2)}) collective-permute-start(bf16[512,1024]{1,0:T(8,128)(2,1)} %get-tuple-element.88), channel_id=1, source_target_pairs={{0,8},{4,12},{8,0},{12,4},{16,24},{20,28},{24,16},{28,20},{1,9},{5... | collective-permute-start | bytes 3145736 | tf_op jit(solution)/shard_map/ppermute | solution.py:756
  439.4 25.1 %collective-permute-start.40 = (bf16[512,1024]{1,0:T(8,128)(2,1)}, bf16[512,1024]{1,0:T(8,128)(2,1)S(1)}, u32[]{:S(2)}, u32[]{:S(2)}) collective-permute-start(bf16[512,1024]{1,0:T(8,128)(2,1)} %get-tuple-element.90), channel_id=1, source_target_pairs={{0,16},{4,20},{8,24},{12,28},{16,0},{20,4},{24,8},{28,12},{1,17},{... | collective-permute-start | bytes 3145736 | tf_op jit(solution)/shard_map/ppermute | solution.py:756
  504.6 33.5 %collective-permute-start.43 = (bf16[512,1024]{1,0:T(8,128)(2,1)}, bf16[512,1024]{1,0:T(8,128)(2,1)}, u32[]{:S(2)}, u32[]{:S(2)}) collective-permute-start(bf16[512,1024]{1,0:T(8,128)(2,1)} %pad_maximum_fusion.2), channel_id=1, source_target_pairs={{0,8},{4,12},{8,0},{12,4},{16,24},{20,28},{24,16},{28,20},{1,9},{5... | collective-permute-start | bytes 3145736 | tf_op jit(solution)/shard_map/ppermute | solution.py:756
  507.1 29.3 %collective-permute-start.47 = (bf16[512,1024]{1,0:T(8,128)(2,1)}, bf16[512,1024]{1,0:T(8,128)(2,1)}, u32[]{:S(2)}, u32[]{:S(2)}) collective-permute-start(bf16[512,1024]{1,0:T(8,128)(2,1)} %pad_maximum_fusion.3), channel_id=1, source_target_pairs={{0,16},{4,20},{8,24},{12,28},{16,0},{20,4},{24,8},{28,12},{1,17},{... | collective-permute-start | bytes 3145736 | tf_op jit(solution)/shard_map/ppermute | solution.py:756
  508.7 26.2 %collective-permute-start.33 = (bf16[48,2176]{1,0:T(8,128)(2,1)S(1)}, bf16[48,2176]{1,0:T(8,128)(2,1)S(1)}, u32[]{:S(2)}, u32[]{:S(2)}) collective-permute-start(bf16[48,2176]{1,0:T(8,128)(2,1)S(1)} %add_convert_fusion.11), channel_id=1, source_target_pairs={{0,8},{4,12},{8,0},{12,4},{16,24},{20,28},{24,16},{28,20},{1,9},{5... | collective-permute-start | bytes 626696 | tf_op jit(solution)/shard_map/ppermute | solution.py:756
  (66 other events, 1338.8 us)
Sparse Core Ops, SparseCore 0:
  89.6 83.5 all-gather.4
  174.8 44.4 all-gather.2
  280.5 80.3 reduce-scatter.10
  363.1 43.1 reduce-scatter.6
  412.1 75.8 reduce-scatter.8
  490.8 44.3 reduce-scatter.4
Sparse Core Ops, SparseCore 1:
  115.9 268.0 all-reduce.3

commit v5 on v4

--- a/solution.py
+++ b/solution.py
@@ -102,7 +102,7 @@
     hist_count, rows, width = histories.shape
     count = norm_gains.shape[0]
     return pl.pallas_call(
-        functools.partial(mix_kernel, 16),
+        functools.partial(mix_kernel, min(32, rows)),
         out_shape=(
             jax.ShapeDtypeStruct((rows, width), bf16),
             jax.ShapeDtypeStruct((rows, 2 * width), bf16),
@@ -913,7 +913,8 @@
     for axis in ("seq", "head"):
         if axis == "head":
             x = after(x, midway)
-        for bit in bits_of(lax.axis_size(axis)):
+        bits = bits_of(lax.axis_size(axis))
+        for bit in bits[1:] + bits[:1]:
             x = summed(x, flipped(x, axis, bit))
     return x.astype(f32)
 

time: 587 us -> 590 us (level)
  no operation moved by 1% of the time
where the time goes in v5:
time: 590 us; the launch traced here: 581 us
  waiting for transfers between devices  272 us (46%)
  Pallas kernels  162 us (27%)
  starting transfers between devices  79.9 us (14%)
  other arithmetic  27.9 us (5%)
  between operations  16.5 us (3%)
  local copies, waits for them, and re-layouts  12.6 us (2%)
  matrix products  9.39 us (2%)
    ppermute x37, waiting for transfers between devices, flipped(): return lax.ppermute(x, axis, [(i, i ^ bit) for i in sends])  172 us
    ppermute x37, starting transfers between devices, flipped(): return lax.ppermute(x, axis, [(i, i ^ bit) for i in sends])  58.8 us
    all_gather x2, waiting for transfers between devices, gather(): return lax.all_gather(x, 'head', axis=0, tiled=True)  52.7 us
    ppermute x6, waiting for transfers between devices, ring(): lax.ppermute(down, axis, [(i, i - 1) for i in range(1, count - k + 1)])  46.4 us
    pallas_call x1, Pallas kernels, feed_forward(): pl.pallas_call(functools.partial(ff_kernel, count), grid_spec=grid_spec,...  25.5 us
    pallas_call x2, Pallas kernels, widened(): pl.pallas_call(widen_kernel, grid=(rows // min(512, rows),), out_shape=ja...  19.1 us
    pallas_call x1, Pallas kernels, feed_forward_sums(): pl.pallas_call(ff_sums_kernel, grid=(width // block,), out_shape=(jax.Sha...  15.2 us
    pallas_call x1, Pallas kernels, attend_back(): pl.pallas_call(functools.partial(attend_back_kernel, scale, scale * log2e...  15.1 us
  transfers between devices with their start and end apart: 56, of which 23 were waited for; matrix products, arithmetic and copies ran while one was open for 7% of the time, Pallas kernels for 28%

profile of v5, /device:TPU:0, one launch (start us, length us, event | category | flops | bytes accessed | tf_op | source)
XLA Modules:
  0.0 581.1 jit_solution(12525517146816779170)
XLA Ops:
  9.5 5.6 collective-permute-start.6
  17.0 9.7 %mix_forward.1 = (bf16[128,2048]{1,0:T(8,128)(2,1)}, bf16[128,4096]{1,0:T(8,128)(2,1)}, bf16[128,2048]{1,0:T(8,128)(2,1)}, f32[4,128,2048]{2,1,0:T(8,128)}, f32[128,36]{1,0:T(8,128)}, /*index=5*/f32[128,40]{1,0:T(8,128)}) custom-call(bf16[9,128,2048]{2,1,0:T(8,128)(2,1)} %hist.3, f32[4,2048]{1,0:T(4,128)} %gains.3, bf16[2048,40]{1,0:T(8,128)(2,1)} %copy.45.mix_in, ...), custom_call_target="tpu_custom_call" | custom-call | tf_op jit(solution)/shard_map/mix_forward/pallas_call | solution.py:104
  34.6 9.0 %collective-permute-done.3.refs_4_ = bf16[128,2048]{1,0:T(8,128)(2,1)S(1)} collective-permute-done((bf16[128,2048]{1,0:T(8,128)(2,1)}, bf16[128,2048]{1,0:T(8,128)(2,1)S(1)}, u32[]{:S(2)}, u32[]{:S(2)}) %collective-permute-start.3) | collective-permute-done | bytes 524320 | tf_op jit(solution)/shard_map/ppermute | solution.py:893
  45.7 9.2 %collective-permute-done.10.refs_12_.refs_11_ = bf16[128,2048]{1,0:T(8,128)(2,1)S(1)} collective-permute-done((bf16[128,2048]{1,0:T(8,128)(2,1)S(1)}, bf16[128,2048]{1,0:T(8,128)(2,1)S(1)}, u32[]{:S(2)}, u32[]{:S(2)}) %collective-permute-start.10) | collective-permute-done | bytes 524320 | tf_op jit(solution)/shard_map/ppermute | solution.py:893
  56.9 9.2 %collective-permute-done.4.refs_5_ = bf16[128,2048]{1,0:T(8,128)(2,1)S(1)} collective-permute-done((bf16[128,2048]{1,0:T(8,128)(2,1)S(1)}, bf16[128,2048]{1,0:T(8,128)(2,1)S(1)}, u32[]{:S(2)}, u32[]{:S(2)}) %collective-permute-start.4) | collective-permute-done | bytes 524320 | tf_op jit(solution)/shard_map/ppermute | solution.py:893
  68.2 9.2 %collective-permute-done.11.refs_13_.refs_12_ = bf16[128,2048]{1,0:T(8,128)(2,1)S(1)} collective-permute-done((bf16[128,2048]{1,0:T(8,128)(2,1)S(1)}, bf16[128,2048]{1,0:T(8,128)(2,1)S(1)}, u32[]{:S(2)}, u32[]{:S(2)}) %collective-permute-start.11) | collective-permute-done | bytes 524320 | tf_op jit(solution)/shard_map/ppermute | solution.py:893
  77.4 9.7 %collective-permute-done.5.refs_6_ = bf16[128,2048]{1,0:T(8,128)(2,1)S(1)} collective-permute-done((bf16[128,2048]{1,0:T(8,128)(2,1)S(1)}, bf16[128,2048]{1,0:T(8,128)(2,1)S(1)}, u32[]{:S(2)}, u32[]{:S(2)}) %collective-permute-start.5) | collective-permute-done | bytes 524320 | tf_op jit(solution)/shard_map/ppermute | solution.py:893
  89.6 25.5 %feed_forward.1 = (bf16[512,2048]{1,0:T(8,128)(2,1)}, bf16[512,2048]{1,0:T(8,128)(2,1)}, bf16[2048,2048]{1,0:T(8,128)(2,1)}, bf16[2048,2048]{1,0:T(8,128)(2,1)}, bf16[512,2048]{1,0:T(8,128)(2,1)}) custom-call(s32[1]{0:T(128)} %bitcast.2.rank_ref, bf16[128,2048]{1,0:T(8,128)(2,1)} %get-tuple-element.57.refs_0_, bf16[128,2048]{1,0:T(8,128)(2,1)} %copy-done.22, ...), custom_call_target="tpu_custom_call" | custom-call | flops 1048576 | bytes 1048576 | tf_op jit(solution)/shard_map/feed_forward/pallas_call | solution.py:313
  119.8 52.7 %all-gather.5.cloned.1.call-done.n.nk.nv = bf16[512,4096]{1,0:T(8,128)(2,1)} async-done(((bf16[128,4096]{1,0:T(8,128)(2,1)}), bf16[512,4096]{1,0:T(8,128)(2,1)}) %all-gather.5.cloned.1.call-update) | async-done | bytes 4194320 | tf_op jit(solution)/shard_map/all_gather | solution.py:947
  172.5 6.5 %project_kv.1 = (bf16[512,512]{1,0:T(8,128)(2,1)}, bf16[512,512]{1,0:T(8,128)(2,1)}) custom-call(bf16[512,4096]{1,0:T(8,128)(2,1)} %all-gather.5.cloned.1.call-done.n.nk.nv, bf16[2048,512]{1,0:T(8,128)(2,1)} %refs_8_.1, bf16[2048,512]{1,0:T(8,128)(2,1)} %refs_9_.1, f32[512,128]{1,0:T(8,128)} %after.11.same, f32[512,128]{1,0:T(8,128)} %concatenate.27.down.refs_10_.refs_11_, ...), custom_call_target="tpu_custom_call" | custom-call | flops 1048576 | bytes 1048576 | tf_op jit(solution)/shard_map/project_kv/pallas_call | solution.py:386
  186.6 16.0 %collective-permute-done.15.refs_6_.refs_18_ = bf16[512,512]{1,0:T(8,128)(2,1)S(1)} collective-permute-done((bf16[512,512]{1,0:T(8,128)(2,1)}, bf16[512,512]{1,0:T(8,128)(2,1)S(1)}, u32[]{:S(2)}, u32[]{:S(2)}) %collective-permute-start.15) | collective-permute-done | bytes 524320 | tf_op jit(solution)/shard_map/ppermute | solution.py:756
  209.4 5.7 collective-permute-done.22.refs_14_.refs_26_
  218.7 18.5 %collective-permute-done.17.refs_7_.refs_19_ = bf16[512,512]{1,0:T(8,128)(2,1)} collective-permute-done((bf16[512,512]{1,0:T(8,128)(2,1)S(1)}, bf16[512,512]{1,0:T(8,128)(2,1)}, u32[]{:S(2)}, u32[]{:S(2)}) %collective-permute-start.17) | collective-permute-done | bytes 524320 | tf_op jit(solution)/shard_map/ppermute | solution.py:756
  251.9 8.2 %attend.1 = (bf16[512,512]{1,0:T(8,128)(2,1)}, f32[8,512]{1,0:T(8,128)}) custom-call(s32[2]{0:T(128)} %pad_add_fusion.info.refs_0_, s32[8]{0:T(128)} %broadcast_xor_fusion.offsets.refs_1_, bf16[512,512]{1,0:T(8,128)(2,1)} %project_q.1.q.refs_4_, s32[8,512]{1,0:T(8,128)} %after.9.span, bf16[512,512]{1,0:T(8,128)(2,1)} %collective-permute-done.12.refs_0_.refs_12_, ...), custom_call_target="tpu_custom_call" | custom-call | flops 1048576 | bytes 1048576 | tf_op jit(solution)/shard_map/attend/pallas_call | solution.py:502
  260.1 15.1 %attend_back.1 = (bf16[512,512]{1,0:T(8,128)(2,1)}, bf16[2048,512]{1,0:T(8,128)(2,1)}, bf16[2048,512]{1,0:T(8,128)(2,1)}, bf16[2048,512]{1,0:T(8,128)(2,1)}, bf16[2048,512]{1,0:T(8,128)(2,1)}) custom-call(s32[2]{0:T(128)} %pad_add_fusion.info.refs_0_, s32[8]{0:T(128)} %broadcast_xor_fusion.offsets.refs_1_, s32[8]{0:T(128)} %constant.81.clone.refs_2_, ...), custom_call_target="tpu_custom_call" | custom-call | flops 1048576 | bytes 1048576 | tf_op jit(solution)/shard_map/attend_back/pallas_call | solution.py:610
  279.7 6.0 %collective-permute-start.26 = (bf16[2048,512]{1,0:T(8,128)(2,1)}, bf16[2048,512]{1,0:T(8,128)(2,1)}, u32[]{:S(2)}, u32[]{:S(2)}) collective-permute-start(bf16[2048,512]{1,0:T(8,128)(2,1)} %get-tuple-element.71), channel_id=1, source_target_pairs={{0,4},{4,0},{8,12},{12,8},{16,20},{20,16},{24,28},{28,24},{1,5},{5... | collective-permute-start | bytes 6291464 | tf_op jit(solution)/shard_map/ppermute | solution.py:756
  285.8 15.2 %feed_forward_sums.1 = (f32[512,2048]{1,0:T(8,128)}, bf16[512,2048]{1,0:T(8,128)(2,1)}) custom-call(bf16[512,2048]{1,0:T(8,128)(2,1)} %after.12.act, bf16[512,2048]{1,0:T(8,128)(2,1)} %get-tuple-element.67.grad, bf16[2048,2048]{1,0:T(8,128)(2,1)} %w_up.1, bf16[2048,2048]{1,0:T(8,128)(2,1)} %w_down.1), custom_call_target="tpu_custom_call" | custom-call | flops 1048576 | bytes 1048576 | tf_op jit(solution)/shard_map/feed_forward_sums/pallas_call | solution.py:340
  306.1 11.4 %collective-permute-start.30 = (bf16[1024,512]{1,0:T(8,128)(2,1)S(1)}, bf16[1024,512]{1,0:T(8,128)(2,1)S(1)}, u32[]{:S(2)}, u32[]{:S(2)}) collective-permute-start(bf16[1024,512]{1,0:T(8,128)(2,1)S(1)} %add_convert_fusion.1), channel_id=1, source_target_pairs={{0,8},{4,12},{8,0},{12,4},{16,24},{20,28},{24,16},{28,20},{1,9},{5... | collective-permute-start | bytes 3145736 | tf_op jit(solution)/shard_map/ppermute | solution.py:756
  318.8 54.2 %collective-permute-done.27.refs_2_ = bf16[1024,512]{1,0:T(8,128)(2,1)S(1)} collective-permute-done((bf16[1024,512]{1,0:T(8,128)(2,1)S(1)}, bf16[1024,512]{1,0:T(8,128)(2,1)S(1)}, u32[]{:S(2)}, u32[]{:S(2)}) %collective-permute-start.27) | collective-permute-done | bytes 1048608 | tf_op jit(solution)/shard_map/ppermute | solution.py:756
  374.8 10.9 %collective-permute-start.28 = (bf16[512,512]{1,0:T(8,128)(2,1)S(1)}, bf16[512,512]{1,0:T(8,128)(2,1)S(1)}, u32[]{:S(2)}, u32[]{:S(2)}) collective-permute-start(bf16[512,512]{1,0:T(8,128)(2,1)S(1)} %add_convert_fusion.6), channel_id=1, source_target_pairs={{0,8},{4,12},{8,0},{12,4},{16,24},{20,28},{24,16},{28,20},{1,9},{5... | collective-permute-start | bytes 1572872 | tf_op jit(solution)/shard_map/ppermute | solution.py:756
  390.6 7.1 %collective-permute-done.28.refs_3_ = bf16[512,512]{1,0:T(8,128)(2,1)S(1)} collective-permute-done((bf16[512,512]{1,0:T(8,128)(2,1)S(1)}, bf16[512,512]{1,0:T(8,128)(2,1)S(1)}, u32[]{:S(2)}, u32[]{:S(2)}) %collective-permute-start.28) | collective-permute-done | bytes 524320 | tf_op jit(solution)/shard_map/ppermute | solution.py:756
  403.5 7.7 %key_value_back.1 = (bf16[512,512]{1,0:T(8,128)(2,1)}, bf16[512,512]{1,0:T(8,128)(2,1)}, bf16[512,4096]{1,0:T(8,128)(2,1)}) custom-call(bf16[2048,512]{1,0:T(8,128)(2,1)} %get-tuple-element.70.refs_0_, bf16[2048,512]{1,0:T(8,128)(2,1)} %collective-permute-done.26.refs_1_, bf16[1024,512]{1,0:T(8,128)(2,1)} %copy-done.9, bf16[512,512]{1,0:T(8,128)(2,1)} %copy-done.35, ...), custom_call_target="tpu_custom_call" | custom-call | flops 1048576 | bytes 1048576 | tf_op jit(solution)/shard_map/key_value_back/pallas_call | solution.py:638
  411.3 12.3 %weight_grads.1 = (bf16[1024,1024]{1,0:T(8,128)(2,1)}, bf16[1024,1024]{1,0:T(8,128)(2,1)}, bf16[1024,1024]{1,0:T(8,128)(2,1)}, bf16[1024,1024]{1,0:T(8,128)(2,1)}) custom-call(s32[1]{0:T(128)} %bitcast.10.core, bf16[512,2048]{1,0:T(8,128)(2,1)} %all-gather.3.cloned.1.call-done.n.nq, bf16[512,4096]{1,0:T(8,128)(2,1)} %all-gather.5.cloned.1.call-done.n.nk.nv, ...), custom_call_target="tpu_custom_call" | custom-call | flops 1048576 | bytes 1048576 | tf_op jit(solution)/shard_map/weight_grads/pallas_call | solution.py:691
  431.5 6.7 %merge.2 = (bf16[512,1024]{1,0:T(8,128)(2,1)}, bf16[512,1024]{1,0:T(8,128)(2,1)}, bf16[512,1024]{1,0:T(8,128)(2,1)}, bf16[512,1024]{1,0:T(8,128)(2,1)}) custom-call(s32[2]{0:T(128)} %pad_add_fusion.2.sides, bf16[1024,1024]{1,0:T(8,128)(2,1)} %get-tuple-element.83.refs_0_, bf16[1024,1024]{1,0:T(8,128)(2,1)} %copy-done.15, ...), custom_call_target="tpu_custom_call" | custom-call | flops 1048576 | bytes 1048576 | tf_op jit(solution)/shard_map/merge/pallas_call | solution.py:830
  439.2 9.6 %widen.3.refs_1_ = f32[2048,2048]{1,0:T(8,128)} custom-call(bf16[2048,2048]{1,0:T(8,128)(2,1)} %get-tuple-element.100.refs_1_.x), custom_call_target="tpu_custom_call" | custom-call | tf_op jit(solution)/shard_map/widen/pallas_call | solution.py:854
  448.8 14.8 %collective-permute-done.39.refs_1_ = bf16[512,1024]{1,0:T(8,128)(2,1)S(1)} collective-permute-done((bf16[512,1024]{1,0:T(8,128)(2,1)}, bf16[512,1024]{1,0:T(8,128)(2,1)S(1)}, u32[]{:S(2)}, u32[]{:S(2)}) %collective-permute-start.39) | collective-permute-done | bytes 1048608 | tf_op jit(solution)/shard_map/ppermute | solution.py:756
  471.9 11.7 %collective-permute-done.41 = bf16[256,1024]{1,0:T(8,128)(2,1)S(1)} collective-permute-done((bf16[256,1024]{1,0:T(8,128)(2,1)}, bf16[256,1024]{1,0:T(8,128)(2,1)S(1)}, u32[]{:S(2)}, u32[]{:S(2)}) %collective-permute-start.41) | collective-permute-done | bytes 524320 | tf_op jit(solution)/shard_map/ppermute | solution.py:756
  487.3 14.4 %unmix.1 = (bf16[9,128,2048]{2,1,0:T(8,128)(2,1)}, f32[48,2176]{1,0:T(8,128)}) custom-call(bf16[9,128,2048]{2,1,0:T(8,128)(2,1)} %hist.3, f32[4,128,2048]{2,1,0:T(8,128)} %get-tuple-element.56.streams, bf16[128,2048]{1,0:T(8,128)(2,1)} %reduce-scatter.7.cloned.1.call-done.gn3, bf16[128,4096]{1,0:T(8,128)(2,1)} %reduce-scatter.9.cloned.1.call-done.gnkv, ...), custom_call_target="tpu_custom_call" | custom-call | tf_op jit(solution)/shard_map/unmix/pallas_call | solution.py:206
  512.9 9.6 %widen.2.refs_1_ = f32[2048,2048]{1,0:T(8,128)} custom-call(bf16[2048,2048]{1,0:T(8,128)(2,1)} %get-tuple-element.99.x.refs_2_), custom_call_target="tpu_custom_call" | custom-call | tf_op jit(solution)/shard_map/widen/pallas_call | solution.py:854
  522.5 13.6 %collective-permute-done.33 = bf16[48,2176]{1,0:T(8,128)(2,1)S(1)} collective-permute-done((bf16[48,2176]{1,0:T(8,128)(2,1)S(1)}, bf16[48,2176]{1,0:T(8,128)(2,1)S(1)}, u32[]{:S(2)}, u32[]{:S(2)}) %collective-permute-start.33) | collective-permute-done | bytes 208928 | tf_op jit(solution)/shard_map/ppermute | solution.py:756
  545.9 9.5 %collective-permute-done.35 = bf16[48,2176]{1,0:T(8,128)(2,1)S(1)} collective-permute-done((bf16[48,2176]{1,0:T(8,128)(2,1)}, bf16[48,2176]{1,0:T(8,128)(2,1)S(1)}, u32[]{:S(2)}, u32[]{:S(2)}) %collective-permute-start.35) | collective-permute-done | bytes 208928 | tf_op jit(solution)/shard_map/ppermute | solution.py:756
  558.9 12.0 %assemble.1 = (f32[2048,512]{1,0:T(8,128)}, f32[2048,512]{1,0:T(8,128)}, f32[2048,512]{1,0:T(8,128)}, f32[512,2048]{1,0:T(8,128)}) custom-call(s32[8]{0:T(128)} %and_select_fusion.1.a_slot, s32[8]{0:T(128)} %and_select_fusion.b_slot, bf16[1024,1024]{1,0:T(8,128)(2,1)} %pad_maximum_fusion.a_lo, bf16[1024,1024]{1,0:T(8,128)(2,1)} %collective-permute-done.44.a_hi, ...), custom_call_target="tpu_custom_call" | custom-call | tf_op jit(solution)/shard_map/assemble/pallas_call | solution.py:744
  (249 shorter events, 128.0 us)
Async XLA Ops:
  8.0 164.5 %all-gather.5.cloned.1.call-start = ((), (), s32[]{:S(2)}) async-start(), calls=%async_computation.5 | async-start | bytes 5242880 | tf_op jit(solution)/shard_map/all_gather | solution.py:947
  8.1 24.5 %collective-permute-start.9 = (bf16[128,2048]{1,0:T(8,128)(2,1)}, bf16[128,2048]{1,0:T(8,128)(2,1)S(1)}, u32[]{:S(2)}, u32[]{:S(2)}) collective-permute-start(bf16[128,2048]{1,0:T(8,128)(2,1)} %cot.1), channel_id=1, source_target_pairs={{1,0},{2,1},{3,2},{5,4},{6,5},{7,6},{9,8},{10,9},{11,10},{13,12},{... | collective-permute-start | bytes 1572872 | tf_op jit(solution)/shard_map/ppermute | solution.py:893
  9.5 24.4 %collective-permute-start.6 = (bf16[128,2048]{1,0:T(8,128)(2,1)}, bf16[128,2048]{1,0:T(8,128)(2,1)S(1)}, u32[]{:S(2)}, u32[]{:S(2)}) collective-permute-start(bf16[128,2048]{1,0:T(8,128)(2,1)} %cot.1), channel_id=1, source_target_pairs={{0,1},{1,2},{2,3},{4,5},{5,6},{6,7},{8,9},{9,10},{10,11},{12,13},{... | collective-permute-start | bytes 1572872 | tf_op jit(solution)/shard_map/ppermute | solution.py:892
  32.6 22.3 %collective-permute-start.10 = (bf16[128,2048]{1,0:T(8,128)(2,1)S(1)}, bf16[128,2048]{1,0:T(8,128)(2,1)S(1)}, u32[]{:S(2)}, u32[]{:S(2)}) collective-permute-start(bf16[128,2048]{1,0:T(8,128)(2,1)S(1)} %collective-permute-done.9.refs_11_.refs_10_), channel_id=1, source_target_pairs={{1,0},{2,1},{5,4},{6,5},{9,8},{10,9},{13,12},{14,13},{17,16},{18,1... | collective-permute-start | bytes 1572872 | tf_op jit(solution)/shard_map/ppermute | solution.py:893
  33.9 22.3 %collective-permute-start.7 = (bf16[128,2048]{1,0:T(8,128)(2,1)S(1)}, bf16[128,2048]{1,0:T(8,128)(2,1)S(1)}, u32[]{:S(2)}, u32[]{:S(2)}) collective-permute-start(bf16[128,2048]{1,0:T(8,128)(2,1)S(1)} %collective-permute-done.6.refs_8_.refs_7_), channel_id=1, source_target_pairs={{1,2},{2,3},{5,6},{6,7},{9,10},{10,11},{13,14},{14,15},{17,18},{18... | collective-permute-start | bytes 1572872 | tf_op jit(solution)/shard_map/ppermute | solution.py:892
  43.7 22.5 %collective-permute-start.4 = (bf16[128,2048]{1,0:T(8,128)(2,1)S(1)}, bf16[128,2048]{1,0:T(8,128)(2,1)S(1)}, u32[]{:S(2)}, u32[]{:S(2)}) collective-permute-start(bf16[128,2048]{1,0:T(8,128)(2,1)S(1)} %collective-permute-done.3.refs_4_), channel_id=1, source_target_pairs={{1,0},{2,1},{5,4},{6,5},{9,8},{10,9},{13,12},{14,13},{17,16},{18,1... | collective-permute-start | bytes 1572872 | tf_op jit(solution)/shard_map/ppermute | solution.py:893
  45.0 22.5 %collective-permute-start.1 = (bf16[128,2048]{1,0:T(8,128)(2,1)S(1)}, bf16[128,2048]{1,0:T(8,128)(2,1)S(1)}, u32[]{:S(2)}, u32[]{:S(2)}) collective-permute-start(bf16[128,2048]{1,0:T(8,128)(2,1)S(1)} %collective-permute-done.refs_1_), channel_id=1, source_target_pairs={{1,2},{2,3},{5,6},{6,7},{9,10},{10,11},{13,14},{14,15},{17,18},{18... | collective-permute-start | bytes 1572872 | tf_op jit(solution)/shard_map/ppermute | solution.py:892
  54.9 22.5 %collective-permute-start.11 = (bf16[128,2048]{1,0:T(8,128)(2,1)S(1)}, bf16[128,2048]{1,0:T(8,128)(2,1)S(1)}, u32[]{:S(2)}, u32[]{:S(2)}) collective-permute-start(bf16[128,2048]{1,0:T(8,128)(2,1)S(1)} %collective-permute-done.10.refs_12_.refs_11_), channel_id=1, source_target_pairs={{1,0},{5,4},{9,8},{13,12},{17,16},{21,20},{25,24},{29,28}} | collective-permute-start | bytes 1572872 | tf_op jit(solution)/shard_map/ppermute | solution.py:893
  88.8 158.1 %all-gather.3.cloned.1.call-start = ((), (), s32[]{:S(2)}) async-start(), calls=%async_computation.4 | async-start | bytes 2621440 | tf_op jit(solution)/shard_map/all_gather | solution.py:947
  89.5 321.7 %all-reduce.4.cloned.1.call-start = ((), (), s32[]{:S(2)}) async-start(), calls=%async_computation.10 | async-start | bytes 33554432 | tf_op jit(solution)/shard_map/psum | solution.py:979
  115.1 372.1 %reduce-scatter.11.cloned.1.call-start = ((), (), s32[]{:S(2)}) async-start(), calls=%async_computation.9 | async-start | bytes 2621440 | tf_op jit(solution)/shard_map/reduce_scatter | solution.py:950
  179.0 23.6 %collective-permute-start.15 = (bf16[512,512]{1,0:T(8,128)(2,1)}, bf16[512,512]{1,0:T(8,128)(2,1)S(1)}, u32[]{:S(2)}, u32[]{:S(2)}) collective-permute-start(bf16[512,512]{1,0:T(8,128)(2,1)} %get-tuple-element.62.refs_4_.refs_16_), channel_id=1, source_target_pairs={{0,16},{4,20},{8,24},{12,28},{1,17},{5,21},{9,25},{13,29},{2,18},{... | collective-permute-start | bytes 1572872 | tf_op jit(solution)/shard_map/ppermute | solution.py:756
  182.4 22.7 %collective-permute-start.13 = (bf16[512,512]{1,0:T(8,128)(2,1)}, bf16[512,512]{1,0:T(8,128)(2,1)S(1)}, u32[]{:S(2)}, u32[]{:S(2)}) collective-permute-start(bf16[512,512]{1,0:T(8,128)(2,1)} %get-tuple-element.62.refs_4_.refs_16_), channel_id=1, source_target_pairs={{0,8},{4,12},{8,0},{12,4},{16,24},{20,28},{24,16},{28,20},{1,9},{5... | collective-permute-start | bytes 1572872 | tf_op jit(solution)/shard_map/ppermute | solution.py:756
  183.9 31.2 %collective-permute-start.22 = (bf16[512,512]{1,0:T(8,128)(2,1)}, bf16[512,512]{1,0:T(8,128)(2,1)}, u32[]{:S(2)}, u32[]{:S(2)}) collective-permute-start(bf16[512,512]{1,0:T(8,128)(2,1)} %get-tuple-element.63.refs_12_.refs_24_), channel_id=1, source_target_pairs={{0,16},{4,20},{8,24},{12,28},{1,17},{5,21},{9,25},{13,29},{2,18},{... | collective-permute-start | bytes 1572872 | tf_op jit(solution)/shard_map/ppermute | solution.py:756
  186.0 32.0 %collective-permute-start.20 = (bf16[512,512]{1,0:T(8,128)(2,1)}, bf16[512,512]{1,0:T(8,128)(2,1)}, u32[]{:S(2)}, u32[]{:S(2)}) collective-permute-start(bf16[512,512]{1,0:T(8,128)(2,1)} %get-tuple-element.63.refs_12_.refs_24_), channel_id=1, source_target_pairs={{0,8},{4,12},{8,0},{12,4},{16,24},{20,28},{24,16},{28,20},{1,9},{5... | collective-permute-start | bytes 1572872 | tf_op jit(solution)/shard_map/ppermute | solution.py:756
  205.1 32.0 %collective-permute-start.17 = (bf16[512,512]{1,0:T(8,128)(2,1)S(1)}, bf16[512,512]{1,0:T(8,128)(2,1)}, u32[]{:S(2)}, u32[]{:S(2)}) collective-permute-start(bf16[512,512]{1,0:T(8,128)(2,1)S(1)} %collective-permute-done.13.refs_5_.refs_17_), channel_id=1, source_target_pairs={{0,16},{4,20},{8,24},{12,28},{1,17},{5,21},{9,25},{13,29},{2,18},{... | collective-permute-start | bytes 1572872 | tf_op jit(solution)/shard_map/ppermute | solution.py:756
  215.1 25.7 %collective-permute-start.24 = (bf16[512,512]{1,0:T(8,128)(2,1)}, bf16[512,512]{1,0:T(8,128)(2,1)}, u32[]{:S(2)}, u32[]{:S(2)}) collective-permute-start(bf16[512,512]{1,0:T(8,128)(2,1)} %collective-permute-done.22.refs_14_.refs_26_), channel_id=1, source_target_pairs={{0,8},{4,12},{8,0},{12,4},{16,24},{20,28},{24,16},{28,20},{1,9},{5... | collective-permute-start | bytes 1572872 | tf_op jit(solution)/shard_map/ppermute | solution.py:756
  218.0 33.8 %collective-permute-start.14 = (bf16[512,512]{1,0:T(8,128)(2,1)S(1)}, bf16[512,512]{1,0:T(8,128)(2,1)}, u32[]{:S(2)}, u32[]{:S(2)}) collective-permute-start(bf16[512,512]{1,0:T(8,128)(2,1)S(1)} %collective-permute-done.13.refs_5_.refs_17_), channel_id=1, source_target_pairs={{0,4},{4,0},{8,12},{12,8},{16,20},{20,16},{24,28},{28,24},{1,5},{5... | collective-permute-start | bytes 1572872 | tf_op jit(solution)/shard_map/ppermute | solution.py:756
  218.1 33.8 %collective-permute-start.23 = (bf16[512,512]{1,0:T(8,128)(2,1)}, bf16[512,512]{1,0:T(8,128)(2,1)}, u32[]{:S(2)}, u32[]{:S(2)}) collective-permute-start(bf16[512,512]{1,0:T(8,128)(2,1)} %collective-permute-done.22.refs_14_.refs_26_), channel_id=1, source_target_pairs={{0,4},{4,0},{8,12},{12,8},{16,20},{20,16},{24,28},{28,24},{1,5},{5... | collective-permute-start | bytes 1572872 | tf_op jit(solution)/shard_map/ppermute | solution.py:756
  218.6 33.3 %collective-permute-start.21 = (bf16[512,512]{1,0:T(8,128)(2,1)}, bf16[512,512]{1,0:T(8,128)(2,1)}, u32[]{:S(2)}, u32[]{:S(2)}) collective-permute-start(bf16[512,512]{1,0:T(8,128)(2,1)} %collective-permute-done.20.refs_13_.refs_25_), channel_id=1, source_target_pairs={{0,4},{4,0},{8,12},{12,8},{16,20},{20,16},{24,28},{28,24},{1,5},{5... | collective-permute-start | bytes 1572872 | tf_op jit(solution)/shard_map/ppermute | solution.py:756
  279.7 207.6 %reduce-scatter.7.cloned.1.call-start = ((), (), s32[]{:S(2)}) async-start(), calls=%async_computation.7 | async-start | bytes 2621440 | tf_op jit(solution)/shard_map/reduce_scatter | solution.py:950
  301.0 186.3 %reduce-scatter.9.cloned.1.call-start = ((), (), s32[]{:S(2)}) async-start(), calls=%async_computation.8 | async-start | bytes 5242880 | tf_op jit(solution)/shard_map/reduce_scatter | solution.py:950
  303.1 70.0 %collective-permute-start.27 = (bf16[1024,512]{1,0:T(8,128)(2,1)S(1)}, bf16[1024,512]{1,0:T(8,128)(2,1)S(1)}, u32[]{:S(2)}, u32[]{:S(2)}) collective-permute-start(bf16[1024,512]{1,0:T(8,128)(2,1)S(1)} %add_convert_fusion.2), channel_id=1, source_target_pairs={{16,0},{20,4},{24,8},{28,12},{17,1},{21,5},{25,9},{29,13},{18,2},{... | collective-permute-start | bytes 3145736 | tf_op jit(solution)/shard_map/ppermute | solution.py:756
  306.1 79.6 %collective-permute-start.30 = (bf16[1024,512]{1,0:T(8,128)(2,1)S(1)}, bf16[1024,512]{1,0:T(8,128)(2,1)S(1)}, u32[]{:S(2)}, u32[]{:S(2)}) collective-permute-start(bf16[1024,512]{1,0:T(8,128)(2,1)S(1)} %add_convert_fusion.1), channel_id=1, source_target_pairs={{0,8},{4,12},{8,0},{12,4},{16,24},{20,28},{24,16},{28,20},{1,9},{5... | collective-permute-start | bytes 3145736 | tf_op jit(solution)/shard_map/ppermute | solution.py:756
  374.8 22.9 %collective-permute-start.28 = (bf16[512,512]{1,0:T(8,128)(2,1)S(1)}, bf16[512,512]{1,0:T(8,128)(2,1)S(1)}, u32[]{:S(2)}, u32[]{:S(2)}) collective-permute-start(bf16[512,512]{1,0:T(8,128)(2,1)S(1)} %add_convert_fusion.6), channel_id=1, source_target_pairs={{0,8},{4,12},{8,0},{12,4},{16,24},{20,28},{24,16},{28,20},{1,9},{5... | collective-permute-start | bytes 1572872 | tf_op jit(solution)/shard_map/ppermute | solution.py:756
  411.2 145.4 %reduce-scatter.5.cloned.1.call-start = ((), (), s32[]{:S(2)}) async-start(), calls=%async_computation.6 | async-start | bytes 2621440 | tf_op jit(solution)/shard_map/reduce_scatter | solution.py:950
  438.2 25.4 %collective-permute-start.39 = (bf16[512,1024]{1,0:T(8,128)(2,1)}, bf16[512,1024]{1,0:T(8,128)(2,1)S(1)}, u32[]{:S(2)}, u32[]{:S(2)}) collective-permute-start(bf16[512,1024]{1,0:T(8,128)(2,1)} %get-tuple-element.88), channel_id=1, source_target_pairs={{0,8},{4,12},{8,0},{12,4},{16,24},{20,28},{24,16},{28,20},{1,9},{5... | collective-permute-start | bytes 3145736 | tf_op jit(solution)/shard_map/ppermute | solution.py:756
  438.7 25.1 %collective-permute-start.40 = (bf16[512,1024]{1,0:T(8,128)(2,1)}, bf16[512,1024]{1,0:T(8,128)(2,1)S(1)}, u32[]{:S(2)}, u32[]{:S(2)}) collective-permute-start(bf16[512,1024]{1,0:T(8,128)(2,1)} %get-tuple-element.90), channel_id=1, source_target_pairs={{0,16},{4,20},{8,24},{12,28},{16,0},{20,4},{24,8},{28,12},{1,17},{... | collective-permute-start | bytes 3145736 | tf_op jit(solution)/shard_map/ppermute | solution.py:756
  484.4 21.5 %collective-permute-start.46 = (bf16[256,1024]{1,0:T(8,128)(2,1)S(1)}, bf16[256,1024]{1,0:T(8,128)(2,1)S(1)}, u32[]{:S(2)}, u32[]{:S(2)}) collective-permute-start(bf16[256,1024]{1,0:T(8,128)(2,1)S(1)} %add_convert_fusion.3), channel_id=1, source_target_pairs={{0,8},{4,12},{8,0},{12,4},{16,24},{20,28},{24,16},{28,20},{1,9},{5... | collective-permute-start | bytes 1572872 | tf_op jit(solution)/shard_map/ppermute | solution.py:756
  505.3 33.0 %collective-permute-start.43 = (bf16[512,1024]{1,0:T(8,128)(2,1)}, bf16[512,1024]{1,0:T(8,128)(2,1)}, u32[]{:S(2)}, u32[]{:S(2)}) collective-permute-start(bf16[512,1024]{1,0:T(8,128)(2,1)} %pad_maximum_fusion.2), channel_id=1, source_target_pairs={{0,8},{4,12},{8,0},{12,4},{16,24},{20,28},{24,16},{28,20},{1,9},{5... | collective-permute-start | bytes 3145736 | tf_op jit(solution)/shard_map/ppermute | solution.py:756
  507.1 29.1 %collective-permute-start.47 = (bf16[512,1024]{1,0:T(8,128)(2,1)}, bf16[512,1024]{1,0:T(8,128)(2,1)}, u32[]{:S(2)}, u32[]{:S(2)}) collective-permute-start(bf16[512,1024]{1,0:T(8,128)(2,1)} %pad_maximum_fusion.3), channel_id=1, source_target_pairs={{0,16},{4,20},{8,24},{12,28},{16,0},{20,4},{24,8},{28,12},{1,17},{... | collective-permute-start | bytes 3145736 | tf_op jit(solution)/shard_map/ppermute | solution.py:756
  510.9 25.1 %collective-permute-start.33 = (bf16[48,2176]{1,0:T(8,128)(2,1)S(1)}, bf16[48,2176]{1,0:T(8,128)(2,1)S(1)}, u32[]{:S(2)}, u32[]{:S(2)}) collective-permute-start(bf16[48,2176]{1,0:T(8,128)(2,1)S(1)} %add_convert_fusion.11), channel_id=1, source_target_pairs={{0,16},{4,20},{8,24},{12,28},{16,0},{20,4},{24,8},{28,12},{1,17},{... | collective-permute-start | bytes 626696 | tf_op jit(solution)/shard_map/ppermute | solution.py:756
  (66 other events, 1354.3 us)
Sparse Core Ops, SparseCore 0:
  88.9 83.5 all-gather.4
  174.0 44.4 all-gather.2
  279.8 80.3 reduce-scatter.10
  362.4 43.1 reduce-scatter.6
  411.3 75.8 reduce-scatter.8
  490.1 44.3 reduce-scatter.4
Sparse Core Ops, SparseCore 1:
  115.2 268.0 all-reduce.3
